TPU v7x, 256 devices: a whole 4x4x8 slice. The times are simulated.
256 devices in a mesh: az: 64 (over z, x, y_hi), ax: 4 (over y_lo, core).
Axes of the slice: x: 4, y: 4 (y_hi: 2, y_lo: 2; y = y_hi * 2 + y_lo), z: 8, core: 2. Of those that a mesh axis runs over, the one named last changes fastest.
Arguments:
- tangent: float32 [256, 64, 2048], P('az', 'ax'), may hold values from -6 to 6
- velocity: float32 [3, 256, 64, 64], P(None, 'az', 'ax'), may hold values from -0.25 to 0.25
- face_frac: float32 [2, 3, 256, 64, 64], P(None, None, 'az', 'ax'), may hold values from 0.05 to 1
- branch: int32 [2, 3, 256, 64, 64], P(None, None, 'az', 'ax'), may hold values from 0 to 2
- basis: bfloat16 [3, 256, 64, 2048], P(None, 'az', 'ax'), may hold values from -0.5 to 0.5
- design: bfloat16 [32, 32], replicated, may hold values from -5 to 5
- exit_film: float32 [256, 64], P('az'), may hold values from 0.15 to 4.5, as said below
Outputs:
- tangent_out: float32 [256, 64, 2048], P('az', 'ax')
- velocity_tangent: bfloat16 [3, 256, 64, 2048], P(None, 'az', 'ax')
- film: float32 [256, 32], P('az', 'ax')
Inputs may be any that keep to these rules, and one draw needn't show every extreme that they name: `branch`: 0 upwind, 1 blended, 2 central. `exit_film`: positive film thickness.
All inputs are finite; a program needn't handle non-finite values.
Results may differ from a plain program's by a relative error of at most 0.0034.
Values sent between devices are 32-bit elements; how exact they have to be, the bound alone decides.
No kernel may reach another device: no remote copies, remote signals or barrier semaphores. Data moves between devices by JAX's collectives and lax.ppermute only.
A program may use at most 128 MiB of HBM per device.

v0:
```python
import jax
import jax.numpy as jnp
from jax import lax
from jax.sharding import PartitionSpec as P


def shifted(value, axis, steps):
    count = lax.axis_size(axis)
    pairs = [(source, (source + steps) % count) for source in range(count)]
    return lax.ppermute(value, axis, pairs)


def passed_along(block, axis, distance):
    devices = range(lax.axis_size(axis))
    route = [(i - distance, i) for i in devices if i - distance in devices]
    return lax.ppermute(block, axis, route)


def face_flux(here, there, speed, frac, coef, dspeed):
    upwind = jnp.where(speed > 0, here, there)
    downwind = jnp.where(speed > 0, there, here)
    return dspeed * frac + speed * (upwind + coef * (downwind - upwind))


def spread(values, dirs):
    return jnp.repeat(values, dirs, axis=-1)


def local(tangent, velocity, face_frac, branch, basis, design, exit_film):
    cells_az, cells_ax, lanes = tangent.shape
    params, dirs = design.shape
    radial = lanes // dirs
    steps = face_frac.shape[0]
    product = jnp.einsum(
        "caxrp,pd->caxrd",
        basis.reshape(3, cells_az, cells_ax, radial, params),
        design,
        preferred_element_type=jnp.float32,
    )
    velocity_tangent = product.astype(jnp.bfloat16).reshape(3, cells_az, cells_ax, lanes)
    dspeed = velocity_tangent.astype(jnp.float32)
    speed = spread(velocity, dirs)
    frac = spread(face_frac, dirs)
    coef_small = 0.25 * branch.astype(jnp.float32)
    coef = spread(coef_small, dirs)
    wall = spread((jnp.arange(radial) < radial - 1).astype(jnp.float32), dirs)
    is_last = lax.axis_index("ax") == lax.axis_size("ax") - 1
    field = tangent
    exit_sum = jnp.zeros((cells_az, lanes), jnp.float32)
    for step in range(steps):
        ahead = shifted(field[:1], "az", -1)
        upper = face_flux(
            field,
            jnp.concatenate([field[1:], ahead], 0),
            speed[0],
            frac[step, 0],
            coef[step, 0],
            dspeed[0],
        )
        lower_face = shifted(upper[-1:], "az", 1)
        change = upper - jnp.concatenate([lower_face, upper[:-1]], 0)
        ahead = passed_along(field[:, :1], "ax", -1)
        upper = face_flux(
            field,
            jnp.concatenate([field[:, 1:], ahead], 1),
            speed[1],
            frac[step, 1],
            coef[step, 1],
            dspeed[1],
        )
        exit_sum = exit_sum + jnp.where(is_last, upper[:, -1, :], jnp.zeros_like(upper[:, -1, :]))
        lower_face = passed_along(upper[:, -1:], "ax", 1)
        change = change + (upper - jnp.concatenate([lower_face, upper[:, :-1]], 1))
        blank = jnp.zeros((cells_az, cells_ax, dirs), jnp.float32)
        upper = (
            face_flux(
                field,
                jnp.concatenate([field[..., dirs:], blank], -1),
                speed[2],
                frac[step, 2],
                coef[step, 2],
                dspeed[2],
            )
            * wall
        )
        change = change + (upper - jnp.concatenate([blank, upper[..., :-dirs]], -1))
        field = field - change
    weights = (jnp.arange(radial).astype(jnp.float32) + 0.5) / radial
    raw = jnp.sum(exit_sum.reshape(cells_az, radial, dirs) * weights[None, :, None], axis=1)
    row_film = jnp.sum(exit_film * weights[None, :], axis=1)
    total_cells = cells_az * lax.axis_size("az")
    mean_film = lax.psum(jnp.sum(row_film), "az") / total_cells
    factor = (mean_film / row_film)[:, None]
    film = lax.psum_scatter(raw * factor, "ax", scatter_dimension=1, tiled=True)
    return (field, velocity_tangent, film)


def solution(mesh):
    in_specs = (
        P("az", "ax", None),
        P(None, "az", "ax", None),
        P(None, None, "az", "ax", None),
        P(None, None, "az", "ax", None),
        P(None, "az", "ax", None),
        P(),
        P("az", None),
    )
    out_specs = (P("az", "ax", None), P(None, "az", "ax", None), P("az", "ax"))
    return jax.shard_map(local, mesh=mesh, in_specs=in_specs, out_specs=out_specs, check_vma=False)
```

profile of v0, /device:TPU:1, one launch (start us, length us, event | category | flops | bytes accessed | tf_op | source)
XLA Modules:
  0.0 309.8 jit_solution(836453343634975034)
XLA Ops:
  0.6 1.6 slice.148
  2.2 5.1 %collective-permute-start.2 = (f32[4,1,2048]{2,1,0:T(1,128)}, f32[4,1,2048]{2,1,0:T(1,128)}, u32[]{:S(2)}, u32[]{:S(2)}) collective-permute-start(f32[4,1,2048]{2,1,0:T(1,128)} %slice.148), channel_id=1, source_target_pairs={{1,0},{2,1},{3,2},{5,4},{6,5},{7,6},{9,8},{10,9},{11,10},{13,12},{... | collective-permute-start | bytes 98312 | tf_op jit(solution)/shard_map/ppermute | solution.py:16
  8.3 8.7 %collective-permute-start = (f32[1,16,2048]{2,1,0:T(8,128)S(1)}, f32[1,16,2048]{2,1,0:T(8,128)}, u32[]{:S(2)}, u32[]{:S(2)}) collective-permute-start(f32[1,16,2048]{2,1,0:T(8,128)S(1)} %slice.139), channel_id=1, source_target_pairs={{0,252},{4,0},{8,4},{12,8},{16,12},{20,16},{24,20},{28,24},{32,28}... | collective-permute-start | bytes 393224 | tf_op jit(solution)/shard_map/ppermute | solution.py:10
  17.0 0.9 convert_multiply_fusion
  18.0 3.7 %reshape.61 = bf16[3,4,16,64,32]{4,3,2,1,0:T(8,128)(2,1)S(1)} reshape(bf16[3,4,16,2048]{3,2,1,0:T(8,128)(2,1)} %param.11) | data formatting | bytes 1572864 | tf_op jit(solution)/shard_map/reshape | solution.py:36
  21.7 4.2 %convolution_convert_fusion = bf16[3,4,16,64,32]{3,4,2,1,0:T(8,128)(2,1)} fusion(bf16[3,4,16,64,32]{4,3,2,1,0:T(8,128)(2,1)S(1)} %reshape.61, bf16[32,32]{1,0:T(8,128)(2,1)S(1)} %copy-done), kind=kOutput, calls=%fused_computation | convolution fusion | flops 25559040 | bytes 1574912 | tf_op jit(solution)/shard_map/caxrp,pd->caxrd/dot_general | solution.py:34
  26.0 1.0 slice.156
  28.4 1.8 broadcast_in_dim.34
  30.2 7.2 %broadcast_in_dim.30 = f32[2,3,4,16,64,32]{5,4,3,2,1,0:T(8,128)} broadcast(f32[2,3,4,16,64]{4,3,2,1,0:T(8,128)S(1)} %convert_multiply_fusion), dimensions={0,1,2,3,4} | broadcast | bytes 3244032 | tf_op jit(solution)/shard_map/broadcast_in_dim | solution.py:26
  37.3 10.6 %reshape.64 = f32[2,3,4,16,2048]{4,3,2,1,0:T(8,128)} reshape(f32[2,3,4,16,64,32]{5,4,3,2,1,0:T(8,128)} %broadcast_in_dim.30) | data formatting | bytes 6291456 | tf_op jit(solution)/shard_map/reshape | solution.py:26
  47.9 7.2 %broadcast_in_dim.27 = f32[2,3,4,16,64,32]{5,4,3,2,1,0:T(8,128)} broadcast(f32[2,3,4,16,64]{4,3,2,1,0:T(8,128)S(1)} %copy-done.6), dimensions={0,1,2,3,4} | broadcast | bytes 3244032 | tf_op jit(solution)/shard_map/broadcast_in_dim | solution.py:26
  55.1 10.5 %reshape.63 = f32[2,3,4,16,2048]{4,3,2,1,0:T(8,128)} reshape(f32[2,3,4,16,64,32]{5,4,3,2,1,0:T(8,128)} %broadcast_in_dim.27) | data formatting | bytes 6291456 | tf_op jit(solution)/shard_map/reshape | solution.py:26
  65.6 3.0 copy.17
  68.6 4.3 %reshape.62 = bf16[3,4,16,2048]{3,2,1,0:T(8,128)(2,1)} reshape(bf16[3,4,16,64,32]{4,3,2,1,0:T(8,128)(2,1)S(1)} %copy.17) | data formatting | bytes 1572864 | tf_op jit(solution)/shard_map/reshape | solution.py:40
  72.9 1.3 convert_element_type.28
  74.3 1.9 broadcast_in_dim.31
  76.3 3.2 %broadcast_in_dim.32 = f32[4,16,2048]{2,1,0:T(8,128)} reshape(f32[4,16,64,32]{3,2,1,0:T(8,128)} %broadcast_in_dim.31) | data formatting | bytes 1048576 | tf_op jit(solution)/shard_map/broadcast_in_dim | solution.py:26
  79.5 1.9 broadcast_in_dim.28
  81.5 3.1 %broadcast_in_dim.29 = f32[4,16,2048]{2,1,0:T(8,128)} reshape(f32[4,16,64,32]{3,2,1,0:T(8,128)} %broadcast_in_dim.28) | data formatting | bytes 1048576 | tf_op jit(solution)/shard_map/broadcast_in_dim | solution.py:26
  84.7 4.2 %fusion.20 = (f32[4,16,2048]{2,1,0:T(8,128)}, f32[4,16,2048]{2,1,0:T(8,128)S(1)}, f32[4,16,2048]{2,1,0:T(8,128)S(1)}) fusion(f32[4,16,2048]{2,1,0:T(8,128)S(1)} %copy-done.3, f32[2,3,4,16,2048]{4,3,2,1,0:T(8,128)} %reshape.64, f32[2,3,4,16,2048]{4,3,2,1,0:T(8,128)} %reshape.63, f32[4,16,2048]{2,1,0:T(8,128)S(1)} %copy-done.2, f32[4,16,2016]{2,1,0:T(8,128)} %slice.156, ...), kind=kLoop, calls=%fused_computation.28 | loop fusion | flops 3932160 | bytes 9961472 | tf_op jit(solution)/shard_map/mul | solution.py:76
  89.9 2.7 collective-permute-start.3
  93.2 157.6 %psum.7 = f32[]{:T(128)} all-reduce(f32[]{:T(128)} %get-tuple-element.3), channel_id=1, replica_groups=mesh['az'=64,'ax'=4] {'az'}, use_global_device_ids=true, to_apply=%region_2.3 | all-reduce | flops 1 | bytes 8 | tf_op jit(solution)/shard_map/psum | solution.py:92
  251.4 1.0 slice.179
  253.1 1.9 fusion.34
  255.1 28.4 %collective-permute-start.6 = (f32[4,1,2048]{2,1,0:T(1,128)S(1)}, f32[4,1,2048]{2,1,0:T(1,128)S(1)}, u32[]{:S(2)}, u32[]{:S(2)}) collective-permute-start(f32[4,1,2048]{2,1,0:T(1,128)S(1)} %slice.197), channel_id=1, source_target_pairs={{1,0},{2,1},{3,2},{5,4},{6,5},{7,6},{9,8},{10,9},{11,10},{13,12},{... | collective-permute-start | bytes 98312 | tf_op jit(solution)/shard_map/ppermute | solution.py:16
  284.2 1.3 dynamic-slice
  287.1 3.3 %collective-permute-done.4 = f32[1,16,2048]{2,1,0:T(8,128)} collective-permute-done((f32[1,16,2048]{2,1,0:T(8,128)S(1)}, f32[1,16,2048]{2,1,0:T(8,128)}, u32[]{:S(2)}, u32[]{:S(2)}) %collective-permute-start.4) | collective-permute-done | bytes 131104 | tf_op jit(solution)/shard_map/ppermute | solution.py:10
  290.4 4.0 %fusion.4 = (f32[4,16,2048]{2,1,0:T(8,128)}, f32[4,16,2048]{2,1,0:T(8,128)S(1)}, f32[4,16,2048]{2,1,0:T(8,128)S(1)}) fusion(f32[4,16,2048]{2,1,0:T(8,128)} %broadcast_in_dim.34, f32[2,3,4,16,2048]{4,3,2,1,0:T(8,128)} %reshape.64, f32[2,3,4,16,2048]{4,3,2,1,0:T(8,128)} %reshape.63, f32[4,16,2048]{2,1,0:T(8,128)S(1)} %fusion.34, f32[4,16,2016]{2,1,0:T(8,128)S(1)} %slice.202, ...), kind=kLoop, calls=%fused_computation.6 | loop fusion | flops 3932160 | bytes 9961472 | tf_op jit(solution)/shard_map/mul | solution.py:76
  295.2 3.5 %collective-permute-start.7 = (f32[4,1,2048]{2,1,0:T(1,128)S(1)}, f32[4,1,2048]{2,1,0:T(1,128)S(1)}, u32[]{:S(2)}, u32[]{:S(2)}) collective-permute-start(f32[4,1,2048]{2,1,0:T(1,128)S(1)} %get-tuple-element.12), channel_id=1, source_target_pairs={{0,1},{1,2},{2,3},{4,5},{5,6},{6,7},{8,9},{9,10},{10,11},{12,13},{... | collective-permute-start | bytes 98312 | tf_op jit(solution)/shard_map/ppermute | solution.py:16
  300.2 5.4 %all-reduce.4 = f32[4,32]{1,0:T(4,128)S(1)} all-reduce(f32[4,32]{1,0:T(4,128)S(1)} %broadcast_multiply_fusion), channel_id=2, replica_groups=mesh['az'=64,'ax'=4] {'ax'}, use_global_device_ids=true, to_apply=%region_4.5.clone | all-reduce | flops 128 | bytes 1024
  306.3 1.0 slice.194
  307.3 2.5 fusion.37
  (63 shorter events, 9.4 us)
Async XLA Ops:
  0.6 21.1 %copy-start = (bf16[32,32]{1,0:T(8,128)(2,1)S(1)}, bf16[32,32]{1,0:T(8,128)(2,1)}, u32[]{:S(2)}) copy-start(bf16[32,32]{1,0:T(8,128)(2,1)} %param.12) | copy-start | bytes 6148
  2.2 82.4 %collective-permute-start.2 = (f32[4,1,2048]{2,1,0:T(1,128)}, f32[4,1,2048]{2,1,0:T(1,128)}, u32[]{:S(2)}, u32[]{:S(2)}) collective-permute-start(f32[4,1,2048]{2,1,0:T(1,128)} %slice.148), channel_id=1, source_target_pairs={{1,0},{2,1},{3,2},{5,4},{6,5},{7,6},{9,8},{10,9},{11,10},{13,12},{... | collective-permute-start | bytes 98312 | tf_op jit(solution)/shard_map/ppermute | solution.py:16
  8.3 76.3 %collective-permute-start = (f32[1,16,2048]{2,1,0:T(8,128)S(1)}, f32[1,16,2048]{2,1,0:T(8,128)}, u32[]{:S(2)}, u32[]{:S(2)}) collective-permute-start(f32[1,16,2048]{2,1,0:T(8,128)S(1)} %slice.139), channel_id=1, source_target_pairs={{0,252},{4,0},{8,4},{12,8},{16,12},{20,16},{24,20},{28,24},{32,28}... | collective-permute-start | bytes 393224 | tf_op jit(solution)/shard_map/ppermute | solution.py:10
  21.7 4.2 %copy-start.8 = (f32[3,4,16,64]{3,2,1,0:T(8,128)S(1)}, f32[3,4,16,64]{3,2,1,0:T(8,128)}, u32[]{:S(2)}) copy-start(f32[3,4,16,64]{3,2,1,0:T(8,128)} %param.8) | copy-start | bytes 147460
  21.7 4.2 %copy-start.1 = (f32[4,16,2048]{2,1,0:T(8,128)S(1)}, f32[4,16,2048]{2,1,0:T(8,128)}, u32[]{:S(2)}) copy-start(f32[4,16,2048]{2,1,0:T(8,128)} %param.7) | copy-start | bytes 1572868
  37.3 10.6 %copy-start.6 = (f32[2,3,4,16,64]{4,3,2,1,0:T(8,128)S(1)}, f32[2,3,4,16,64]{4,3,2,1,0:T(8,128)}, u32[]{:S(2)}) copy-start(f32[2,3,4,16,64]{4,3,2,1,0:T(8,128)} %param.9) | copy-start | bytes 294916
  76.3 8.3 %copy-start.2 = (f32[4,16,2048]{2,1,0:T(8,128)S(1)}, f32[4,16,2048]{2,1,0:T(8,128)}, u32[]{:S(2)}) copy-start(f32[4,16,2048]{2,1,0:T(8,128)} %param.7) | copy-start | bytes 1572868
  76.3 8.3 %slice-start = ((f32[4,16,2048]{2,1,0:T(8,128)}), f32[3,16,2048]{2,1,0:T(8,128)S(1)}, s32[]{:S(2)}) async-start(f32[4,16,2048]{2,1,0:T(8,128)} %param.7), calls=%async_computation | async-start | bytes 786432 | tf_op jit(solution)/shard_map/slice | solution.py:54
  76.3 8.4 %copy-start.3 = (f32[4,16,2048]{2,1,0:T(8,128)S(1)}, f32[4,16,2048]{2,1,0:T(8,128)}, u32[]{:S(2)}) copy-start(f32[4,16,2048]{2,1,0:T(8,128)} %broadcast_in_dim.34) | copy-start | bytes 1572868
  84.6 7.9 %copy-start.12 = (f32[4,64]{1,0:T(4,128)S(1)}, f32[4,64]{1,0:T(4,128)}, u32[]{:S(2)}) copy-start(f32[4,64]{1,0:T(4,128)} %param.13) | copy-start | bytes 3076
  88.9 0.8 copy-start.5
  89.7 162.7 %collective-permute-start.1 = (f32[1,16,2048]{2,1,0:T(8,128)S(1)}, f32[1,16,2048]{2,1,0:T(8,128)S(1)}, u32[]{:S(2)}, u32[]{:S(2)}) collective-permute-start(f32[1,16,2048]{2,1,0:T(8,128)S(1)} %slice.178), channel_id=1, source_target_pairs={{0,4},{4,8},{8,12},{12,16},{16,20},{20,24},{24,28},{28,32},{32,36}... | collective-permute-start | bytes 393224 | tf_op jit(solution)/shard_map/ppermute | solution.py:10
  89.8 162.7 %copy-start.11 = (f32[64]{0:T(128)}, f32[64]{0:T(128)S(1)}, u32[]{:S(2)}) copy-start(f32[64]{0:T(128)S(1)} %add_multiply_fusion) | copy-start | bytes 772
  89.9 162.6 %collective-permute-start.3 = (f32[4,1,2048]{2,1,0:T(1,128)S(1)}, f32[4,1,2048]{2,1,0:T(1,128)S(1)}, u32[]{:S(2)}, u32[]{:S(2)}) collective-permute-start(f32[4,1,2048]{2,1,0:T(1,128)S(1)} %slice.183), channel_id=1, source_target_pairs={{0,1},{1,2},{2,3},{4,5},{5,6},{6,7},{8,9},{9,10},{10,11},{12,13},{... | collective-permute-start | bytes 98312 | tf_op jit(solution)/shard_map/ppermute | solution.py:16
  251.4 32.2 %copy-start.13 = (f32[4]{0:T(128)S(1)}, f32[4]{0:T(128)}, u32[]{:S(2)}) copy-start(f32[4]{0:T(128)} %get-tuple-element.4) | copy-start | bytes 52
  252.4 0.6 copy-start.10
  252.5 0.6 copy-start.7
  255.1 31.4 %collective-permute-start.6 = (f32[4,1,2048]{2,1,0:T(1,128)S(1)}, f32[4,1,2048]{2,1,0:T(1,128)S(1)}, u32[]{:S(2)}, u32[]{:S(2)}) collective-permute-start(f32[4,1,2048]{2,1,0:T(1,128)S(1)} %slice.197), channel_id=1, source_target_pairs={{1,0},{2,1},{3,2},{5,4},{6,5},{7,6},{9,8},{10,9},{11,10},{13,12},{... | collective-permute-start | bytes 98312 | tf_op jit(solution)/shard_map/ppermute | solution.py:16
  283.5 6.9 %collective-permute-start.4 = (f32[1,16,2048]{2,1,0:T(8,128)S(1)}, f32[1,16,2048]{2,1,0:T(8,128)}, u32[]{:S(2)}, u32[]{:S(2)}) collective-permute-start(f32[1,16,2048]{2,1,0:T(8,128)S(1)} %slice.191), channel_id=1, source_target_pairs={{0,252},{4,0},{8,4},{12,8},{16,12},{20,16},{24,20},{28,24},{32,28}... | collective-permute-start | bytes 393224 | tf_op jit(solution)/shard_map/ppermute | solution.py:10
  286.5 0.6 copy-start.9
  294.4 0.8 copy-start.4
  294.4 12.9 %collective-permute-start.5 = (f32[1,16,2048]{2,1,0:T(8,128)S(1)}, f32[1,16,2048]{2,1,0:T(8,128)S(1)}, u32[]{:S(2)}, u32[]{:S(2)}) collective-permute-start(f32[1,16,2048]{2,1,0:T(8,128)S(1)} %slice.193), channel_id=1, source_target_pairs={{0,4},{4,8},{8,12},{12,16},{16,20},{20,24},{24,28},{28,32},{32,36}... | collective-permute-start | bytes 393224 | tf_op jit(solution)/shard_map/ppermute | solution.py:10
  295.2 12.1 %collective-permute-start.7 = (f32[4,1,2048]{2,1,0:T(1,128)S(1)}, f32[4,1,2048]{2,1,0:T(1,128)S(1)}, u32[]{:S(2)}, u32[]{:S(2)}) collective-permute-start(f32[4,1,2048]{2,1,0:T(1,128)S(1)} %get-tuple-element.12), channel_id=1, source_target_pairs={{0,1},{1,2},{2,3},{4,5},{5,6},{6,7},{8,9},{9,10},{10,11},{12,13},{... | collective-permute-start | bytes 98312 | tf_op jit(solution)/shard_map/ppermute | solution.py:16
where the time goes:
time: 311 us; the launch traced here: 310 us
  blocking collectives  163 us (52%)
  local copies, waits for them, and re-layouts  70.6 us (23%)
  starting transfers between devices  48.7 us (16%)
  other arithmetic  17.8 us (6%)
  matrix products  4.2 us (1%)
  waiting for transfers between devices  3.3 us (1%)
    psum x1, blocking collectives, local(): mean_film = lax.psum(jnp.sum(row_film), 'az') / total_cells  158 us
    ppermute x4, starting transfers between devices, passed_along(): return lax.ppermute(block, axis, route)  39.7 us
    broadcast_in_dim x9, local copies, waits for them, and re-layouts, spread(): return jnp.repeat(values, dirs, axis=-1)  27 us
    reshape x2, local copies, waits for them, and re-layouts, spread(): return jnp.repeat(values, dirs, axis=-1)  21.1 us
    ppermute x4, starting transfers between devices, shifted(): return lax.ppermute(value, axis, pairs)  8.99 us
    mul x2, other arithmetic, local(): face_flux(field, jnp.concatenate([field[..., dirs:], blank], -1), speed[2...  8.24 us
  transfers between devices with their start and end apart: 8, of which 1 were waited for; matrix products, arithmetic and copies ran while one was open for 24% of the time, Pallas kernels for 0%

commit v1 on v0

v1 whole, which is shorter than its diff:
```python
import jax
import jax.numpy as jnp
from jax import lax
from jax.experimental import pallas as pl
from jax.experimental.pallas import tpu as pltpu
from jax.sharding import PartitionSpec as P

F32, BF16 = jnp.float32, jnp.bfloat16
CHUNK = 256
RADIAL = 64
CELLS = 4
UNROLL = 8
AT_C1, AT_B2, AT_C2, AT_ROW_A, AT_ROW_B, AT_COEF, AT_FIRST, AT_END = 0, 256, 512, 768, 1024, 1280, 1408, 1664


def mix(speed, branch):
    part = speed * (0.25 * branch.astype(F32))
    rest = speed - part
    ahead = speed > 0
    return jnp.where(ahead, rest, part), jnp.where(ahead, part, rest)


def two_terms(values):
    high = values.astype(BF16)
    low = (values - high.astype(F32)).astype(BF16)
    return jnp.concatenate([high, low], axis=-1)


def spreader(offset, lanes, radial, dirs):
    row = lax.broadcasted_iota(jnp.int32, (2 * radial, lanes), 0)
    lane = lax.broadcasted_iota(jnp.int32, (2 * radial, lanes), 1) + offset
    shift = dirs.bit_length() - 1
    return jnp.where((row & (radial - 1)) == (lane >> shift), 1.0, 0.0).astype(BF16)


def spread_all(packed, outs, radial, dirs):
    lanes = outs[0].shape[1]

    @pl.loop(0, lanes // CHUNK, unroll=UNROLL)
    def _(k):
        at = pl.multiple_of(k * CHUNK, CHUNK)
        ones = spreader(at, CHUNK, radial, dirs)
        row = 0
        for out in outs:
            count = out.shape[0]
            left = packed[pl.ds(row, count), :]
            out[:, pl.ds(at, CHUNK)] = jnp.dot(left, ones, preferred_element_type=F32)
            row += count


def blocks_of(design):
    dirs = design.shape[1]
    row = lax.broadcasted_iota(jnp.int32, (CHUNK, dirs), 0)
    col = lax.broadcasted_iota(jnp.int32, (CHUNK, dirs), 1)
    pick = jnp.where((row & (dirs - 1)) == col, 1.0, 0.0).astype(BF16)
    tiled = jnp.dot(pick, design, preferred_element_type=F32).astype(BF16)
    tiled = lax.dot_general(tiled, pick, (((1,), (1,)), ((), ())), preferred_element_type=F32)
    row = lax.broadcasted_iota(jnp.int32, (CHUNK, CHUNK), 0)
    col = lax.broadcasted_iota(jnp.int32, (CHUNK, CHUNK), 1)
    shift = dirs.bit_length() - 1
    return jnp.where((row >> shift) == (col >> shift), tiled, 0.0).astype(BF16)


def wall(radial):
    lane = lax.broadcasted_iota(jnp.int32, (1, radial), 1)
    return jnp.where(lane < radial - 1, 1.0, 0.0)


def ahead_x(rows, last):
    n = rows.shape[0]
    at = lax.broadcasted_iota(jnp.int32, rows.shape, 0)
    return jnp.where(at == n - 1, last, pltpu.roll(rows, n - 1, 0))


def behind_x(rows, first):
    at = lax.broadcasted_iota(jnp.int32, rows.shape, 0)
    return jnp.where(at == 0, first, pltpu.roll(rows, 1, 0))


def ahead_r(rows, dirs):
    return pltpu.roll(rows, rows.shape[1] - dirs, 1)


def behind_r(rows, dirs):
    return pltpu.roll(rows, dirs, 1)


def even_az():
    return lax.rem(lax.axis_index("az"), 2) == 0


def radial_weights(radial):
    return (lax.broadcasted_iota(jnp.int32, (1, radial), 1).astype(F32) + 0.5) / radial


EDGE = ((0, 0), (0, 2), (0, 3), (1, 0), (1, 3), (2, 0), (2, 3))


def edge_kernel(
    tangent, velocity, frac, branch, basis, design, exit_film,
    msg_e, msg_o, sums,
    field, vel, share, share_2, kind, kind_2, left, mat, film, vel_tan, packed, spread, work, ends, edge, faces, face_a, sems,
):
    cells, rows, lanes = field.shape
    radial = vel.shape[-1]
    dirs = lanes // radial
    last, end = cells - 1, rows - 1
    inner = wall(radial)
    pairs = [
        (exit_film, film), (velocity, vel), (branch.at[0], kind), (frac.at[0], share), (frac.at[1, 0, last], share_2),
        (branch.at[1, 0, last], kind_2), (design, mat), (tangent, field),
    ]
    copies = [pltpu.make_async_copy(src, dst, sems.at[i]) for i, (src, dst) in enumerate(pairs)]
    base = len(copies)
    copies += [
        pltpu.make_async_copy(basis.at[c, a], left.at[pl.ds(i * rows, rows)], sems.at[base + i])
        for i, (c, a) in enumerate(EDGE)
    ]
    for copy in copies:
        copy.start()
    copies[0].wait()
    sums[...] = jnp.full(sums.shape, jnp.sum(film[...] * radial_weights(radial)), F32)
    for copy in copies[1:6]:
        copy.wait()

    at = {}
    row = 0
    for c, a in EDGE:
        low, high = mix(vel[c, a], kind[c, a])
        if (c, a) == (0, last):
            high_a = high
        if c == 1:
            at["high", a] = high
        for name, part in zip("plh", (share[c, a], low, high), strict=True):
            packed[pl.ds(row, rows), :] = two_terms(part * inner if c == 2 else part)
            at[name, c, a] = row
            row += rows
    low_2, high_2 = mix(vel[0, last], kind_2[...])
    for name, part in zip("pl", (share_2[...], low_2), strict=True):
        packed[pl.ds(row, rows), :] = two_terms(part)
        at[name] = row
        row += rows
    spread_all(packed, [spread], radial, dirs)

    for copy in copies[6:]:
        copy.wait()
    weights = blocks_of(mat[...])

    @pl.loop(0, lanes // CHUNK, unroll=UNROLL)
    def _(k):
        lane = pl.ds(pl.multiple_of(k * CHUNK, CHUNK), CHUNK)
        vel_tan[:, lane] = jnp.dot(left[:, lane], weights, preferred_element_type=F32).astype(BF16)

    def sp(*key):
        return spread[pl.ds(at[key], rows), :]

    def speed(c, a):
        return vel_tan[pl.ds(EDGE.index((c, a)) * rows, rows), :].astype(F32)

    def along_az(a):
        f = field[a]
        face = speed(0, a) * sp("p", 0, a) + sp("l", 0, a) * f
        return face if a == last else face + sp("h", 0, a) * field[a + 1]

    faces[0] = along_az(0)
    faces[1] = along_az(last - 1)
    face_a[...] = along_az(last)
    for i, a in enumerate((0, last)):
        f = field[a]
        change = faces[0] if a == 0 else face_a[...] - faces[1]
        face = speed(1, a) * sp("p", 1, a) + sp("l", 1, a) * f + sp("h", 1, a) * ahead_x(f, 0.0)
        ends[pl.ds(i, 1), :] = face[end:, :]
        change = change + (face - behind_x(face, 0.0))
        face = speed(2, a) * sp("p", 2, a) + sp("l", 2, a) * f + sp("h", 2, a) * ahead_r(f, dirs)
        change = change + (face - behind_r(face, dirs))
        edge[i] = f - change
    work[...] = speed(0, last) * spread[pl.ds(at["p"], rows), :] + spread[pl.ds(at["l"], rows), :] * edge[1]

    def small_rows(msg, lane, block):
        for k in range(lanes // CHUNK):
            msg[pl.ds(2 * rows + k, 1), pl.ds(lane, CHUNK)] = block[:, k * CHUNK:(k + 1) * CHUNK]

    def halves(msg, lane, block):
        for k in range(rows // 8):
            msg[pl.ds(2 * rows, 8), pl.ds(lane + 128 * k, radial)] = block[8 * k:8 * k + 8]

    def fill(up_msg, down_msg):
        for msg in (up_msg, down_msg):
            msg[pl.ds(2 * rows, 8), :] = jnp.zeros((8, lanes), F32)
        up_msg[pl.ds(0, rows), :] = face_a[...]
        up_msg[pl.ds(rows, rows), :] = work[...]
        halves(up_msg, AT_C1, high_a)
        halves(up_msg, AT_B2, low_2)
        halves(up_msg, AT_C2, high_2)
        small_rows(up_msg, AT_ROW_A, ends[pl.ds(1, 1), :])
        small_rows(up_msg, AT_ROW_B, field[last, pl.ds(0, 1), :])
        small_rows(up_msg, AT_FIRST, sp("h", 0, last)[0:1])
        small_rows(up_msg, AT_END, sp("h", 0, last)[end:])
        up_msg[pl.ds(2 * rows, 1), pl.ds(AT_COEF, radial)] = at["high", last][end:, :]
        down_msg[pl.ds(0, rows), :] = field[0]
        down_msg[pl.ds(rows, rows), :] = edge[0]
        small_rows(down_msg, AT_ROW_A, ends[pl.ds(0, 1), :])
        down_msg[pl.ds(2 * rows, 1), pl.ds(AT_COEF, radial)] = at["high", 0][end:, :]

    even = even_az()

    @pl.when(even)
    def _():
        fill(msg_e, msg_o)

    @pl.when(jnp.logical_not(even))
    def _():
        fill(msg_o, msg_e)


MIDDLE = dict(
    ends=0, end_fixed=4, low_end=8, first=12, partial_first=16, partial_end=20, front=24, coef_a=26, coefs=28
)


def local_kernel(
    tangent, velocity, frac, branch, basis, design, exit_film,
    vel_tan, coef_2, middle, partial, fixed, edges,
    field, vel, share, kind, left, mat, film, product, packed, spread, mixed, sems,
):
    cells, rows, lanes = field.shape
    radial = vel.shape[-1]
    dirs = lanes // radial
    n = cells * rows
    last, end = cells - 1, rows - 1
    inner = wall(radial)
    pairs = [
        (velocity, vel), (branch, kind), (frac, share), (design, mat), (basis, left), (tangent, field), (exit_film, film),
    ]
    copies = [pltpu.make_async_copy(src, dst, sems.at[i]) for i, (src, dst) in enumerate(pairs)]
    for copy in copies:
        copy.start()
    for copy in copies[:3]:
        copy.wait()

    for step in range(2):
        for c in range(3):
            low, high = mix(vel[c], kind[step, c])
            for k, part in enumerate((share[step, c], low, high)):
                part = part.reshape(n, radial)
                part = two_terms(part * inner if c == 2 else part)
                if step == 0 or k == 0:
                    packed[pl.ds(((step * 3 + k) * 3 + c) * n, n), :] = part
                else:
                    for a in range(cells):
                        row = 12 * n + ((a * 2 + k - 1) * 3 + c) * rows
                        packed[pl.ds(row, rows), :] = part[a * rows:(a + 1) * rows]
            if c == 1:
                segments = [(0, high)] if step == 0 else [(6, low), (10, high)]
                if step == 0:
                    middle[pl.ds(MIDDLE["coefs"], 1), :] = jnp.zeros((1, lanes), F32)
                for start, part in segments:
                    for a in range(cells):
                        middle[pl.ds(MIDDLE["coefs"], 1), pl.ds(128 * (start + a), radial)] = part[a, end:, :]
    spread_all(packed, [spread, mixed], radial, dirs)
    done = [pltpu.make_async_copy(mixed, coef_2, sems.at[len(copies) + 1])]
    done[0].start()
    for copy in copies[3:5]:
        copy.wait()
    weights = blocks_of(mat[...])

    @pl.loop(0, lanes // CHUNK, unroll=UNROLL)
    def _(k):
        lane = pl.ds(pl.multiple_of(k * CHUNK, CHUNK), CHUNK)
        block = jnp.dot(left[:, :, :, lane].reshape(3 * n, CHUNK), weights, preferred_element_type=F32)
        product[:, :, :, lane] = block.astype(BF16).reshape(3, cells, rows, CHUNK)

    done.append(pltpu.make_async_copy(product, vel_tan, sems.at[len(copies)]))
    done[-1].start()
    for copy in copies[5:]:
        copy.wait()

    def sp(k, c, a):
        return spread[pl.ds((k * 3 + c) * n + a * rows, rows), :]

    def speed(c, a):
        return product[c, a].astype(F32)

    def put(name, a, block):
        middle[pl.ds(MIDDLE[name] + a, block.shape[0]), :] = block

    before = before_2 = None
    for a in range(cells):
        f = field[a]
        here = speed(0, a) * sp(0, 0, a) + sp(1, 0, a) * f
        if a < last:
            here = here + sp(2, 0, a) * field[a + 1]
        change = here if before is None else here - before
        before = here
        face = speed(1, a) * sp(0, 1, a) + sp(1, 1, a) * f + sp(2, 1, a) * ahead_x(f, 0.0)
        put("ends", a, face[end:])
        edges[pl.ds(2 * rows + a, 1), :] = face[end:]
        change = change + (face - behind_x(face, 0.0))
        face = speed(2, a) * sp(0, 2, a) + sp(1, 2, a) * f + sp(2, 2, a) * ahead_r(f, dirs)
        change = change + (face - behind_r(face, dirs))
        block = f - change
        partial[a] = block
        put("first", a, f[0:1])
        edges[pl.ds(2 * rows + 4 + a, 1), :] = f[0:1]
        put("partial_first", a, block[0:1])
        put("partial_end", a, block[end:])
        put("low_end", a, mixed[pl.ds((a * 6 + 1) * rows + end, 1), :])
        edges[pl.ds(2 * rows + 8 + a, 1), :] = sp(2, 1, a)[end:]
        here_2 = speed(0, a) * sp(3, 0, a)
        change = here_2 if before_2 is None else here_2 - before_2
        before_2 = here_2
        face = speed(1, a) * sp(3, 1, a)
        put("end_fixed", a, face[end:])
        change = change + (face - behind_x(face, 0.0))
        face = speed(2, a) * sp(3, 2, a)
        fixed[a] = change + (face - behind_r(face, dirs))
    edges[pl.ds(0, rows), :] = before
    edges[pl.ds(2 * rows + 16, rows), :] = field[0]
    edges[pl.ds(rows, rows), :] = sp(2, 0, last)
    for k, x in enumerate((0, end)):
        put("front", k, field[0, pl.ds(x, 1), :])
        put("coef_a", k, sp(2, 0, last)[x:x + 1])
    row_film = jnp.sum(film[...] * radial_weights(radial), axis=1, keepdims=True)
    edges[pl.ds(2 * rows + 12, cells), :] = jnp.broadcast_to(row_film, (cells, lanes))
    for copy in done:
        copy.wait()


def gathered_row(msg, row, lane, lanes):
    return jnp.concatenate([msg[pl.ds(row + k, 1), pl.ds(lane, CHUNK)] for k in range(lanes // CHUNK)], axis=1)


def middle_kernel(
    middle, in_e, in_o, totals,
    msg_e, msg_o, film_msg,
):
    cells, rows, lanes = CELLS, (in_e.shape[0] - 8) // 2, in_e.shape[1]
    radial, dirs = RADIAL, lanes // RADIAL
    last, end = cells - 1, rows - 1

    def take(name, count=CELLS, at=0):
        return middle[pl.ds(MIDDLE[name] + at, count), :]

    even = even_az()

    def work(up, down, out_up, out_down):
        at_a = lax.broadcasted_iota(jnp.int32, (cells, 1), 0)
        partial_x = []
        for k, (x, lane, name) in enumerate(((0, AT_FIRST, "partial_first"), (end, AT_END, "partial_end"))):
            face = up[pl.ds(x, 1), :] + gathered_row(up, 2 * rows, lane, lanes) * take("front", 1, k)
            beyond = take("coef_a", 1, k) * down[pl.ds(x, 1), :]
            partial_x.append(take(name) + jnp.where(at_a == 0, face, 0.0) - jnp.where(at_a == last, beyond, 0.0))
        second = take("end_fixed") + take("low_end") * partial_x[1]

        lane = lax.broadcasted_iota(jnp.int32, (1, lanes), 1)
        weight = ((lane // dirs).astype(F32) + 0.5) / radial
        raw = (take("ends") + second) * weight
        film = raw[:, 0:128]
        for k in range(1, lanes // 128):
            film = film + raw[:, 128 * k:128 * k + 128]
        shift = 64
        while shift >= dirs:
            film = film + pltpu.roll(film, shift, 1)
            shift //= 2
        quarter = jnp.sum(totals[...], axis=0)
        film_msg[...] = jnp.zeros(film_msg.shape, F32)
        film_msg[pl.ds(0, cells), :] = film
        film_msg[pl.ds(cells, 1), :] = quarter

        def finish(up_msg, down_msg):
            for msg in (up_msg, down_msg):
                msg[1, pl.ds(2, 2), :] = jnp.zeros((2, lanes), F32)
                for a in range(cells):
                    msg[1, pl.ds(3, 1), pl.ds(128 * a, 128)] = film[a:a + 1]
                msg[1, pl.ds(3, 1), pl.ds(128 * cells, 128)] = quarter
            up_msg[0] = take("ends")
            up_msg[1, pl.ds(0, 1), :] = gathered_row(up, 2 * rows, AT_ROW_A, lanes)
            up_msg[1, pl.ds(1, 1), :] = gathered_row(down, 2 * rows, AT_ROW_A, lanes)
            up_msg[1, pl.ds(2, 1), :] = take("coefs", 1)
            up_msg[1, pl.ds(2, 1), pl.ds(128 * 4, radial)] = up[pl.ds(2 * rows, 1), pl.ds(AT_COEF, radial)]
            up_msg[1, pl.ds(2, 1), pl.ds(128 * 5, radial)] = down[pl.ds(2 * rows, 1), pl.ds(AT_COEF, radial)]
            up_msg[2] = second
            down_msg[0] = take("first")
            down_msg[1, pl.ds(0, 1), :] = gathered_row(up, 2 * rows, AT_ROW_B, lanes)
            down_msg[1, pl.ds(1, 1), :] = down[pl.ds(0, 1), :]
            down_msg[2] = partial_x[0]

        even_x = lax.rem(lax.axis_index("ax"), 2) == 0

        @pl.when(even_x)
        def _():
            finish(out_up, out_down)

        @pl.when(jnp.logical_not(even_x))
        def _():
            finish(out_down, out_up)

    @pl.when(even)
    def _():
        work(in_o, in_e, msg_e, msg_o)

    @pl.when(jnp.logical_not(even))
    def _():
        work(in_e, in_o, msg_e, msg_o)


def last_kernel(
    coef_2, partial, fixed, edges, in_e, in_o, x_e, x_o, film_own, film_1,
    out, film_out,
    packed, spread, up, down, below, above, now, edge, result, mixed, sems,
):
    cells, rows, lanes = partial.shape
    radial = packed.shape[1] // 2
    dirs = lanes // radial
    n = cells * rows
    last, end = cells - 1, rows - 1
    even = even_az()
    place = lax.axis_index("ax")
    even_x = lax.rem(place, 2) == 0
    final = lax.axis_size("ax") - 1
    layer = 6 * rows
    loads = [
        pltpu.make_async_copy(coef_2.at[pl.ds(a * layer, layer)], mixed.at[pl.ds(a * layer, layer)], sems.at[cells + a])
        for a in range(cells)
    ]
    for copy in loads:
        copy.start()

    @pl.when(even)
    def _():
        up[...] = in_o[...]
        down[...] = in_e[...]

    @pl.when(jnp.logical_not(even))
    def _():
        up[...] = in_e[...]
        down[...] = in_o[...]

    @pl.when(even_x)
    def _():
        below[...] = jnp.where(place == 0, 0.0, x_o[...])
        above[...] = x_e[...]

    @pl.when(jnp.logical_not(even_x))
    def _():
        below[...] = x_e[...]
        above[...] = jnp.where(place == final, 0.0, x_o[...])

    face_a, coef_a = edges[pl.ds(0, rows), :], edges[pl.ds(rows, rows), :]
    ends, first, coef_x = (edges[pl.ds(2 * rows + 4 * k, cells), :] for k in range(3))

    def joined(msg, lane):
        return jnp.concatenate([msg[pl.ds(2 * rows, 8), pl.ds(lane + 128 * k, radial)] for k in range(rows // 8)], axis=0)

    for k, lane in enumerate((AT_C1, AT_B2, AT_C2)):
        packed[pl.ds(k * rows, rows), :] = two_terms(joined(up, lane))
    singles = [below[1, pl.ds(2, 1), pl.ds(128 * k, radial)] for k in range(14)]
    singles += [msg[pl.ds(2 * rows, 1), pl.ds(AT_COEF, radial)] for msg in (up, down)]
    packed[pl.ds(3 * rows, 16), :] = two_terms(jnp.concatenate(singles, axis=0))
    spread_all(packed, [spread], radial, dirs)
    in_c1, in_b2, in_c2 = (spread[pl.ds(k * rows, rows), :] for k in range(3))
    below_c = spread[pl.ds(3 * rows, 6), :]
    below_b2, below_c2 = spread[pl.ds(3 * rows + 6, 4), :], spread[pl.ds(3 * rows + 10, 4), :]
    own_c = jnp.concatenate([coef_x, spread[pl.ds(3 * rows + 14, 2), :]], axis=0)

    starts = jnp.concatenate([first, gathered_row(up, 2 * rows, AT_ROW_B, lanes), down[pl.ds(0, 1), :]], axis=0)
    enter = jnp.concatenate([below[0], below[1, pl.ds(0, 2), :]], axis=0) + below_c * starts
    leave = own_c * jnp.concatenate([above[0], above[1, pl.ds(0, 2), :]], axis=0)
    crossing = in_c1 * edges[pl.ds(2 * rows + 16, rows), :]
    beyond = coef_a * down[pl.ds(0, rows), :]
    at_x = lax.broadcasted_iota(jnp.int32, (rows, 1), 0)

    def with_edges(block, k):
        return block + jnp.where(at_x == 0, enter[k:k + 1], 0.0) - jnp.where(at_x == end, leave[k:k + 1], 0.0)

    for a in range(cells):
        f = partial[a]
        if a == 0:
            f = f + up[pl.ds(0, rows), :] + crossing
        if a == last:
            f = f - beyond
        now[a] = with_edges(f, a)
    now[cells] = with_edges(down[pl.ds(rows, rows), :] + face_a + beyond, 5)
    lower = up[pl.ds(rows, rows), :] + in_b2 * (
        jnp.where(at_x == 0, enter[4:5], 0.0) - jnp.where(at_x == end, leave[4:5], 0.0) - crossing
    )
    before = lower + in_c2 * now[0]

    first_now = jnp.concatenate([now[a, pl.ds(0, 1), :] for a in range(cells)], axis=0)
    enter_2 = below[2] - below_b2 * (below_c[0:4] * first) + below_c2 * first_now
    inside = jnp.where(place == final, 0.0, 1.0)
    edge[...] = inside * (above[2] + ends + leave[0:4])

    def low(c, a):
        return mixed[pl.ds((a * 6 + c) * rows, rows), :]

    def high(c, a):
        return mixed[pl.ds((a * 6 + 3 + c) * rows, rows), :]

    copies = []
    for a in range(cells):
        loads[a].wait()
        f = now[a]
        face = low(0, a) * f + high(0, a) * now[a + 1]
        change = fixed[a] + (face - before)
        before = face
        face = low(1, a) * f + high(1, a) * ahead_x(f, edge[pl.ds(a, 1), :])
        change = change + (face - behind_x(face, enter_2[a:a + 1]))
        face = low(2, a) * f + high(2, a) * ahead_r(f, dirs)
        change = change + (face - behind_r(face, dirs))
        result[a] = f - change
        copies.append(pltpu.make_async_copy(result.at[a], out.at[a], sems.at[a]))
        copies[a].start()

    share = film_out.shape[1]
    total = film_own[pl.ds(cells, 1), :] + film_1[pl.ds(cells, 1), :]
    for msg in (x_e, x_o):
        total = total + msg[1, pl.ds(3, 1), pl.ds(128 * cells, 128)]
    mean = total / (cells * lax.axis_size("az"))
    factor = mean / edges[pl.ds(2 * rows + 12, cells), pl.ds(0, 128)]
    for k, source in enumerate((x_o, film_1, x_e, film_own)):

        @pl.when(place == k)
        def _():
            if len(source.shape) == 2:
                film = source[pl.ds(0, cells), :]
            else:
                film = jnp.concatenate([source[1, pl.ds(3, 1), pl.ds(128 * a, 128)] for a in range(cells)], axis=0)
            film_out[...] = (film * factor)[:, k * share:(k + 1) * share]

    for copy in copies:
        copy.wait()


def swap(value, axis, pairing):
    count = lax.axis_size(axis)
    if axis == "ax":
        other = [i ^ pairing for i in range(count)]
    elif pairing == 0:
        other = [i ^ 1 for i in range(count)]
    else:
        other = [(i - 1 if i % 2 == 0 else i + 1) % count for i in range(count)]
    return lax.ppermute(value, axis, list(enumerate(other)))


def quarter_sums(value):
    count, quarters = lax.axis_size("az"), lax.axis_size("ax")
    part = count // quarters
    pairs = [
        ((i + part * j) % count * quarters + j, i * quarters + j) for i in range(count) for j in range(quarters)
    ]
    value = lax.ppermute(value, ("az", "ax"), pairs)
    groups = [list(range(part * k, part * (k + 1))) for k in range(quarters)]
    return lax.all_to_all(value, "az", 0, 0, axis_index_groups=groups)


def pinned(value, space):
    return pltpu.with_memory_space_constraint(value, space)


def placed(space, shape, dtype):
    return space(shape, dtype)


def call(kernel, args, outs, scratch, in_hbm=0, out_hbm=0, free=0, sems=0, cost=None):
    vmem, hbm = pl.BlockSpec(memory_space=pltpu.VMEM), pl.BlockSpec(memory_space=pl.ANY)
    shapes = [pltpu.VMEM(shape, dtype) for shape, dtype in scratch]
    pinned_outs = len(outs) - free
    shapes_out = [placed(pltpu.HBM if i < out_hbm else pltpu.VMEM, *out) for i, out in enumerate(outs[:pinned_outs])]
    shapes_out += [jax.ShapeDtypeStruct(*out) for out in outs[pinned_outs:]]
    args = [pinned(arg, pltpu.HBM if i < in_hbm else pltpu.VMEM) for i, arg in enumerate(args)]
    if sems:
        shapes.append(pltpu.SemaphoreType.DMA((sems,)))
    return pl.pallas_call(
        kernel,
        out_shape=shapes_out,
        in_specs=[hbm] * in_hbm + [vmem] * (len(args) - in_hbm),
        out_specs=[hbm] * out_hbm + [vmem] * (len(outs) - out_hbm),
        scratch_shapes=shapes,
        compiler_params=pltpu.CompilerParams(vmem_limit_bytes=32 * 2**20),
        cost_estimate=cost,
        name=kernel.__name__,
    )(*args)


def local(tangent, velocity, face_frac, branch, basis, design, exit_film):
    cells, rows, lanes = tangent.shape
    radial = velocity.shape[-1]
    dirs = design.shape[1]
    n = cells * rows
    devices = lax.axis_size("az")
    layer, cell_layer = (rows, lanes), (rows, radial)
    z_msg, x_msg, line = (2 * rows + 8, lanes), (3, cells, lanes), (cells, lanes)
    inputs = (tangent, velocity, face_frac, branch, basis, design, exit_film)
    count = (3 * len(EDGE) + 2) * rows
    z_e, z_o, sums = call(
        edge_kernel,
        inputs,
        [(z_msg, F32), (z_msg, F32), ((devices // lax.axis_size("ax"), 1, 128), F32)],
        [
            (tangent.shape, F32), (velocity.shape, F32), (velocity.shape, F32), (cell_layer, F32),
            (velocity.shape, branch.dtype), (cell_layer, branch.dtype), ((len(EDGE) * rows, lanes), BF16),
            (design.shape, BF16), (exit_film.shape, F32), ((len(EDGE) * rows, lanes), BF16),
            ((count, 2 * radial), BF16), ((count, lanes), F32), (layer, F32), ((2, lanes), F32),
            ((2, *layer), F32), ((2, *layer), F32), (layer, F32),
        ],
        in_hbm=7,
        sems=8 + len(EDGE),
    )
    in_e, in_o = swap(z_e, "az", 0), swap(z_o, "az", 1)
    totals = quarter_sums(sums)
    velocity_tangent, coef_2, middle, partial, fixed, edges = call(
        local_kernel,
        inputs,
        [
            (basis.shape, BF16), ((6 * n, lanes), F32), ((32, lanes), F32), (tangent.shape, F32), (tangent.shape, F32),
            ((3 * rows + 16, lanes), F32),
        ],
        [
            (tangent.shape, F32), (velocity.shape, F32), (face_frac.shape, F32), (branch.shape, branch.dtype),
            (basis.shape, BF16), (design.shape, BF16), (exit_film.shape, F32), (basis.shape, BF16),
            ((18 * n, 2 * radial), BF16), ((12 * n, lanes), F32), ((6 * n, lanes), F32),
        ],
        in_hbm=7,
        out_hbm=2,
        sems=9,
        cost=pl.CostEstimate(flops=10**9, bytes_accessed=16 * 10**6, transcendentals=0),
    )
    x_e, x_o, film = call(
        middle_kernel, (middle, in_e, in_o, totals), [(x_msg, F32), (x_msg, F32), ((8, 128), F32)], []
    )
    from_o, from_e, film_1 = swap(x_o, "ax", 3), swap(x_e, "ax", 1), swap(film, "ax", 2)
    count = 3 * rows + 16
    out, film_out = call(
        last_kernel,
        (coef_2, partial, fixed, edges, in_e, in_o, from_e, from_o, film, film_1),
        [(tangent.shape, F32), ((cells, dirs // lax.axis_size("ax")), F32)],
        [
            ((count, 2 * radial), BF16), ((count, lanes), F32), (z_msg, F32), (z_msg, F32), (x_msg, F32), (x_msg, F32),
            ((cells + 1, *layer), F32), (line, F32), (tangent.shape, F32), ((6 * n, lanes), F32),
        ],
        in_hbm=1,
        out_hbm=1,
        free=1,
        sems=2 * cells,
    )
    return out, velocity_tangent, film_out


def solution(mesh):
    in_specs = (
        P("az", "ax", None),
        P(None, "az", "ax", None),
        P(None, None, "az", "ax", None),
        P(None, None, "az", "ax", None),
        P(None, "az", "ax", None),
        P(),
        P("az", None),
    )
    out_specs = (P("az", "ax", None), P(None, "az", "ax", None), P("az", "ax"))
    return jax.shard_map(local, mesh=mesh, in_specs=in_specs, out_specs=out_specs, check_vma=False)
```

time: 311 us -> 46.1 us (0.15)
  blocking collectives: 163 us -> 0 us
  local copies, waits for them, and re-layouts: 70.6 us -> 0 us
  starting transfers between devices: 48.7 us -> 25.3 us
  other arithmetic: 17.8 us -> 0 us
  Pallas kernels: 0 us -> 10.8 us
  waiting for transfers between devices: 3.3 us -> 9.1 us
  matrix products: 4.2 us -> 0 us
    psum x1 -> x0, blocking collectives: 158 us -> none  [local(): mean_film = lax.psum(jnp.sum(row_film), 'az') / total_cells]
    reshape x4 -> x0, local copies, waits for them, and re-layouts: 29.1 us -> none  [the longest x2 21.1 us: spread(): return jnp.repeat(values, dirs, axis=-1)]
    broadcast_in_dim x9 -> x0, local copies, waits for them, and re-layouts: 27 us -> none  [spread(): return jnp.repeat(values, dirs, axis=-1)]
    ppermute x8 -> x6, starting transfers between devices: 48.7 us -> 21.8 us  [the longest x5 18.7 us: swap(): return lax.ppermute(value, axis, list(enumerate(other)))]
    pallas_call x0 -> x4, Pallas kernels: none -> 10.8 us  [call(): pl.pallas_call(kernel, out_shape=shapes_out, in_specs=[hbm] * in_hbm + [v...]
    mul x4 -> x0, other arithmetic: 9.89 us -> none  [the longest x2 8.24 us: local(): face_flux(field, jnp.concatenate([field[..., dirs:], blank], -1), speed[2...]
    slice x17 -> x0, local copies, waits for them, and re-layouts: 6.75 us -> none  [the longest x2 2.04 us: local(): change = upper - jnp.concatenate([lower_face, upper[:-1]], 0)]
    unnamed x1 -> x0, blocking collectives: 5.38 us -> none
  transfers between devices with their start and end apart: 8 -> 7, of which waited for: 1 -> 3; matrix products, arithmetic and copies ran while one was open for 24% -> 0% of each run, Pallas kernels for 0% -> 10%
where the time goes in v1:
time: 46.1 us; the launch traced here: 45.9 us
  starting transfers between devices  25.3 us (55%)
  Pallas kernels  10.8 us (23%)
  waiting for transfers between devices  9.1 us (20%)
  between operations  0.68 us (1%)
    ppermute x5, starting transfers between devices, swap(): return lax.ppermute(value, axis, list(enumerate(other)))  18.7 us
    pallas_call x4, Pallas kernels, call(): pl.pallas_call(kernel, out_shape=shapes_out, in_specs=[hbm] * in_hbm + [v...  10.8 us
    all_to_all x1, starting transfers between devices, quarter_sums(): return lax.all_to_all(value, 'az', 0, 0, axis_index_groups=groups)  3.48 us
    ppermute x1, waiting for transfers between devices, quarter_sums(): value = lax.ppermute(value, ('az', 'ax'), pairs)  3.3 us
    ppermute x1, starting transfers between devices, quarter_sums(): value = lax.ppermute(value, ('az', 'ax'), pairs)  3.07 us
    ppermute x5, waiting for transfers between devices, swap(): return lax.ppermute(value, axis, list(enumerate(other)))  3.07 us
    all_to_all x1, waiting for transfers between devices, quarter_sums(): return lax.all_to_all(value, 'az', 0, 0, axis_index_groups=groups)  2.73 us
  transfers between devices with their start and end apart: 7, of which 3 were waited for; matrix products, arithmetic and copies ran while one was open for 0% of the time, Pallas kernels for 10%

profile of v1, /device:TPU:1, one launch (start us, length us, event | category | flops | bytes accessed | tf_op | source)
XLA Modules:
  0.0 45.9 jit_solution(12166839995076933794)
XLA Ops:
  0.6 2.7 %edge_kernel.1 = (f32[40,2048]{1,0:T(8,128)S(1)}, f32[40,2048]{1,0:T(8,128)S(1)}, f32[16,1,128]{2,1,0:T(1,128)S(1)}) custom-call(f32[4,16,2048]{2,1,0:T(8,128)} %tangent.3, f32[3,4,16,64]{3,2,1,0:T(8,128)} %velocity.3, f32[2,3,4,16,64]{4,3,2,1,0:T(8,128)} %frac.3, s32[2,3,4,16,64]{4,3,2,1,0:T(8,128)} %branch.3, bf16[3,4,16,2048]{3,2,1,0:T(8,128)(2,1)} %basis.3, ...), custom_call_target="tpu_custom_call" | custom-call | tf_op jit(solution)/shard_map/edge_kernel/pallas_call | solution.py:574
  3.3 3.8 %collective-permute-start = (f32[40,2048]{1,0:T(8,128)S(1)}, f32[40,2048]{1,0:T(8,128)S(1)}, u32[]{:S(2)}, u32[]{:S(2)}) collective-permute-start(f32[40,2048]{1,0:T(8,128)S(1)} %get-tuple-element.21), channel_id=1, source_target_pairs={{0,4},{4,0},{8,12},{12,8},{16,20},{20,16},{24,28},{28,24},{32,36},... | collective-permute-start | bytes 983048 | tf_op jit(solution)/shard_map/ppermute | solution.py:543
  7.2 7.6 %collective-permute-start.1 = (f32[40,2048]{1,0:T(8,128)S(1)}, f32[40,2048]{1,0:T(8,128)S(1)}, u32[]{:S(2)}, u32[]{:S(2)}) collective-permute-start(f32[40,2048]{1,0:T(8,128)S(1)} %get-tuple-element.22), channel_id=1, source_target_pairs={{0,252},{4,8},{8,4},{12,16},{16,12},{20,24},{24,20},{28,32},{32,28... | collective-permute-start | bytes 983048 | tf_op jit(solution)/shard_map/ppermute | solution.py:543
  14.8 3.1 %collective-permute-start.2 = (f32[16,1,128]{2,1,0:T(1,128)S(1)}, f32[16,1,128]{2,1,0:T(1,128)}, u32[]{:S(2)}, u32[]{:S(2)}) collective-permute-start(f32[16,1,128]{2,1,0:T(1,128)S(1)} %get-tuple-element.24), channel_id=1, source_target_pairs={{0,0},{65,1},{130,2},{195,3},{4,4},{69,5},{134,6},{199,7},{8,8},{7... | collective-permute-start | bytes 24584 | tf_op jit(solution)/shard_map/ppermute | solution.py:552
  17.8 3.3 %collective-permute-done.2 = f32[16,1,128]{2,1,0:T(1,128)} collective-permute-done((f32[16,1,128]{2,1,0:T(1,128)S(1)}, f32[16,1,128]{2,1,0:T(1,128)}, u32[]{:S(2)}, u32[]{:S(2)}) %collective-permute-start.2) | collective-permute-done | bytes 8224 | tf_op jit(solution)/shard_map/ppermute | solution.py:552
  21.1 3.5 %all-to-all-start = ((f32[16,1,128]{2,1,0:T(1,128)}), f32[16,1,128]{2,1,0:T(1,128)S(1)}, u32[]{:S(2)}, u32[]{:S(2)}) async-start(f32[16,1,128]{2,1,0:T(1,128)} %collective-permute-done.2), calls=%async_computation | async-start | bytes 16384 | tf_op jit(solution)/shard_map/all_to_all | solution.py:554
  24.6 4.5 %local_kernel.1 = (bf16[3,4,16,2048]{3,2,1,0:T(8,128)(2,1)}, f32[384,2048]{1,0:T(8,128)}, f32[32,2048]{1,0:T(8,128)S(1)}, f32[4,16,2048]{2,1,0:T(8,128)S(1)}, f3...) custom-call(f32[4,16,2048]{2,1,0:T(8,128)} %tangent.3, f32[3,4,16,64]{3,2,1,0:T(8,128)} %velocity.3, ...), custom_call_target="tpu_custom_call" | custom-call | flops 1000000000 | bytes 16000000 | tf_op jit(solution)/shard_map/local_kernel/pallas_call | solution.py:574
  29.2 2.7 %all-to-all-done.totals = f32[16,1,128]{2,1,0:T(1,128)S(1)} async-done(((f32[16,1,128]{2,1,0:T(1,128)}), f32[16,1,128]{2,1,0:T(1,128)S(1)}, u32[]{:S(2)}, u32[]{:S(2)}) %all-to-all-start) | async-done | bytes 8224 | tf_op jit(solution)/shard_map/all_to_all | solution.py:554
  31.9 0.0 collective-permute-done.in_e
  31.9 0.0 collective-permute-done.1.in_o
  31.9 0.2 middle_kernel.1
  32.1 0.1 collective-permute-start.3
  32.2 7.2 %collective-permute-start.4 = (f32[3,4,2048]{2,1,0:T(4,128)S(1)}, f32[3,4,2048]{2,1,0:T(4,128)S(1)}, u32[]{:S(2)}, u32[]{:S(2)}) collective-permute-start(f32[3,4,2048]{2,1,0:T(4,128)S(1)} %get-tuple-element.26), channel_id=1, source_target_pairs={{0,3},{1,2},{2,1},{3,0},{4,7},{5,6},{6,5},{7,4},{8,11},{9,10},{10,... | collective-permute-start | bytes 294920 | tf_op jit(solution)/shard_map/ppermute | solution.py:543
  39.4 0.1 collective-permute-start.5
  39.5 3.0 %collective-permute-done.5.film_1 = f32[8,128]{1,0:T(8,128)S(1)} collective-permute-done((f32[8,128]{1,0:T(8,128)S(1)}, f32[8,128]{1,0:T(8,128)S(1)}, u32[]{:S(2)}, u32[]{:S(2)}) %collective-permute-start.5) | collective-permute-done | bytes 4128 | tf_op jit(solution)/shard_map/ppermute | solution.py:543
  42.5 0.0 collective-permute-done.3.x_e
  42.5 0.0 collective-permute-done.4.x_o
  42.5 3.3 %last_kernel.1 = (f32[4,16,2048]{2,1,0:T(8,128)}, f32[4,8]{1,0:T(4,128)}) custom-call(f32[384,2048]{1,0:T(8,128)} %get-tuple-element.17.coef_2, f32[4,16,2048]{2,1,0:T(8,128)S(1)} %get-tuple-element.18.partial, f32[4,16,2048]{2,1,0:T(8,128)S(1)} %get-tuple-element.19.fixed, f32[64,2048]{1,0:T(8,128)S(1)} %get-tuple-element.20.edges, ...), custom_call_target="tpu_custom_call" | custom-call | tf_op jit(solution)/shard_map/last_kernel/pallas_call | solution.py:574
Async XLA Ops:
  3.3 28.6 %collective-permute-start = (f32[40,2048]{1,0:T(8,128)S(1)}, f32[40,2048]{1,0:T(8,128)S(1)}, u32[]{:S(2)}, u32[]{:S(2)}) collective-permute-start(f32[40,2048]{1,0:T(8,128)S(1)} %get-tuple-element.21), channel_id=1, source_target_pairs={{0,4},{4,0},{8,12},{12,8},{16,20},{20,16},{24,28},{28,24},{32,36},... | collective-permute-start | bytes 983048 | tf_op jit(solution)/shard_map/ppermute | solution.py:543
  7.2 24.7 %collective-permute-start.1 = (f32[40,2048]{1,0:T(8,128)S(1)}, f32[40,2048]{1,0:T(8,128)S(1)}, u32[]{:S(2)}, u32[]{:S(2)}) collective-permute-start(f32[40,2048]{1,0:T(8,128)S(1)} %get-tuple-element.22), channel_id=1, source_target_pairs={{0,252},{4,8},{8,4},{12,16},{16,12},{20,24},{24,20},{28,32},{32,28... | collective-permute-start | bytes 983048 | tf_op jit(solution)/shard_map/ppermute | solution.py:543
  14.8 6.4 %collective-permute-start.2 = (f32[16,1,128]{2,1,0:T(1,128)S(1)}, f32[16,1,128]{2,1,0:T(1,128)}, u32[]{:S(2)}, u32[]{:S(2)}) collective-permute-start(f32[16,1,128]{2,1,0:T(1,128)S(1)} %get-tuple-element.24), channel_id=1, source_target_pairs={{0,0},{65,1},{130,2},{195,3},{4,4},{69,5},{134,6},{199,7},{8,8},{7... | collective-permute-start | bytes 24584 | tf_op jit(solution)/shard_map/ppermute | solution.py:552
  21.1 10.8 %all-to-all-start = ((f32[16,1,128]{2,1,0:T(1,128)}), f32[16,1,128]{2,1,0:T(1,128)S(1)}, u32[]{:S(2)}, u32[]{:S(2)}) async-start(f32[16,1,128]{2,1,0:T(1,128)} %collective-permute-done.2), calls=%async_computation | async-start | bytes 16384 | tf_op jit(solution)/shard_map/all_to_all | solution.py:554
  32.1 10.3 %collective-permute-start.3 = (f32[3,4,2048]{2,1,0:T(4,128)S(1)}, f32[3,4,2048]{2,1,0:T(4,128)S(1)}, u32[]{:S(2)}, u32[]{:S(2)}) collective-permute-start(f32[3,4,2048]{2,1,0:T(4,128)S(1)} %get-tuple-element.25), channel_id=1, source_target_pairs={{0,1},{1,0},{2,3},{3,2},{4,5},{5,4},{6,7},{7,6},{8,9},{9,8},{10,11... | collective-permute-start | bytes 294920 | tf_op jit(solution)/shard_map/ppermute | solution.py:543
  32.2 10.3 %collective-permute-start.4 = (f32[3,4,2048]{2,1,0:T(4,128)S(1)}, f32[3,4,2048]{2,1,0:T(4,128)S(1)}, u32[]{:S(2)}, u32[]{:S(2)}) collective-permute-start(f32[3,4,2048]{2,1,0:T(4,128)S(1)} %get-tuple-element.26), channel_id=1, source_target_pairs={{0,3},{1,2},{2,1},{3,0},{4,7},{5,6},{6,5},{7,4},{8,11},{9,10},{10,... | collective-permute-start | bytes 294920 | tf_op jit(solution)/shard_map/ppermute | solution.py:543
  39.4 3.1 %collective-permute-start.5 = (f32[8,128]{1,0:T(8,128)S(1)}, f32[8,128]{1,0:T(8,128)S(1)}, u32[]{:S(2)}, u32[]{:S(2)}) collective-permute-start(f32[8,128]{1,0:T(8,128)S(1)} %get-tuple-element.27.film_own), channel_id=1, source_target_pairs={{0,2},{1,3},{2,0},{3,1},{4,6},{5,7},{6,4},{7,5},{8,10},{9,11},{10,... | collective-permute-start | bytes 12296 | tf_op jit(solution)/shard_map/ppermute | solution.py:543

commit v2 on v1

--- a/solution.py
+++ b/solution.py
@@ -326,6 +326,11 @@
         copy.wait()
 
 
+def after_kernel(done, value, out):
+    del done
+    out[...] = value[...]
+
+
 def gathered_row(msg, row, lane, lanes):
     return jnp.concatenate([msg[pl.ds(row + k, 1), pl.ds(lane, CHUNK)] for k in range(lanes // CHUNK)], axis=1)
 
@@ -405,7 +410,7 @@
 
 
 def last_kernel(
-    coef_2, partial, fixed, edges, in_e, in_o, x_e, x_o, film_own, film_1,
+    coef_2, partial, fixed, edges, in_e, in_o, film_own, film_1, x_o, x_e,
     out, film_out,
     packed, spread, up, down, below, above, now, edge, result, mixed, sems,
 ):
@@ -543,13 +548,18 @@
     return lax.ppermute(value, axis, list(enumerate(other)))
 
 
-def quarter_sums(value):
+def shifted_by_quarters(value):
     count, quarters = lax.axis_size("az"), lax.axis_size("ax")
     part = count // quarters
     pairs = [
         ((i + part * j) % count * quarters + j, i * quarters + j) for i in range(count) for j in range(quarters)
     ]
-    value = lax.ppermute(value, ("az", "ax"), pairs)
+    return lax.ppermute(value, ("az", "ax"), pairs)
+
+
+def quarter_sums(value):
+    count, quarters = lax.axis_size("az"), lax.axis_size("ax")
+    part = count // quarters
     groups = [list(range(part * k, part * (k + 1))) for k in range(quarters)]
     return lax.all_to_all(value, "az", 0, 0, axis_index_groups=groups)
 
@@ -607,8 +617,8 @@
         in_hbm=7,
         sems=8 + len(EDGE),
     )
+    other_sums = shifted_by_quarters(sums)
     in_e, in_o = swap(z_e, "az", 0), swap(z_o, "az", 1)
-    totals = quarter_sums(sums)
     velocity_tangent, coef_2, middle, partial, fixed, edges = call(
         local_kernel,
         inputs,
@@ -626,14 +636,17 @@
         sems=9,
         cost=pl.CostEstimate(flops=10**9, bytes_accessed=16 * 10**6, transcendentals=0),
     )
+    (ready_sums,) = call(after_kernel, (coef_2, other_sums), [(sums.shape, F32)], [], in_hbm=1)
+    totals = quarter_sums(ready_sums)
     x_e, x_o, film = call(
         middle_kernel, (middle, in_e, in_o, totals), [(x_msg, F32), (x_msg, F32), ((8, 128), F32)], []
     )
-    from_o, from_e, film_1 = swap(x_o, "ax", 3), swap(x_e, "ax", 1), swap(film, "ax", 2)
+    film_1 = swap(film, "ax", 2)
+    from_o, from_e = swap(x_o, "ax", 3), swap(x_e, "ax", 1)
     count = 3 * rows + 16
     out, film_out = call(
         last_kernel,
-        (coef_2, partial, fixed, edges, in_e, in_o, from_e, from_o, film, film_1),
+        (coef_2, partial, fixed, edges, in_e, in_o, film, film_1, from_o, from_e),
         [(tangent.shape, F32), ((cells, dirs // lax.axis_size("ax")), F32)],
         [
             ((count, 2 * radial), BF16), ((count, lanes), F32), (z_msg, F32), (z_msg, F32), (x_msg, F32), (x_msg, F32),

time: 46.1 us -> 45.1 us (0.978)
  blocking collectives: 0 us -> 12.3 us
  waiting for transfers between devices: 9.1 us -> 2.24 us
  starting transfers between devices: 25.3 us -> 18.9 us
    all_to_all x0 -> x1, blocking collectives: none -> 12.3 us  [quarter_sums(): return lax.all_to_all(value, 'az', 0, 0, axis_index_groups=groups)]
    all_to_all x1 -> x0, starting transfers between devices: 3.48 us -> none  [quarter_sums(): return lax.all_to_all(value, 'az', 0, 0, axis_index_groups=groups)]
    ppermute x1, waiting for transfers between devices: 3.3 us -> 0.01 us  [shifted_by_quarters(): return lax.ppermute(value, ('az', 'ax'), pairs)]
    ppermute x5, starting transfers between devices: 18.7 us -> 15.9 us  [swap(): return lax.ppermute(value, axis, list(enumerate(other)))]
    all_to_all x1 -> x0, waiting for transfers between devices: 2.73 us -> none  [quarter_sums(): return lax.all_to_all(value, 'az', 0, 0, axis_index_groups=groups)]
    ppermute x5, waiting for transfers between devices: 3.07 us -> 2.24 us  [swap(): return lax.ppermute(value, axis, list(enumerate(other)))]
    pallas_call x4 -> x5, Pallas kernels: 10.8 us -> 10.8 us  [call(): pl.pallas_call(kernel, out_shape=shapes_out, in_specs=[hbm] * in_hbm + [v...]
  transfers between devices with their start and end apart: 7 -> 6, of which waited for: 3 -> 1; matrix products, arithmetic and copies ran while one was open for 0% -> 0% of each run, Pallas kernels for 10% -> 10%
where the time goes in v2:
time: 45.1 us; the launch traced here: 44.9 us
  starting transfers between devices  18.9 us (42%)
  blocking collectives  12.3 us (27%)
  Pallas kernels  10.8 us (24%)
  waiting for transfers between devices  2.24 us (5%)
  between operations  0.68 us (2%)
    ppermute x5, starting transfers between devices, swap(): return lax.ppermute(value, axis, list(enumerate(other)))  15.9 us
    all_to_all x1, blocking collectives, quarter_sums(): return lax.all_to_all(value, 'az', 0, 0, axis_index_groups=groups)  12.3 us
    pallas_call x5, Pallas kernels, call(): pl.pallas_call(kernel, out_shape=shapes_out, in_specs=[hbm] * in_hbm + [v...  10.8 us
    ppermute x1, starting transfers between devices, shifted_by_quarters(): return lax.ppermute(value, ('az', 'ax'), pairs)  3.07 us
    ppermute x5, waiting for transfers between devices, swap(): return lax.ppermute(value, axis, list(enumerate(other)))  2.24 us
  transfers between devices with their start and end apart: 6, of which 1 were waited for; matrix products, arithmetic and copies ran while one was open for 0% of the time, Pallas kernels for 10%

profile of v2, /device:TPU:1, one launch (start us, length us, event | category | flops | bytes accessed | tf_op | source)
XLA Modules:
  0.0 44.9 jit_solution(16195397433391914870)
XLA Ops:
  0.6 2.7 %edge_kernel.1 = (f32[40,2048]{1,0:T(8,128)S(1)}, f32[40,2048]{1,0:T(8,128)S(1)}, f32[16,1,128]{2,1,0:T(1,128)S(1)}) custom-call(f32[4,16,2048]{2,1,0:T(8,128)} %tangent.3, f32[3,4,16,64]{3,2,1,0:T(8,128)} %velocity.3, f32[2,3,4,16,64]{4,3,2,1,0:T(8,128)} %frac.3, s32[2,3,4,16,64]{4,3,2,1,0:T(8,128)} %branch.3, bf16[3,4,16,2048]{3,2,1,0:T(8,128)(2,1)} %basis.3, ...), custom_call_target="tpu_custom_call" | custom-call | tf_op jit(solution)/shard_map/edge_kernel/pallas_call | solution.py:584
  3.3 3.8 %collective-permute-start = (f32[40,2048]{1,0:T(8,128)S(1)}, f32[40,2048]{1,0:T(8,128)S(1)}, u32[]{:S(2)}, u32[]{:S(2)}) collective-permute-start(f32[40,2048]{1,0:T(8,128)S(1)} %get-tuple-element.21), channel_id=1, source_target_pairs={{0,4},{4,0},{8,12},{12,8},{16,20},{20,16},{24,28},{28,24},{32,36},... | collective-permute-start | bytes 983048 | tf_op jit(solution)/shard_map/ppermute | solution.py:548
  7.2 7.6 %collective-permute-start.1 = (f32[40,2048]{1,0:T(8,128)S(1)}, f32[40,2048]{1,0:T(8,128)S(1)}, u32[]{:S(2)}, u32[]{:S(2)}) collective-permute-start(f32[40,2048]{1,0:T(8,128)S(1)} %get-tuple-element.22), channel_id=1, source_target_pairs={{0,252},{4,8},{8,4},{12,16},{16,12},{20,24},{24,20},{28,32},{32,28... | collective-permute-start | bytes 983048 | tf_op jit(solution)/shard_map/ppermute | solution.py:548
  14.8 3.1 %collective-permute-start.2 = (f32[16,1,128]{2,1,0:T(1,128)S(1)}, f32[16,1,128]{2,1,0:T(1,128)S(1)}, u32[]{:S(2)}, u32[]{:S(2)}) collective-permute-start(f32[16,1,128]{2,1,0:T(1,128)S(1)} %get-tuple-element.24), channel_id=1, source_target_pairs={{0,0},{65,1},{130,2},{195,3},{4,4},{69,5},{134,6},{199,7},{8,8},{7... | collective-permute-start | bytes 24584 | tf_op jit(solution)/shard_map/ppermute | solution.py:557
  17.8 4.5 %local_kernel.1 = (bf16[3,4,16,2048]{3,2,1,0:T(8,128)(2,1)}, f32[384,2048]{1,0:T(8,128)}, f32[32,2048]{1,0:T(8,128)S(1)}, f32[4,16,2048]{2,1,0:T(8,128)S(1)}, f3...) custom-call(f32[4,16,2048]{2,1,0:T(8,128)} %tangent.3, f32[3,4,16,64]{3,2,1,0:T(8,128)} %velocity.3, ...), custom_call_target="tpu_custom_call" | custom-call | flops 1000000000 | bytes 16000000 | tf_op jit(solution)/shard_map/local_kernel/pallas_call | solution.py:584
  22.4 0.0 collective-permute-done.2.value
  22.4 12.3 %all_to_all.5.totals = f32[16,1,128]{2,1,0:T(1,128)S(1)} all-to-all(f32[16,1,128]{2,1,0:T(1,128)S(1)} %after_kernel.1), channel_id=1, replica_groups={{0,4,8,12,16,20,24,28,32,36,40,44,48,52,56,60},{64,68,72,76,80,84,88,92..., dimensions={0} | all-to-all | bytes 16384 | tf_op jit(solution)/shard_map/all_to_all | solution.py:564
  34.7 0.0 collective-permute-done.in_e
  34.7 0.0 collective-permute-done.1.in_o
  34.7 0.2 middle_kernel.1
  34.9 4.2 %collective-permute-start.4 = (f32[3,4,2048]{2,1,0:T(4,128)S(1)}, f32[3,4,2048]{2,1,0:T(4,128)S(1)}, u32[]{:S(2)}, u32[]{:S(2)}) collective-permute-start(f32[3,4,2048]{2,1,0:T(4,128)S(1)} %get-tuple-element.26), channel_id=1, source_target_pairs={{0,3},{1,2},{2,1},{3,0},{4,7},{5,6},{6,5},{7,4},{8,11},{9,10},{10,... | collective-permute-start | bytes 294920 | tf_op jit(solution)/shard_map/ppermute | solution.py:548
  39.1 0.0 collective-permute-start.5
  39.1 0.2 collective-permute-start.3
  39.4 2.2 %collective-permute-done.3.film_1 = f32[8,128]{1,0:T(8,128)S(1)} collective-permute-done((f32[8,128]{1,0:T(8,128)S(1)}, f32[8,128]{1,0:T(8,128)S(1)}, u32[]{:S(2)}, u32[]{:S(2)}) %collective-permute-start.3) | collective-permute-done | bytes 4128 | tf_op jit(solution)/shard_map/ppermute | solution.py:548
  41.6 0.0 collective-permute-done.4.x_o
  41.6 0.0 collective-permute-done.5.x_e
  41.6 3.3 %last_kernel.1 = (f32[4,16,2048]{2,1,0:T(8,128)}, f32[4,8]{1,0:T(4,128)}) custom-call(f32[384,2048]{1,0:T(8,128)} %get-tuple-element.17.done.coef_2, f32[4,16,2048]{2,1,0:T(8,128)S(1)} %get-tuple-element.18.partial, f32[4,16,2048]{2,1,0:T(8,128)S(1)} %get-tuple-element.19.fixed, f32[64,2048]{1,0:T(8,128)S(1)} %get-tuple-element.20.edges, ...), custom_call_target="tpu_custom_call" | custom-call | tf_op jit(solution)/shard_map/last_kernel/pallas_call | solution.py:584
  (1 shorter events, 0.0 us)
Async XLA Ops:
  3.3 31.4 %collective-permute-start = (f32[40,2048]{1,0:T(8,128)S(1)}, f32[40,2048]{1,0:T(8,128)S(1)}, u32[]{:S(2)}, u32[]{:S(2)}) collective-permute-start(f32[40,2048]{1,0:T(8,128)S(1)} %get-tuple-element.21), channel_id=1, source_target_pairs={{0,4},{4,0},{8,12},{12,8},{16,20},{20,16},{24,28},{28,24},{32,36},... | collective-permute-start | bytes 983048 | tf_op jit(solution)/shard_map/ppermute | solution.py:548
  7.2 27.5 %collective-permute-start.1 = (f32[40,2048]{1,0:T(8,128)S(1)}, f32[40,2048]{1,0:T(8,128)S(1)}, u32[]{:S(2)}, u32[]{:S(2)}) collective-permute-start(f32[40,2048]{1,0:T(8,128)S(1)} %get-tuple-element.22), channel_id=1, source_target_pairs={{0,252},{4,8},{8,4},{12,16},{16,12},{20,24},{24,20},{28,32},{32,28... | collective-permute-start | bytes 983048 | tf_op jit(solution)/shard_map/ppermute | solution.py:548
  14.8 7.6 %collective-permute-start.2 = (f32[16,1,128]{2,1,0:T(1,128)S(1)}, f32[16,1,128]{2,1,0:T(1,128)S(1)}, u32[]{:S(2)}, u32[]{:S(2)}) collective-permute-start(f32[16,1,128]{2,1,0:T(1,128)S(1)} %get-tuple-element.24), channel_id=1, source_target_pairs={{0,0},{65,1},{130,2},{195,3},{4,4},{69,5},{134,6},{199,7},{8,8},{7... | collective-permute-start | bytes 24584 | tf_op jit(solution)/shard_map/ppermute | solution.py:557
  34.9 6.7 %collective-permute-start.4 = (f32[3,4,2048]{2,1,0:T(4,128)S(1)}, f32[3,4,2048]{2,1,0:T(4,128)S(1)}, u32[]{:S(2)}, u32[]{:S(2)}) collective-permute-start(f32[3,4,2048]{2,1,0:T(4,128)S(1)} %get-tuple-element.26), channel_id=1, source_target_pairs={{0,3},{1,2},{2,1},{3,0},{4,7},{5,6},{6,5},{7,4},{8,11},{9,10},{10,... | collective-permute-start | bytes 294920 | tf_op jit(solution)/shard_map/ppermute | solution.py:548
  39.1 2.5 %collective-permute-start.5 = (f32[3,4,2048]{2,1,0:T(4,128)S(1)}, f32[3,4,2048]{2,1,0:T(4,128)S(1)}, u32[]{:S(2)}, u32[]{:S(2)}) collective-permute-start(f32[3,4,2048]{2,1,0:T(4,128)S(1)} %get-tuple-element.27), channel_id=1, source_target_pairs={{0,1},{1,0},{2,3},{3,2},{4,5},{5,4},{6,7},{7,6},{8,9},{9,8},{10,11... | collective-permute-start | bytes 294920 | tf_op jit(solution)/shard_map/ppermute | solution.py:548
  39.1 2.5 %collective-permute-start.3 = (f32[8,128]{1,0:T(8,128)S(1)}, f32[8,128]{1,0:T(8,128)S(1)}, u32[]{:S(2)}, u32[]{:S(2)}) collective-permute-start(f32[8,128]{1,0:T(8,128)S(1)} %get-tuple-element.25.film_own), channel_id=1, source_target_pairs={{0,2},{1,3},{2,0},{3,1},{4,6},{5,7},{6,4},{7,5},{8,10},{9,11},{10,... | collective-permute-start | bytes 12296 | tf_op jit(solution)/shard_map/ppermute | solution.py:548

commit v3 on v1

--- a/solution.py
+++ b/solution.py
@@ -331,7 +331,7 @@
 
 
 def middle_kernel(
-    middle, in_e, in_o, totals,
+    middle, in_e, in_o,
     msg_e, msg_o, film_msg,
 ):
     cells, rows, lanes = CELLS, (in_e.shape[0] - 8) // 2, in_e.shape[1]
@@ -362,17 +362,14 @@
         while shift >= dirs:
             film = film + pltpu.roll(film, shift, 1)
             shift //= 2
-        quarter = jnp.sum(totals[...], axis=0)
         film_msg[...] = jnp.zeros(film_msg.shape, F32)
         film_msg[pl.ds(0, cells), :] = film
-        film_msg[pl.ds(cells, 1), :] = quarter
 
         def finish(up_msg, down_msg):
             for msg in (up_msg, down_msg):
                 msg[1, pl.ds(2, 2), :] = jnp.zeros((2, lanes), F32)
                 for a in range(cells):
                     msg[1, pl.ds(3, 1), pl.ds(128 * a, 128)] = film[a:a + 1]
-                msg[1, pl.ds(3, 1), pl.ds(128 * cells, 128)] = quarter
             up_msg[0] = take("ends")
             up_msg[1, pl.ds(0, 1), :] = gathered_row(up, 2 * rows, AT_ROW_A, lanes)
             up_msg[1, pl.ds(1, 1), :] = gathered_row(down, 2 * rows, AT_ROW_A, lanes)
@@ -405,7 +402,7 @@
 
 
 def last_kernel(
-    coef_2, partial, fixed, edges, in_e, in_o, x_e, x_o, film_own, film_1,
+    coef_2, partial, fixed, edges, in_e, in_o, film_own, film_1, x_o, x_e, totals,
     out, film_out,
     packed, spread, up, down, below, above, now, edge, result, mixed, sems,
 ):
@@ -513,10 +510,7 @@
         copies[a].start()
 
     share = film_out.shape[1]
-    total = film_own[pl.ds(cells, 1), :] + film_1[pl.ds(cells, 1), :]
-    for msg in (x_e, x_o):
-        total = total + msg[1, pl.ds(3, 1), pl.ds(128 * cells, 128)]
-    mean = total / (cells * lax.axis_size("az"))
+    mean = jnp.sum(totals[:, 0:1, :], axis=0) / (cells * totals.shape[0])
     factor = mean / edges[pl.ds(2 * rows + 12, cells), pl.ds(0, 128)]
     for k, source in enumerate((x_o, film_1, x_e, film_own)):
 
@@ -541,17 +535,6 @@
     else:
         other = [(i - 1 if i % 2 == 0 else i + 1) % count for i in range(count)]
     return lax.ppermute(value, axis, list(enumerate(other)))
-
-
-def quarter_sums(value):
-    count, quarters = lax.axis_size("az"), lax.axis_size("ax")
-    part = count // quarters
-    pairs = [
-        ((i + part * j) % count * quarters + j, i * quarters + j) for i in range(count) for j in range(quarters)
-    ]
-    value = lax.ppermute(value, ("az", "ax"), pairs)
-    groups = [list(range(part * k, part * (k + 1))) for k in range(quarters)]
-    return lax.all_to_all(value, "az", 0, 0, axis_index_groups=groups)
 
 
 def pinned(value, space):
@@ -596,7 +579,7 @@
     z_e, z_o, sums = call(
         edge_kernel,
         inputs,
-        [(z_msg, F32), (z_msg, F32), ((devices // lax.axis_size("ax"), 1, 128), F32)],
+        [(z_msg, F32), (z_msg, F32), ((devices, 2, 128), F32)],
         [
             (tangent.shape, F32), (velocity.shape, F32), (velocity.shape, F32), (cell_layer, F32),
             (velocity.shape, branch.dtype), (cell_layer, branch.dtype), ((len(EDGE) * rows, lanes), BF16),
@@ -608,7 +591,7 @@
         sems=8 + len(EDGE),
     )
     in_e, in_o = swap(z_e, "az", 0), swap(z_o, "az", 1)
-    totals = quarter_sums(sums)
+    totals = lax.all_to_all(sums, "az", 0, 0)
     velocity_tangent, coef_2, middle, partial, fixed, edges = call(
         local_kernel,
         inputs,
@@ -627,13 +610,13 @@
         cost=pl.CostEstimate(flops=10**9, bytes_accessed=16 * 10**6, transcendentals=0),
     )
     x_e, x_o, film = call(
-        middle_kernel, (middle, in_e, in_o, totals), [(x_msg, F32), (x_msg, F32), ((8, 128), F32)], []
+        middle_kernel, (middle, in_e, in_o), [(x_msg, F32), (x_msg, F32), ((8, 128), F32)], []
     )
     from_o, from_e, film_1 = swap(x_o, "ax", 3), swap(x_e, "ax", 1), swap(film, "ax", 2)
     count = 3 * rows + 16
     out, film_out = call(
         last_kernel,
-        (coef_2, partial, fixed, edges, in_e, in_o, from_e, from_o, film, film_1),
+        (coef_2, partial, fixed, edges, in_e, in_o, film, film_1, from_o, from_e, totals),
         [(tangent.shape, F32), ((cells, dirs // lax.axis_size("ax")), F32)],
         [
             ((count, 2 * radial), BF16), ((count, lanes), F32), (z_msg, F32), (z_msg, F32), (x_msg, F32), (x_msg, F32),

time: 46.1 us -> 37.6 us (0.82)
  waiting for transfers between devices: 9.1 us -> 3.3 us
  starting transfers between devices: 25.3 us -> 21.8 us
  Pallas kernels: 10.8 us -> 11.4 us
    ppermute x5, starting transfers between devices: 18.7 us -> 14.4 us  [swap(): return lax.ppermute(value, axis, list(enumerate(other)))]
    all_to_all x1, starting transfers between devices: 3.48 us -> 7.37 us  [local(): totals = lax.all_to_all(sums, 'az', 0, 0)]
    ppermute x1 -> x0, waiting for transfers between devices: 3.3 us -> none  [quarter_sums(): value = lax.ppermute(value, ('az', 'ax'), pairs)]
    ppermute x1 -> x0, starting transfers between devices: 3.07 us -> none  [quarter_sums(): value = lax.ppermute(value, ('az', 'ax'), pairs)]
    ppermute x5, waiting for transfers between devices: 3.07 us -> 0.01 us  [swap(): return lax.ppermute(value, axis, list(enumerate(other)))]
    pallas_call x4, Pallas kernels: 10.8 us -> 11.4 us  [call(): pl.pallas_call(kernel, out_shape=shapes_out, in_specs=[hbm] * in_hbm + [v...]
    all_to_all x1, waiting for transfers between devices: 2.73 us -> 3.29 us  [local(): totals = lax.all_to_all(sums, 'az', 0, 0)]
  transfers between devices with their start and end apart: 7 -> 6, of which waited for: 3 -> 1; matrix products, arithmetic and copies ran while one was open for 0% -> 0% of each run, Pallas kernels for 10% -> 13%
where the time goes in v3:
time: 37.6 us; the launch traced here: 37.2 us
  starting transfers between devices  21.8 us (58%)
  Pallas kernels  11.4 us (30%)
  waiting for transfers between devices  3.3 us (9%)
  between operations  0.68 us (2%)
    ppermute x5, starting transfers between devices, swap(): return lax.ppermute(value, axis, list(enumerate(other)))  14.4 us
    pallas_call x4, Pallas kernels, call(): pl.pallas_call(kernel, out_shape=shapes_out, in_specs=[hbm] * in_hbm + [v...  11.4 us
    all_to_all x1, starting transfers between devices, local(): totals = lax.all_to_all(sums, 'az', 0, 0)  7.37 us
    all_to_all x1, waiting for transfers between devices, local(): totals = lax.all_to_all(sums, 'az', 0, 0)  3.29 us
  transfers between devices with their start and end apart: 6, of which 1 were waited for; matrix products, arithmetic and copies ran while one was open for 0% of the time, Pallas kernels for 13%

profile of v3, /device:TPU:1, one launch (start us, length us, event | category | flops | bytes accessed | tf_op | source)
XLA Modules:
  0.0 37.2 jit_solution(15547265139887617629)
XLA Ops:
  0.6 3.3 %edge_kernel.1 = (f32[40,2048]{1,0:T(8,128)S(1)}, f32[40,2048]{1,0:T(8,128)S(1)}, f32[64,2,128]{2,1,0:T(2,128)}) custom-call(f32[4,16,2048]{2,1,0:T(8,128)} %tangent.3, f32[3,4,16,64]{3,2,1,0:T(8,128)} %velocity.3, f32[2,3,4,16,64]{4,3,2,1,0:T(8,128)} %frac.3, s32[2,3,4,16,64]{4,3,2,1,0:T(8,128)} %branch.3, bf16[3,4,16,2048]{3,2,1,0:T(8,128)(2,1)} %basis.3, ...), custom_call_target="tpu_custom_call" | custom-call | tf_op jit(solution)/shard_map/edge_kernel/pallas_call | solution.py:557
  4.0 3.8 %collective-permute-start = (f32[40,2048]{1,0:T(8,128)S(1)}, f32[40,2048]{1,0:T(8,128)S(1)}, u32[]{:S(2)}, u32[]{:S(2)}) collective-permute-start(f32[40,2048]{1,0:T(8,128)S(1)} %get-tuple-element.21), channel_id=1, source_target_pairs={{0,4},{4,0},{8,12},{12,8},{16,20},{20,16},{24,28},{28,24},{32,36},... | collective-permute-start | bytes 983048 | tf_op jit(solution)/shard_map/ppermute | solution.py:537
  7.8 7.6 %collective-permute-start.1 = (f32[40,2048]{1,0:T(8,128)S(1)}, f32[40,2048]{1,0:T(8,128)S(1)}, u32[]{:S(2)}, u32[]{:S(2)}) collective-permute-start(f32[40,2048]{1,0:T(8,128)S(1)} %get-tuple-element.22), channel_id=1, source_target_pairs={{0,252},{4,8},{8,4},{12,16},{16,12},{20,24},{24,20},{28,32},{32,28... | collective-permute-start | bytes 983048 | tf_op jit(solution)/shard_map/ppermute | solution.py:537
  15.4 7.4 %all-to-all-start = ((f32[64,2,128]{2,1,0:T(2,128)}), f32[64,2,128]{2,1,0:T(2,128)S(1)}, u32[]{:S(2)}, u32[]{:S(2)}) async-start(f32[64,2,128]{2,1,0:T(2,128)} %get-tuple-element.27), calls=%async_computation | async-start | bytes 131072 | tf_op jit(solution)/shard_map/all_to_all | solution.py:594
  22.8 4.5 %local_kernel.1 = (bf16[3,4,16,2048]{3,2,1,0:T(8,128)(2,1)}, f32[384,2048]{1,0:T(8,128)}, f32[32,2048]{1,0:T(8,128)S(1)}, f32[4,16,2048]{2,1,0:T(8,128)S(1)}, f3...) custom-call(f32[4,16,2048]{2,1,0:T(8,128)} %tangent.3, f32[3,4,16,64]{3,2,1,0:T(8,128)} %velocity.3, ...), custom_call_target="tpu_custom_call" | custom-call | flops 1000000000 | bytes 16000000 | tf_op jit(solution)/shard_map/local_kernel/pallas_call | solution.py:557
  27.3 0.0 collective-permute-done.in_e
  27.3 0.0 collective-permute-done.1.in_o
  27.3 0.2 middle_kernel.1
  27.6 1.9 %collective-permute-start.3 = (f32[3,4,2048]{2,1,0:T(4,128)S(1)}, f32[3,4,2048]{2,1,0:T(4,128)S(1)}, u32[]{:S(2)}, u32[]{:S(2)}) collective-permute-start(f32[3,4,2048]{2,1,0:T(4,128)S(1)} %get-tuple-element.25), channel_id=1, source_target_pairs={{0,3},{1,2},{2,1},{3,0},{4,7},{5,6},{6,5},{7,4},{8,11},{9,10},{10,... | collective-permute-start | bytes 294920 | tf_op jit(solution)/shard_map/ppermute | solution.py:537
  29.5 0.0 collective-permute-start.4
  29.5 1.1 %collective-permute-start.2 = (f32[8,128]{1,0:T(8,128)S(1)}, f32[8,128]{1,0:T(8,128)S(1)}, u32[]{:S(2)}, u32[]{:S(2)}) collective-permute-start(f32[8,128]{1,0:T(8,128)S(1)} %get-tuple-element.24.film_own), channel_id=1, source_target_pairs={{0,2},{1,3},{2,0},{3,1},{4,6},{5,7},{6,4},{7,5},{8,10},{9,11},{10,... | collective-permute-start | bytes 12296 | tf_op jit(solution)/shard_map/ppermute | solution.py:537
  30.5 3.3 %all-to-all-done.totals = f32[64,2,128]{2,1,0:T(2,128)S(1)} async-done(((f32[64,2,128]{2,1,0:T(2,128)}), f32[64,2,128]{2,1,0:T(2,128)S(1)}, u32[]{:S(2)}, u32[]{:S(2)}) %all-to-all-start) | async-done | bytes 65568 | tf_op jit(solution)/shard_map/all_to_all | solution.py:594
  33.8 0.0 collective-permute-done.2.film_1
  33.8 0.0 collective-permute-done.3.x_o
  33.8 0.0 collective-permute-done.4.x_e
  33.8 3.3 %last_kernel.1 = (f32[4,16,2048]{2,1,0:T(8,128)}, f32[4,8]{1,0:T(4,128)}) custom-call(f32[384,2048]{1,0:T(8,128)} %get-tuple-element.17.coef_2, f32[4,16,2048]{2,1,0:T(8,128)S(1)} %get-tuple-element.18.partial, f32[4,16,2048]{2,1,0:T(8,128)S(1)} %get-tuple-element.19.fixed, f32[64,2048]{1,0:T(8,128)S(1)} %get-tuple-element.20.edges, ...), custom_call_target="tpu_custom_call" | custom-call | tf_op jit(solution)/shard_map/last_kernel/pallas_call | solution.py:557
Async XLA Ops:
  4.0 23.4 %collective-permute-start = (f32[40,2048]{1,0:T(8,128)S(1)}, f32[40,2048]{1,0:T(8,128)S(1)}, u32[]{:S(2)}, u32[]{:S(2)}) collective-permute-start(f32[40,2048]{1,0:T(8,128)S(1)} %get-tuple-element.21), channel_id=1, source_target_pairs={{0,4},{4,0},{8,12},{12,8},{16,20},{20,16},{24,28},{28,24},{32,36},... | collective-permute-start | bytes 983048 | tf_op jit(solution)/shard_map/ppermute | solution.py:537
  7.8 19.5 %collective-permute-start.1 = (f32[40,2048]{1,0:T(8,128)S(1)}, f32[40,2048]{1,0:T(8,128)S(1)}, u32[]{:S(2)}, u32[]{:S(2)}) collective-permute-start(f32[40,2048]{1,0:T(8,128)S(1)} %get-tuple-element.22), channel_id=1, source_target_pairs={{0,252},{4,8},{8,4},{12,16},{16,12},{20,24},{24,20},{28,32},{32,28... | collective-permute-start | bytes 983048 | tf_op jit(solution)/shard_map/ppermute | solution.py:537
  15.4 18.4 %all-to-all-start = ((f32[64,2,128]{2,1,0:T(2,128)}), f32[64,2,128]{2,1,0:T(2,128)S(1)}, u32[]{:S(2)}, u32[]{:S(2)}) async-start(f32[64,2,128]{2,1,0:T(2,128)} %get-tuple-element.27), calls=%async_computation | async-start | bytes 131072 | tf_op jit(solution)/shard_map/all_to_all | solution.py:594
  27.6 6.2 %collective-permute-start.3 = (f32[3,4,2048]{2,1,0:T(4,128)S(1)}, f32[3,4,2048]{2,1,0:T(4,128)S(1)}, u32[]{:S(2)}, u32[]{:S(2)}) collective-permute-start(f32[3,4,2048]{2,1,0:T(4,128)S(1)} %get-tuple-element.25), channel_id=1, source_target_pairs={{0,3},{1,2},{2,1},{3,0},{4,7},{5,6},{6,5},{7,4},{8,11},{9,10},{10,... | collective-permute-start | bytes 294920 | tf_op jit(solution)/shard_map/ppermute | solution.py:537
  29.5 4.4 %collective-permute-start.4 = (f32[3,4,2048]{2,1,0:T(4,128)S(1)}, f32[3,4,2048]{2,1,0:T(4,128)S(1)}, u32[]{:S(2)}, u32[]{:S(2)}) collective-permute-start(f32[3,4,2048]{2,1,0:T(4,128)S(1)} %get-tuple-element.26), channel_id=1, source_target_pairs={{0,1},{1,0},{2,3},{3,2},{4,5},{5,4},{6,7},{7,6},{8,9},{9,8},{10,11... | collective-permute-start | bytes 294920 | tf_op jit(solution)/shard_map/ppermute | solution.py:537
  29.5 4.4 %collective-permute-start.2 = (f32[8,128]{1,0:T(8,128)S(1)}, f32[8,128]{1,0:T(8,128)S(1)}, u32[]{:S(2)}, u32[]{:S(2)}) collective-permute-start(f32[8,128]{1,0:T(8,128)S(1)} %get-tuple-element.24.film_own), channel_id=1, source_target_pairs={{0,2},{1,3},{2,0},{3,1},{4,6},{5,7},{6,4},{7,5},{8,10},{9,11},{10,... | collective-permute-start | bytes 12296 | tf_op jit(solution)/shard_map/ppermute | solution.py:537

commit v4 on v3

--- a/solution.py
+++ b/solution.py
@@ -220,7 +220,7 @@
 
 def local_kernel(
     tangent, velocity, frac, branch, basis, design, exit_film,
-    vel_tan, coef_2, middle, partial, fixed, edges,
+    vel_tan, coef_2, middle, partial, fixed, edges, weighted,
     field, vel, share, kind, left, mat, film, product, packed, spread, mixed, sems,
 ):
     cells, rows, lanes = field.shape
@@ -321,7 +321,8 @@
         put("front", k, field[0, pl.ds(x, 1), :])
         put("coef_a", k, sp(2, 0, last)[x:x + 1])
     row_film = jnp.sum(film[...] * radial_weights(radial), axis=1, keepdims=True)
-    edges[pl.ds(2 * rows + 12, cells), :] = jnp.broadcast_to(row_film, (cells, lanes))
+    weighted[...] = jnp.broadcast_to(row_film, weighted.shape)
+    edges[pl.ds(2 * rows + 12, 4), :] = jnp.zeros((4, lanes), F32)
     for copy in done:
         copy.wait()
 
@@ -402,8 +403,8 @@
 
 
 def last_kernel(
-    coef_2, partial, fixed, edges, in_e, in_o, film_own, film_1, x_o, x_e, totals,
-    out, film_out,
+    coef_2, partial, fixed, edges, in_e, in_o, x_o, x_e,
+    out,
     packed, spread, up, down, below, above, now, edge, result, mixed, sems,
 ):
     cells, rows, lanes = partial.shape
@@ -509,9 +510,16 @@
         copies.append(pltpu.make_async_copy(result.at[a], out.at[a], sems.at[a]))
         copies[a].start()
 
-    share = film_out.shape[1]
+    for copy in copies:
+        copy.wait()
+
+
+def film_kernel(done, row_film, film_own, film_1, x_o, x_e, totals, film_out):
+    del done
+    cells, share = film_out.shape
+    place = lax.axis_index("ax")
     mean = jnp.sum(totals[:, 0:1, :], axis=0) / (cells * totals.shape[0])
-    factor = mean / edges[pl.ds(2 * rows + 12, cells), pl.ds(0, 128)]
+    factor = mean / row_film[...]
     for k, source in enumerate((x_o, film_1, x_e, film_own)):
 
         @pl.when(place == k)
@@ -521,9 +529,6 @@
             else:
                 film = jnp.concatenate([source[1, pl.ds(3, 1), pl.ds(128 * a, 128)] for a in range(cells)], axis=0)
             film_out[...] = (film * factor)[:, k * share:(k + 1) * share]
-
-    for copy in copies:
-        copy.wait()
 
 
 def swap(value, axis, pairing):
@@ -592,12 +597,12 @@
     )
     in_e, in_o = swap(z_e, "az", 0), swap(z_o, "az", 1)
     totals = lax.all_to_all(sums, "az", 0, 0)
-    velocity_tangent, coef_2, middle, partial, fixed, edges = call(
+    velocity_tangent, coef_2, middle, partial, fixed, edges, row_film = call(
         local_kernel,
         inputs,
         [
             (basis.shape, BF16), ((6 * n, lanes), F32), ((32, lanes), F32), (tangent.shape, F32), (tangent.shape, F32),
-            ((3 * rows + 16, lanes), F32),
+            ((3 * rows + 16, lanes), F32), ((cells, 128), F32),
         ],
         [
             (tangent.shape, F32), (velocity.shape, F32), (face_frac.shape, F32), (branch.shape, branch.dtype),
@@ -614,18 +619,25 @@
     )
     from_o, from_e, film_1 = swap(x_o, "ax", 3), swap(x_e, "ax", 1), swap(film, "ax", 2)
     count = 3 * rows + 16
-    out, film_out = call(
+    (out,) = call(
         last_kernel,
-        (coef_2, partial, fixed, edges, in_e, in_o, film, film_1, from_o, from_e, totals),
-        [(tangent.shape, F32), ((cells, dirs // lax.axis_size("ax")), F32)],
+        (coef_2, partial, fixed, edges, in_e, in_o, from_o, from_e),
+        [(tangent.shape, F32)],
         [
             ((count, 2 * radial), BF16), ((count, lanes), F32), (z_msg, F32), (z_msg, F32), (x_msg, F32), (x_msg, F32),
             ((cells + 1, *layer), F32), (line, F32), (tangent.shape, F32), ((6 * n, lanes), F32),
         ],
         in_hbm=1,
         out_hbm=1,
+        sems=2 * cells,
+    )
+    (film_out,) = call(
+        film_kernel,
+        (out, row_film, film, film_1, from_o, from_e, totals),
+        [((cells, dirs // lax.axis_size("ax")), F32)],
+        [],
+        in_hbm=1,
         free=1,
-        sems=2 * cells,
     )
     return out, velocity_tangent, film_out
 

time: 37.6 us -> 36.4 us (0.968)
  waiting for transfers between devices: 3.3 us -> 2 us
    all_to_all x1, waiting for transfers between devices: 3.29 us -> 0.01 us  [local(): totals = lax.all_to_all(sums, 'az', 0, 0)]
    ppermute x5, waiting for transfers between devices: 0.01 us -> 2 us  [swap(): return lax.ppermute(value, axis, list(enumerate(other)))]
    pallas_call x4 -> x5, Pallas kernels: 11.4 us -> 11.6 us  [call(): pl.pallas_call(kernel, out_shape=shapes_out, in_specs=[hbm] * in_hbm + [v...]
  transfers between devices with their start and end apart: 6 -> 6, of which waited for: 1 -> 1; matrix products, arithmetic and copies ran while one was open for 0% -> 0% of each run, Pallas kernels for 13% -> 21%
where the time goes in v4:
time: 36.4 us; the launch traced here: 36 us
  starting transfers between devices  21.8 us (60%)
  Pallas kernels  11.6 us (32%)
  waiting for transfers between devices  2 us (5%)
  between operations  0.7 us (2%)
    ppermute x5, starting transfers between devices, swap(): return lax.ppermute(value, axis, list(enumerate(other)))  14.4 us
    pallas_call x5, Pallas kernels, call(): pl.pallas_call(kernel, out_shape=shapes_out, in_specs=[hbm] * in_hbm + [v...  11.6 us
    all_to_all x1, starting transfers between devices, local(): totals = lax.all_to_all(sums, 'az', 0, 0)  7.37 us
    ppermute x5, waiting for transfers between devices, swap(): return lax.ppermute(value, axis, list(enumerate(other)))  2 us
  transfers between devices with their start and end apart: 6, of which 1 were waited for; matrix products, arithmetic and copies ran while one was open for 0% of the time, Pallas kernels for 21%

profile of v4, /device:TPU:1, one launch (start us, length us, event | category | flops | bytes accessed | tf_op | source)
XLA Modules:
  0.0 36.0 jit_solution(14947444120699339093)
XLA Ops:
  0.6 3.3 %edge_kernel.1 = (f32[40,2048]{1,0:T(8,128)S(1)}, f32[40,2048]{1,0:T(8,128)S(1)}, f32[64,2,128]{2,1,0:T(2,128)}) custom-call(f32[4,16,2048]{2,1,0:T(8,128)} %tangent.3, f32[3,4,16,64]{3,2,1,0:T(8,128)} %velocity.3, f32[2,3,4,16,64]{4,3,2,1,0:T(8,128)} %frac.3, s32[2,3,4,16,64]{4,3,2,1,0:T(8,128)} %branch.3, bf16[3,4,16,2048]{3,2,1,0:T(8,128)(2,1)} %basis.3, ...), custom_call_target="tpu_custom_call" | custom-call | tf_op jit(solution)/shard_map/edge_kernel/pallas_call | solution.py:562
  3.9 3.8 %collective-permute-start = (f32[40,2048]{1,0:T(8,128)S(1)}, f32[40,2048]{1,0:T(8,128)S(1)}, u32[]{:S(2)}, u32[]{:S(2)}) collective-permute-start(f32[40,2048]{1,0:T(8,128)S(1)} %get-tuple-element.20), channel_id=1, source_target_pairs={{0,4},{4,0},{8,12},{12,8},{16,20},{20,16},{24,28},{28,24},{32,36},... | collective-permute-start | bytes 983048 | tf_op jit(solution)/shard_map/ppermute | solution.py:542
  7.8 7.6 %collective-permute-start.1 = (f32[40,2048]{1,0:T(8,128)S(1)}, f32[40,2048]{1,0:T(8,128)S(1)}, u32[]{:S(2)}, u32[]{:S(2)}) collective-permute-start(f32[40,2048]{1,0:T(8,128)S(1)} %get-tuple-element.21), channel_id=1, source_target_pairs={{0,252},{4,8},{8,4},{12,16},{16,12},{20,24},{24,20},{28,32},{32,28... | collective-permute-start | bytes 983048 | tf_op jit(solution)/shard_map/ppermute | solution.py:542
  15.4 7.4 %all-to-all-start = ((f32[64,2,128]{2,1,0:T(2,128)}), f32[64,2,128]{2,1,0:T(2,128)S(1)}, u32[]{:S(2)}, u32[]{:S(2)}) async-start(f32[64,2,128]{2,1,0:T(2,128)} %get-tuple-element.28), calls=%async_computation | async-start | bytes 131072 | tf_op jit(solution)/shard_map/all_to_all | solution.py:599
  22.7 4.5 %local_kernel.1 = (bf16[3,4,16,2048]{3,2,1,0:T(8,128)(2,1)}, f32[384,2048]{1,0:T(8,128)}, f32[32,2048]{1,0:T(8,128)S(1)}, f32[4,16,2048]{2,1,0:T(8,128)S(1)}, f3...) custom-call(f32[4,16,2048]{2,1,0:T(8,128)} %tangent.3, f32[3,4,16,64]{3,2,1,0:T(8,128)} %velocity.3, ...), custom_call_target="tpu_custom_call" | custom-call | flops 1000000000 | bytes 16000000 | tf_op jit(solution)/shard_map/local_kernel/pallas_call | solution.py:562
  27.3 0.0 collective-permute-done.in_e
  27.3 0.0 collective-permute-done.1.in_o
  27.3 0.2 middle_kernel.1
  27.6 1.9 %collective-permute-start.2 = (f32[3,4,2048]{2,1,0:T(4,128)S(1)}, f32[3,4,2048]{2,1,0:T(4,128)S(1)}, u32[]{:S(2)}, u32[]{:S(2)}) collective-permute-start(f32[3,4,2048]{2,1,0:T(4,128)S(1)} %get-tuple-element.23), channel_id=1, source_target_pairs={{0,3},{1,2},{2,1},{3,0},{4,7},{5,6},{6,5},{7,4},{8,11},{9,10},{10,... | collective-permute-start | bytes 294920 | tf_op jit(solution)/shard_map/ppermute | solution.py:542
  29.5 0.0 collective-permute-start.3
  29.5 1.1 %collective-permute-start.4 = (f32[8,128]{1,0:T(8,128)S(1)}, f32[8,128]{1,0:T(8,128)S(1)}, u32[]{:S(2)}, u32[]{:S(2)}) collective-permute-start(f32[8,128]{1,0:T(8,128)S(1)} %get-tuple-element.27.film_own), channel_id=1, source_target_pairs={{0,2},{1,3},{2,0},{3,1},{4,6},{5,7},{6,4},{7,5},{8,10},{9,11},{10,... | collective-permute-start | bytes 12296 | tf_op jit(solution)/shard_map/ppermute | solution.py:542
  30.5 2.0 %collective-permute-done.2.x_o = f32[3,4,2048]{2,1,0:T(4,128)S(1)} collective-permute-done((f32[3,4,2048]{2,1,0:T(4,128)S(1)}, f32[3,4,2048]{2,1,0:T(4,128)S(1)}, u32[]{:S(2)}, u32[]{:S(2)}) %collective-permute-start.2) | collective-permute-done | bytes 98336 | tf_op jit(solution)/shard_map/ppermute | solution.py:542
  32.5 0.0 collective-permute-done.3.x_e
  32.5 2.7 %last_kernel.1.done = f32[4,16,2048]{2,1,0:T(8,128)} custom-call(f32[384,2048]{1,0:T(8,128)} %get-tuple-element.16.coef_2, f32[4,16,2048]{2,1,0:T(8,128)S(1)} %get-tuple-element.17.partial, f32[4,16,2048]{2,1,0:T(8,128)S(1)} %get-tuple-element.18.fixed, f32[64,2048]{1,0:T(8,128)S(1)} %get-tuple-element.19.edges, f32[40,2048]{1,0:T(8,128)S(1)} %collective-permute-done.in_e, ...), custom_call_target="tpu_custom_call" | custom-call | tf_op jit(solution)/shard_map/last_kernel/pallas_call | solution.py:562
  35.3 0.0 all-to-all-done.totals
  35.3 0.0 collective-permute-done.4.film_1
  35.3 0.7 %film_kernel.1 = f32[4,8]{1,0:T(4,128)} custom-call(f32[4,16,2048]{2,1,0:T(8,128)} %last_kernel.1.done, f32[4,128]{1,0:T(4,128)S(1)} %get-tuple-element.26.row_film, f32[8,128]{1,0:T(8,128)S(1)} %get-tuple-element.27.film_own, f32[8,128]{1,0:T(8,128)S(1)} %collective-permute-done.4.film_1, f32[3,4,2048]{2,1,0:T(4,128)S(1)} %collective-permute-done.2.x_o, ...), custom_call_target="tpu_custom_call" | custom-call | tf_op jit(solution)/shard_map/film_kernel/pallas_call | solution.py:562
Async XLA Ops:
  3.9 23.4 %collective-permute-start = (f32[40,2048]{1,0:T(8,128)S(1)}, f32[40,2048]{1,0:T(8,128)S(1)}, u32[]{:S(2)}, u32[]{:S(2)}) collective-permute-start(f32[40,2048]{1,0:T(8,128)S(1)} %get-tuple-element.20), channel_id=1, source_target_pairs={{0,4},{4,0},{8,12},{12,8},{16,20},{20,16},{24,28},{28,24},{32,36},... | collective-permute-start | bytes 983048 | tf_op jit(solution)/shard_map/ppermute | solution.py:542
  7.8 19.5 %collective-permute-start.1 = (f32[40,2048]{1,0:T(8,128)S(1)}, f32[40,2048]{1,0:T(8,128)S(1)}, u32[]{:S(2)}, u32[]{:S(2)}) collective-permute-start(f32[40,2048]{1,0:T(8,128)S(1)} %get-tuple-element.21), channel_id=1, source_target_pairs={{0,252},{4,8},{8,4},{12,16},{16,12},{20,24},{24,20},{28,32},{32,28... | collective-permute-start | bytes 983048 | tf_op jit(solution)/shard_map/ppermute | solution.py:542
  15.4 19.9 %all-to-all-start = ((f32[64,2,128]{2,1,0:T(2,128)}), f32[64,2,128]{2,1,0:T(2,128)S(1)}, u32[]{:S(2)}, u32[]{:S(2)}) async-start(f32[64,2,128]{2,1,0:T(2,128)} %get-tuple-element.28), calls=%async_computation | async-start | bytes 131072 | tf_op jit(solution)/shard_map/all_to_all | solution.py:599
  27.6 4.9 %collective-permute-start.2 = (f32[3,4,2048]{2,1,0:T(4,128)S(1)}, f32[3,4,2048]{2,1,0:T(4,128)S(1)}, u32[]{:S(2)}, u32[]{:S(2)}) collective-permute-start(f32[3,4,2048]{2,1,0:T(4,128)S(1)} %get-tuple-element.23), channel_id=1, source_target_pairs={{0,3},{1,2},{2,1},{3,0},{4,7},{5,6},{6,5},{7,4},{8,11},{9,10},{10,... | collective-permute-start | bytes 294920 | tf_op jit(solution)/shard_map/ppermute | solution.py:542
  29.5 3.1 %collective-permute-start.3 = (f32[3,4,2048]{2,1,0:T(4,128)S(1)}, f32[3,4,2048]{2,1,0:T(4,128)S(1)}, u32[]{:S(2)}, u32[]{:S(2)}) collective-permute-start(f32[3,4,2048]{2,1,0:T(4,128)S(1)} %get-tuple-element.24), channel_id=1, source_target_pairs={{0,1},{1,0},{2,3},{3,2},{4,5},{5,4},{6,7},{7,6},{8,9},{9,8},{10,11... | collective-permute-start | bytes 294920 | tf_op jit(solution)/shard_map/ppermute | solution.py:542
  29.5 5.8 %collective-permute-start.4 = (f32[8,128]{1,0:T(8,128)S(1)}, f32[8,128]{1,0:T(8,128)S(1)}, u32[]{:S(2)}, u32[]{:S(2)}) collective-permute-start(f32[8,128]{1,0:T(8,128)S(1)} %get-tuple-element.27.film_own), channel_id=1, source_target_pairs={{0,2},{1,3},{2,0},{3,1},{4,6},{5,7},{6,4},{7,5},{8,10},{9,11},{10,... | collective-permute-start | bytes 12296 | tf_op jit(solution)/shard_map/ppermute | solution.py:542

commit v5 on v4

--- a/solution.py
+++ b/solution.py
@@ -220,8 +220,8 @@
 
 def local_kernel(
     tangent, velocity, frac, branch, basis, design, exit_film,
-    vel_tan, coef_2, middle, partial, fixed, edges, weighted,
-    field, vel, share, kind, left, mat, film, product, packed, spread, mixed, sems,
+    vel_tan, middle, partial, edges, row_film,
+    field, vel, share, kind, left, mat, film, product, packed, spread, sems,
 ):
     cells, rows, lanes = field.shape
     radial = vel.shape[-1]
@@ -238,28 +238,21 @@
     for copy in copies[:3]:
         copy.wait()
 
-    for step in range(2):
-        for c in range(3):
-            low, high = mix(vel[c], kind[step, c])
-            for k, part in enumerate((share[step, c], low, high)):
-                part = part.reshape(n, radial)
-                part = two_terms(part * inner if c == 2 else part)
-                if step == 0 or k == 0:
-                    packed[pl.ds(((step * 3 + k) * 3 + c) * n, n), :] = part
-                else:
-                    for a in range(cells):
-                        row = 12 * n + ((a * 2 + k - 1) * 3 + c) * rows
-                        packed[pl.ds(row, rows), :] = part[a * rows:(a + 1) * rows]
-            if c == 1:
-                segments = [(0, high)] if step == 0 else [(6, low), (10, high)]
-                if step == 0:
-                    middle[pl.ds(MIDDLE["coefs"], 1), :] = jnp.zeros((1, lanes), F32)
-                for start, part in segments:
-                    for a in range(cells):
-                        middle[pl.ds(MIDDLE["coefs"], 1), pl.ds(128 * (start + a), radial)] = part[a, end:, :]
-    spread_all(packed, [spread, mixed], radial, dirs)
-    done = [pltpu.make_async_copy(mixed, coef_2, sems.at[len(copies) + 1])]
-    done[0].start()
+    for c in range(3):
+        low, high = mix(vel[c], kind[0, c])
+        for k, part in enumerate((share[0, c], low, high)):
+            part = part.reshape(n, radial)
+            packed[pl.ds((k * 3 + c) * n, n), :] = two_terms(part * inner if c == 2 else part)
+        if c == 1:
+            high_1 = high
+    low_2, high_2 = mix(vel[1], kind[1, 1])
+    tail = [share[1, 1, :, end, :], low_2[:, end, :], jnp.zeros((8, radial), F32)]
+    packed[pl.ds(9 * n, 16), :] = two_terms(jnp.concatenate(tail, axis=0))
+    middle[pl.ds(MIDDLE["coefs"], 1), :] = jnp.zeros((1, lanes), F32)
+    for start, part in ((0, high_1), (6, low_2), (10, high_2)):
+        for a in range(cells):
+            middle[pl.ds(MIDDLE["coefs"], 1), pl.ds(128 * (start + a), radial)] = part[a, end:, :]
+    spread_all(packed, [spread], radial, dirs)
     for copy in copies[3:5]:
         copy.wait()
     weights = blocks_of(mat[...])
@@ -270,8 +263,8 @@
         block = jnp.dot(left[:, :, :, lane].reshape(3 * n, CHUNK), weights, preferred_element_type=F32)
         product[:, :, :, lane] = block.astype(BF16).reshape(3, cells, rows, CHUNK)
 
-    done.append(pltpu.make_async_copy(product, vel_tan, sems.at[len(copies)]))
-    done[-1].start()
+    output = pltpu.make_async_copy(product, vel_tan, sems.at[len(copies)])
+    output.start()
     for copy in copies[5:]:
         copy.wait()
 
@@ -284,7 +277,7 @@
     def put(name, a, block):
         middle[pl.ds(MIDDLE[name] + a, block.shape[0]), :] = block
 
-    before = before_2 = None
+    before = None
     for a in range(cells):
         f = field[a]
         here = speed(0, a) * sp(0, 0, a) + sp(1, 0, a) * f
@@ -292,7 +285,8 @@
             here = here + sp(2, 0, a) * field[a + 1]
         change = here if before is None else here - before
         before = here
-        face = speed(1, a) * sp(0, 1, a) + sp(1, 1, a) * f + sp(2, 1, a) * ahead_x(f, 0.0)
+        speed_x = speed(1, a)
+        face = speed_x * sp(0, 1, a) + sp(1, 1, a) * f + sp(2, 1, a) * ahead_x(f, 0.0)
         put("ends", a, face[end:])
         edges[pl.ds(2 * rows + a, 1), :] = face[end:]
         change = change + (face - behind_x(face, 0.0))
@@ -304,27 +298,60 @@
         edges[pl.ds(2 * rows + 4 + a, 1), :] = f[0:1]
         put("partial_first", a, block[0:1])
         put("partial_end", a, block[end:])
-        put("low_end", a, mixed[pl.ds((a * 6 + 1) * rows + end, 1), :])
+        put("low_end", a, spread[pl.ds(9 * n + cells + a, 1), :])
+        put("end_fixed", a, speed_x[end:] * spread[pl.ds(9 * n + a, 1), :])
         edges[pl.ds(2 * rows + 8 + a, 1), :] = sp(2, 1, a)[end:]
-        here_2 = speed(0, a) * sp(3, 0, a)
-        change = here_2 if before_2 is None else here_2 - before_2
-        before_2 = here_2
-        face = speed(1, a) * sp(3, 1, a)
-        put("end_fixed", a, face[end:])
-        change = change + (face - behind_x(face, 0.0))
-        face = speed(2, a) * sp(3, 2, a)
-        fixed[a] = change + (face - behind_r(face, dirs))
     edges[pl.ds(0, rows), :] = before
+    edges[pl.ds(2 * rows + 12, 4), :] = jnp.zeros((4, lanes), F32)
     edges[pl.ds(2 * rows + 16, rows), :] = field[0]
     edges[pl.ds(rows, rows), :] = sp(2, 0, last)
     for k, x in enumerate((0, end)):
         put("front", k, field[0, pl.ds(x, 1), :])
         put("coef_a", k, sp(2, 0, last)[x:x + 1])
-    row_film = jnp.sum(film[...] * radial_weights(radial), axis=1, keepdims=True)
-    weighted[...] = jnp.broadcast_to(row_film, weighted.shape)
-    edges[pl.ds(2 * rows + 12, 4), :] = jnp.zeros((4, lanes), F32)
-    for copy in done:
+    total = jnp.sum(film[...] * radial_weights(radial), axis=1, keepdims=True)
+    row_film[...] = jnp.broadcast_to(total, row_film.shape)
+    output.wait()
+
+
+def step_kernel(
+    velocity, frac, branch, vel_tan, after,
+    coef_2, fixed,
+    vel, share, kind, product, packed, spread, mixed, sems,
+):
+    del after
+    _, cells, rows, lanes = product.shape
+    radial = vel.shape[-1]
+    dirs = lanes // radial
+    n = cells * rows
+    inner = wall(radial)
+    pairs = [(velocity, vel), (branch.at[1], kind), (frac.at[1], share), (vel_tan, product)]
+    copies = [pltpu.make_async_copy(src, dst, sems.at[i]) for i, (src, dst) in enumerate(pairs)]
+    for copy in copies:
+        copy.start()
+    for copy in copies[:3]:
         copy.wait()
+    for c in range(3):
+        for k, part in enumerate((share[c], *mix(vel[c], kind[c]))):
+            part = part.reshape(n, radial)
+            part = two_terms(part * inner if c == 2 else part)
+            if k == 0:
+                packed[pl.ds(c * n, n), :] = part
+                continue
+            for a in range(cells):
+                row = 3 * n + ((a * 2 + k - 1) * 3 + c) * rows
+                packed[pl.ds(row, rows), :] = part[a * rows:(a + 1) * rows]
+    spread_all(packed, [spread, mixed], radial, dirs)
+    output = pltpu.make_async_copy(mixed, coef_2, sems.at[len(copies)])
+    output.start()
+    copies[3].wait()
+    before = None
+    for a in range(cells):
+        faces = [product[c, a].astype(F32) * spread[pl.ds(c * n + a * rows, rows), :] for c in range(3)]
+        change = faces[0] if before is None else faces[0] - before
+        before = faces[0]
+        change = change + (faces[1] - behind_x(faces[1], 0.0))
+        fixed[a] = change + (faces[2] - behind_r(faces[2], dirs))
+    output.wait()
 
 
 def gathered_row(msg, row, lane, lanes):
@@ -597,27 +624,40 @@
     )
     in_e, in_o = swap(z_e, "az", 0), swap(z_o, "az", 1)
     totals = lax.all_to_all(sums, "az", 0, 0)
-    velocity_tangent, coef_2, middle, partial, fixed, edges, row_film = call(
+    velocity_tangent, middle, partial, edges, row_film = call(
         local_kernel,
         inputs,
         [
-            (basis.shape, BF16), ((6 * n, lanes), F32), ((32, lanes), F32), (tangent.shape, F32), (tangent.shape, F32),
-            ((3 * rows + 16, lanes), F32), ((cells, 128), F32),
+            (basis.shape, BF16), ((32, lanes), F32), (tangent.shape, F32), ((3 * rows + 16, lanes), F32),
+            ((cells, 128), F32),
         ],
         [
             (tangent.shape, F32), (velocity.shape, F32), (face_frac.shape, F32), (branch.shape, branch.dtype),
             (basis.shape, BF16), (design.shape, BF16), (exit_film.shape, F32), (basis.shape, BF16),
-            ((18 * n, 2 * radial), BF16), ((12 * n, lanes), F32), ((6 * n, lanes), F32),
+            ((9 * n + 16, 2 * radial), BF16), ((9 * n + 16, lanes), F32),
         ],
         in_hbm=7,
-        out_hbm=2,
-        sems=9,
-        cost=pl.CostEstimate(flops=10**9, bytes_accessed=16 * 10**6, transcendentals=0),
+        out_hbm=1,
+        sems=8,
+        cost=pl.CostEstimate(flops=10**9, bytes_accessed=10 * 10**6, transcendentals=0),
     )
     x_e, x_o, film = call(
         middle_kernel, (middle, in_e, in_o), [(x_msg, F32), (x_msg, F32), ((8, 128), F32)], []
     )
     from_o, from_e, film_1 = swap(x_o, "ax", 3), swap(x_e, "ax", 1), swap(film, "ax", 2)
+    coef_2, fixed = call(
+        step_kernel,
+        (velocity, face_frac, branch, velocity_tangent, film),
+        [((6 * n, lanes), F32), (tangent.shape, F32)],
+        [
+            (velocity.shape, F32), (velocity.shape, F32), (velocity.shape, branch.dtype), (basis.shape, BF16),
+            ((9 * n, 2 * radial), BF16), ((3 * n, lanes), F32), ((6 * n, lanes), F32),
+        ],
+        in_hbm=4,
+        out_hbm=1,
+        sems=5,
+        cost=pl.CostEstimate(flops=10**9, bytes_accessed=10 * 10**6, transcendentals=0),
+    )
     count = 3 * rows + 16
     (out,) = call(
         last_kernel,

time: 36.4 us -> 36.8 us (1.011)
  Pallas kernels: 11.6 us -> 14.1 us
  waiting for transfers between devices: 2 us -> 0.02 us
    pallas_call x5 -> x6, Pallas kernels: 11.6 us -> 14.1 us  [call(): pl.pallas_call(kernel, out_shape=shapes_out, in_specs=[hbm] * in_hbm + [v...]
    ppermute x5, waiting for transfers between devices: 2 us -> 0.01 us  [swap(): return lax.ppermute(value, axis, list(enumerate(other)))]
  transfers between devices with their start and end apart: 6 -> 6, of which waited for: 1 -> 0; matrix products, arithmetic and copies ran while one was open for 0% -> 0% of each run, Pallas kernels for 21% -> 28%
where the time goes in v5:
time: 36.8 us; the launch traced here: 36.6 us
  starting transfers between devices  21.8 us (59%)
  Pallas kernels  14.1 us (38%)
  between operations  0.73 us (2%)
    ppermute x5, starting transfers between devices, swap(): return lax.ppermute(value, axis, list(enumerate(other)))  14.4 us
    pallas_call x6, Pallas kernels, call(): pl.pallas_call(kernel, out_shape=shapes_out, in_specs=[hbm] * in_hbm + [v...  14.1 us
    all_to_all x1, starting transfers between devices, local(): totals = lax.all_to_all(sums, 'az', 0, 0)  7.37 us
  transfers between devices with their start and end apart: 6, of which 0 were waited for; matrix products, arithmetic and copies ran while one was open for 0% of the time, Pallas kernels for 28%

profile of v5, /device:TPU:1, one launch (start us, length us, event | category | flops | bytes accessed | tf_op | source)
XLA Modules:
  0.0 36.6 jit_solution(11242397503182781721)
XLA Ops:
  0.6 3.3 %edge_kernel.1 = (f32[40,2048]{1,0:T(8,128)S(1)}, f32[40,2048]{1,0:T(8,128)S(1)}, f32[64,2,128]{2,1,0:T(2,128)}) custom-call(f32[4,16,2048]{2,1,0:T(8,128)} %tangent.3, f32[3,4,16,64]{3,2,1,0:T(8,128)} %velocity.5, f32[2,3,4,16,64]{4,3,2,1,0:T(8,128)} %frac.5, s32[2,3,4,16,64]{4,3,2,1,0:T(8,128)} %branch.5, bf16[3,4,16,2048]{3,2,1,0:T(8,128)(2,1)} %basis.3, ...), custom_call_target="tpu_custom_call" | custom-call | tf_op jit(solution)/shard_map/edge_kernel/pallas_call | solution.py:589
  3.9 3.8 %collective-permute-start = (f32[40,2048]{1,0:T(8,128)S(1)}, f32[40,2048]{1,0:T(8,128)S(1)}, u32[]{:S(2)}, u32[]{:S(2)}) collective-permute-start(f32[40,2048]{1,0:T(8,128)S(1)} %get-tuple-element.18), channel_id=1, source_target_pairs={{0,4},{4,0},{8,12},{12,8},{16,20},{20,16},{24,28},{28,24},{32,36},... | collective-permute-start | bytes 983048 | tf_op jit(solution)/shard_map/ppermute | solution.py:569
  7.8 7.6 %collective-permute-start.1 = (f32[40,2048]{1,0:T(8,128)S(1)}, f32[40,2048]{1,0:T(8,128)S(1)}, u32[]{:S(2)}, u32[]{:S(2)}) collective-permute-start(f32[40,2048]{1,0:T(8,128)S(1)} %get-tuple-element.19), channel_id=1, source_target_pairs={{0,252},{4,8},{8,4},{12,16},{16,12},{20,24},{24,20},{28,32},{32,28... | collective-permute-start | bytes 983048 | tf_op jit(solution)/shard_map/ppermute | solution.py:569
  15.4 7.4 %all-to-all-start = ((f32[64,2,128]{2,1,0:T(2,128)}), f32[64,2,128]{2,1,0:T(2,128)S(1)}, u32[]{:S(2)}, u32[]{:S(2)}) async-start(f32[64,2,128]{2,1,0:T(2,128)} %get-tuple-element.28), calls=%async_computation | async-start | bytes 131072 | tf_op jit(solution)/shard_map/all_to_all | solution.py:626
  22.7 3.6 %local_kernel.1 = (bf16[3,4,16,2048]{3,2,1,0:T(8,128)(2,1)}, f32[32,2048]{1,0:T(8,128)S(1)}, f32[4,16,2048]{2,1,0:T(8,128)S(1)}, f32[64,2048]{1,0:T(8,128)S(1)}, f32[4,128]{1,0:T(4,128)S(1)}) custom-call(f32[4,16,2048]{2,1,0:T(8,128)} %tangent.3, f32[3,4,16,64]{3,2,1,0:T(8,128)} %velocity.5, f32[2,3,4,16,64]{4,3,2,1,0:T(8,128)} %frac.5, ...), custom_call_target="tpu_custom_call" | custom-call | flops 1000000000 | bytes 10000000 | tf_op jit(solution)/shard_map/local_kernel/pallas_call | solution.py:589
  26.3 0.0 collective-permute-done.in_e
  26.3 0.0 collective-permute-done.1.in_o
  26.3 0.2 middle_kernel.1
  26.6 1.9 %collective-permute-start.2 = (f32[3,4,2048]{2,1,0:T(4,128)S(1)}, f32[3,4,2048]{2,1,0:T(4,128)S(1)}, u32[]{:S(2)}, u32[]{:S(2)}) collective-permute-start(f32[3,4,2048]{2,1,0:T(4,128)S(1)} %get-tuple-element.25), channel_id=1, source_target_pairs={{0,3},{1,2},{2,1},{3,0},{4,7},{5,6},{6,5},{7,4},{8,11},{9,10},{10,... | collective-permute-start | bytes 294920 | tf_op jit(solution)/shard_map/ppermute | solution.py:569
  28.5 0.0 collective-permute-start.3
  28.5 1.1 %collective-permute-start.4 = (f32[8,128]{1,0:T(8,128)S(1)}, f32[8,128]{1,0:T(8,128)S(1)}, u32[]{:S(2)}, u32[]{:S(2)}) collective-permute-start(f32[8,128]{1,0:T(8,128)S(1)} %get-tuple-element.20.after.film_own), channel_id=1, source_target_pairs={{0,2},{1,3},{2,0},{3,1},{4,6},{5,7},{6,4},{7,5},{8,10},{9,11},{10,... | collective-permute-start | bytes 12296 | tf_op jit(solution)/shard_map/ppermute | solution.py:569
  29.5 3.5 %step_kernel.1 = (f32[384,2048]{1,0:T(8,128)}, f32[4,16,2048]{2,1,0:T(8,128)S(1)}) custom-call(f32[3,4,16,64]{3,2,1,0:T(8,128)} %velocity.5, f32[2,3,4,16,64]{4,3,2,1,0:T(8,128)} %frac.5, s32[2,3,4,16,64]{4,3,2,1,0:T(8,128)} %branch.5, bf16[3,4,16,2048]{3,2,1,0:T(8,128)(2,1)} %get-tuple-element.14.vel_tan, f32[8,128]{1,0:T(8,128)S(1)} %get-tuple-element.20.after.film_own), custom_call_target="tpu_custom_call" | custom-call | flops 1000000000 | bytes 10000000 | tf_op jit(solution)/shard_map/step_kernel/pallas_call | solution.py:589
  33.0 0.0 collective-permute-done.2.x_o
  33.1 0.0 collective-permute-done.3.x_e
  33.1 2.8 %last_kernel.1.done = f32[4,16,2048]{2,1,0:T(8,128)} custom-call(f32[384,2048]{1,0:T(8,128)} %get-tuple-element.21.coef_2, f32[4,16,2048]{2,1,0:T(8,128)S(1)} %get-tuple-element.22.partial, f32[4,16,2048]{2,1,0:T(8,128)S(1)} %get-tuple-element.23.fixed, f32[64,2048]{1,0:T(8,128)S(1)} %get-tuple-element.24.edges, f32[40,2048]{1,0:T(8,128)S(1)} %collective-permute-done.in_e, ...), custom_call_target="tpu_custom_call" | custom-call | tf_op jit(solution)/shard_map/last_kernel/pallas_call | solution.py:589
  35.8 0.0 all-to-all-done.totals
  35.9 0.0 collective-permute-done.4.film_1
  35.9 0.7 %film_kernel.1 = f32[4,8]{1,0:T(4,128)} custom-call(f32[4,16,2048]{2,1,0:T(8,128)} %last_kernel.1.done, f32[4,128]{1,0:T(4,128)S(1)} %get-tuple-element.27.row_film, f32[8,128]{1,0:T(8,128)S(1)} %get-tuple-element.20.after.film_own, f32[8,128]{1,0:T(8,128)S(1)} %collective-permute-done.4.film_1, f32[3,4,2048]{2,1,0:T(4,128)S(1)} %collective-permute-done.2.x_o, ...), custom_call_target="tpu_custom_call" | custom-call | tf_op jit(solution)/shard_map/film_kernel/pallas_call | solution.py:589
Async XLA Ops:
  3.9 22.4 %collective-permute-start = (f32[40,2048]{1,0:T(8,128)S(1)}, f32[40,2048]{1,0:T(8,128)S(1)}, u32[]{:S(2)}, u32[]{:S(2)}) collective-permute-start(f32[40,2048]{1,0:T(8,128)S(1)} %get-tuple-element.18), channel_id=1, source_target_pairs={{0,4},{4,0},{8,12},{12,8},{16,20},{20,16},{24,28},{28,24},{32,36},... | collective-permute-start | bytes 983048 | tf_op jit(solution)/shard_map/ppermute | solution.py:569
  7.8 18.5 %collective-permute-start.1 = (f32[40,2048]{1,0:T(8,128)S(1)}, f32[40,2048]{1,0:T(8,128)S(1)}, u32[]{:S(2)}, u32[]{:S(2)}) collective-permute-start(f32[40,2048]{1,0:T(8,128)S(1)} %get-tuple-element.19), channel_id=1, source_target_pairs={{0,252},{4,8},{8,4},{12,16},{16,12},{20,24},{24,20},{28,32},{32,28... | collective-permute-start | bytes 983048 | tf_op jit(solution)/shard_map/ppermute | solution.py:569
  15.4 20.5 %all-to-all-start = ((f32[64,2,128]{2,1,0:T(2,128)}), f32[64,2,128]{2,1,0:T(2,128)S(1)}, u32[]{:S(2)}, u32[]{:S(2)}) async-start(f32[64,2,128]{2,1,0:T(2,128)} %get-tuple-element.28), calls=%async_computation | async-start | bytes 131072 | tf_op jit(solution)/shard_map/all_to_all | solution.py:626
  26.6 6.5 %collective-permute-start.2 = (f32[3,4,2048]{2,1,0:T(4,128)S(1)}, f32[3,4,2048]{2,1,0:T(4,128)S(1)}, u32[]{:S(2)}, u32[]{:S(2)}) collective-permute-start(f32[3,4,2048]{2,1,0:T(4,128)S(1)} %get-tuple-element.25), channel_id=1, source_target_pairs={{0,3},{1,2},{2,1},{3,0},{4,7},{5,6},{6,5},{7,4},{8,11},{9,10},{10,... | collective-permute-start | bytes 294920 | tf_op jit(solution)/shard_map/ppermute | solution.py:569
  28.5 4.6 %collective-permute-start.3 = (f32[3,4,2048]{2,1,0:T(4,128)S(1)}, f32[3,4,2048]{2,1,0:T(4,128)S(1)}, u32[]{:S(2)}, u32[]{:S(2)}) collective-permute-start(f32[3,4,2048]{2,1,0:T(4,128)S(1)} %get-tuple-element.26), channel_id=1, source_target_pairs={{0,1},{1,0},{2,3},{3,2},{4,5},{5,4},{6,7},{7,6},{8,9},{9,8},{10,11... | collective-permute-start | bytes 294920 | tf_op jit(solution)/shard_map/ppermute | solution.py:569
  28.5 7.4 %collective-permute-start.4 = (f32[8,128]{1,0:T(8,128)S(1)}, f32[8,128]{1,0:T(8,128)S(1)}, u32[]{:S(2)}, u32[]{:S(2)}) collective-permute-start(f32[8,128]{1,0:T(8,128)S(1)} %get-tuple-element.20.after.film_own), channel_id=1, source_target_pairs={{0,2},{1,3},{2,0},{3,1},{4,6},{5,7},{6,4},{7,5},{8,10},{9,11},{10,... | collective-permute-start | bytes 12296 | tf_op jit(solution)/shard_map/ppermute | solution.py:569

commit v6 on v5

--- a/solution.py
+++ b/solution.py
@@ -98,8 +98,8 @@
 
 def edge_kernel(
     tangent, velocity, frac, branch, basis, design, exit_film,
-    msg_e, msg_o, sums,
-    field, vel, share, share_2, kind, kind_2, left, mat, film, vel_tan, packed, spread, work, ends, edge, faces, face_a, sems,
+    msg_e, msg_o, sums, field, vel, share, kind, left, mat, film,
+    vel_tan, packed, spread, work, ends, edge, faces, face_a, sems,
 ):
     cells, rows, lanes = field.shape
     radial = vel.shape[-1]
@@ -107,49 +107,44 @@
     last, end = cells - 1, rows - 1
     inner = wall(radial)
     pairs = [
-        (exit_film, film), (velocity, vel), (branch.at[0], kind), (frac.at[0], share), (frac.at[1, 0, last], share_2),
-        (branch.at[1, 0, last], kind_2), (design, mat), (tangent, field),
+        (exit_film, film), (velocity, vel), (branch, kind), (frac, share), (design, mat), (tangent, field), (basis, left),
     ]
     copies = [pltpu.make_async_copy(src, dst, sems.at[i]) for i, (src, dst) in enumerate(pairs)]
-    base = len(copies)
-    copies += [
-        pltpu.make_async_copy(basis.at[c, a], left.at[pl.ds(i * rows, rows)], sems.at[base + i])
-        for i, (c, a) in enumerate(EDGE)
-    ]
     for copy in copies:
         copy.start()
     copies[0].wait()
     sums[...] = jnp.full(sums.shape, jnp.sum(film[...] * radial_weights(radial)), F32)
-    for copy in copies[1:6]:
+    for copy in copies[1:4]:
         copy.wait()
 
     at = {}
     row = 0
     for c, a in EDGE:
-        low, high = mix(vel[c, a], kind[c, a])
+        low, high = mix(vel[c, a], kind[0, c, a])
         if (c, a) == (0, last):
             high_a = high
         if c == 1:
             at["high", a] = high
-        for name, part in zip("plh", (share[c, a], low, high), strict=True):
+        for name, part in zip("plh", (share[0, c, a], low, high), strict=True):
             packed[pl.ds(row, rows), :] = two_terms(part * inner if c == 2 else part)
             at[name, c, a] = row
             row += rows
-    low_2, high_2 = mix(vel[0, last], kind_2[...])
-    for name, part in zip("pl", (share_2[...], low_2), strict=True):
+    low_2, high_2 = mix(vel[0, last], kind[1, 0, last])
+    for name, part in zip("pl", (share[1, 0, last], low_2), strict=True):
         packed[pl.ds(row, rows), :] = two_terms(part)
         at[name] = row
         row += rows
     spread_all(packed, [spread], radial, dirs)
 
-    for copy in copies[6:]:
+    for copy in copies[4:]:
         copy.wait()
     weights = blocks_of(mat[...])
 
     @pl.loop(0, lanes // CHUNK, unroll=UNROLL)
     def _(k):
         lane = pl.ds(pl.multiple_of(k * CHUNK, CHUNK), CHUNK)
-        vel_tan[:, lane] = jnp.dot(left[:, lane], weights, preferred_element_type=F32).astype(BF16)
+        part = jnp.concatenate([left[c, a, :, lane] for c, a in EDGE], axis=0)
+        vel_tan[:, lane] = jnp.dot(part, weights, preferred_element_type=F32).astype(BF16)
 
     def sp(*key):
         return spread[pl.ds(at[key], rows), :]
@@ -219,9 +214,9 @@
 
 
 def local_kernel(
-    tangent, velocity, frac, branch, basis, design, exit_film,
+    field, vel, share, kind, left, mat, film,
     vel_tan, middle, partial, edges, row_film,
-    field, vel, share, kind, left, mat, film, product, packed, spread, sems,
+    product, packed, spread, sems,
 ):
     cells, rows, lanes = field.shape
     radial = vel.shape[-1]
@@ -229,15 +224,6 @@
     n = cells * rows
     last, end = cells - 1, rows - 1
     inner = wall(radial)
-    pairs = [
-        (velocity, vel), (branch, kind), (frac, share), (design, mat), (basis, left), (tangent, field), (exit_film, film),
-    ]
-    copies = [pltpu.make_async_copy(src, dst, sems.at[i]) for i, (src, dst) in enumerate(pairs)]
-    for copy in copies:
-        copy.start()
-    for copy in copies[:3]:
-        copy.wait()
-
     for c in range(3):
         low, high = mix(vel[c], kind[0, c])
         for k, part in enumerate((share[0, c], low, high)):
@@ -253,8 +239,6 @@
         for a in range(cells):
             middle[pl.ds(MIDDLE["coefs"], 1), pl.ds(128 * (start + a), radial)] = part[a, end:, :]
     spread_all(packed, [spread], radial, dirs)
-    for copy in copies[3:5]:
-        copy.wait()
     weights = blocks_of(mat[...])
 
     @pl.loop(0, lanes // CHUNK, unroll=UNROLL)
@@ -263,10 +247,8 @@
         block = jnp.dot(left[:, :, :, lane].reshape(3 * n, CHUNK), weights, preferred_element_type=F32)
         product[:, :, :, lane] = block.astype(BF16).reshape(3, cells, rows, CHUNK)
 
-    output = pltpu.make_async_copy(product, vel_tan, sems.at[len(copies)])
+    output = pltpu.make_async_copy(product, vel_tan, sems.at[0])
     output.start()
-    for copy in copies[5:]:
-        copy.wait()
 
     def sp(k, c, a):
         return spread[pl.ds((k * 3 + c) * n + a * rows, rows), :]
@@ -314,9 +296,9 @@
 
 
 def step_kernel(
-    velocity, frac, branch, vel_tan, after,
+    vel_tan, vel, share, kind, after,
     coef_2, fixed,
-    vel, share, kind, product, packed, spread, mixed, sems,
+    product, packed, spread, mixed, sems,
 ):
     del after
     _, cells, rows, lanes = product.shape
@@ -324,14 +306,10 @@
     dirs = lanes // radial
     n = cells * rows
     inner = wall(radial)
-    pairs = [(velocity, vel), (branch.at[1], kind), (frac.at[1], share), (vel_tan, product)]
-    copies = [pltpu.make_async_copy(src, dst, sems.at[i]) for i, (src, dst) in enumerate(pairs)]
-    for copy in copies:
-        copy.start()
-    for copy in copies[:3]:
-        copy.wait()
+    fetch = pltpu.make_async_copy(vel_tan, product, sems.at[0])
+    fetch.start()
     for c in range(3):
-        for k, part in enumerate((share[c], *mix(vel[c], kind[c]))):
+        for k, part in enumerate((share[1, c], *mix(vel[c], kind[1, c]))):
             part = part.reshape(n, radial)
             part = two_terms(part * inner if c == 2 else part)
             if k == 0:
@@ -340,10 +318,15 @@
             for a in range(cells):
                 row = 3 * n + ((a * 2 + k - 1) * 3 + c) * rows
                 packed[pl.ds(row, rows), :] = part[a * rows:(a + 1) * rows]
-    spread_all(packed, [spread, mixed], radial, dirs)
-    output = pltpu.make_async_copy(mixed, coef_2, sems.at[len(copies)])
-    output.start()
-    copies[3].wait()
+    copies = []
+    for k in range(lanes // CHUNK):
+        lane = pl.ds(k * CHUNK, CHUNK)
+        ones = spreader(k * CHUNK, CHUNK, radial, dirs)
+        mixed[:, lane] = jnp.dot(packed[pl.ds(3 * n, 6 * n), :], ones, preferred_element_type=F32)
+        copies.append(pltpu.make_async_copy(mixed.at[:, lane], coef_2.at[:, lane], sems.at[1 + k]))
+        copies[k].start()
+        spread[:, lane] = jnp.dot(packed[pl.ds(0, 3 * n), :], ones, preferred_element_type=F32)
+    fetch.wait()
     before = None
     for a in range(cells):
         faces = [product[c, a].astype(F32) * spread[pl.ds(c * n + a * rows, rows), :] for c in range(3)]
@@ -351,7 +334,8 @@
         before = faces[0]
         change = change + (faces[1] - behind_x(faces[1], 0.0))
         fixed[a] = change + (faces[2] - behind_r(faces[2], dirs))
-    output.wait()
+    for copy in copies:
+        copy.wait()
 
 
 def gathered_row(msg, row, lane, lanes):
@@ -606,39 +590,32 @@
     devices = lax.axis_size("az")
     layer, cell_layer = (rows, lanes), (rows, radial)
     z_msg, x_msg, line = (2 * rows + 8, lanes), (3, cells, lanes), (cells, lanes)
-    inputs = (tangent, velocity, face_frac, branch, basis, design, exit_film)
+    inputs = inputs_in_order = (tangent, velocity, face_frac, branch, basis, design, exit_film)
     count = (3 * len(EDGE) + 2) * rows
-    z_e, z_o, sums = call(
+    z_e, z_o, sums, *inputs = call(
         edge_kernel,
         inputs,
-        [(z_msg, F32), (z_msg, F32), ((devices, 2, 128), F32)],
+        [(z_msg, F32), (z_msg, F32), ((devices, 2, 128), F32)] + [(value.shape, value.dtype) for value in inputs_in_order],
         [
-            (tangent.shape, F32), (velocity.shape, F32), (velocity.shape, F32), (cell_layer, F32),
-            (velocity.shape, branch.dtype), (cell_layer, branch.dtype), ((len(EDGE) * rows, lanes), BF16),
-            (design.shape, BF16), (exit_film.shape, F32), ((len(EDGE) * rows, lanes), BF16),
-            ((count, 2 * radial), BF16), ((count, lanes), F32), (layer, F32), ((2, lanes), F32),
-            ((2, *layer), F32), ((2, *layer), F32), (layer, F32),
+            ((len(EDGE) * rows, lanes), BF16), ((count, 2 * radial), BF16), ((count, lanes), F32), (layer, F32),
+            ((2, lanes), F32), ((2, *layer), F32), ((2, *layer), F32), (layer, F32),
         ],
         in_hbm=7,
-        sems=8 + len(EDGE),
-    )
+        sems=7,
+    )
+    field, vel, share, kind, left, mat, film_in = inputs
     in_e, in_o = swap(z_e, "az", 0), swap(z_o, "az", 1)
     totals = lax.all_to_all(sums, "az", 0, 0)
     velocity_tangent, middle, partial, edges, row_film = call(
         local_kernel,
-        inputs,
+        (field, vel, share, kind, left, mat, film_in),
         [
             (basis.shape, BF16), ((32, lanes), F32), (tangent.shape, F32), ((3 * rows + 16, lanes), F32),
             ((cells, 128), F32),
         ],
-        [
-            (tangent.shape, F32), (velocity.shape, F32), (face_frac.shape, F32), (branch.shape, branch.dtype),
-            (basis.shape, BF16), (design.shape, BF16), (exit_film.shape, F32), (basis.shape, BF16),
-            ((9 * n + 16, 2 * radial), BF16), ((9 * n + 16, lanes), F32),
-        ],
-        in_hbm=7,
+        [(basis.shape, BF16), ((9 * n + 16, 2 * radial), BF16), ((9 * n + 16, lanes), F32)],
         out_hbm=1,
-        sems=8,
+        sems=1,
         cost=pl.CostEstimate(flops=10**9, bytes_accessed=10 * 10**6, transcendentals=0),
     )
     x_e, x_o, film = call(
@@ -647,15 +624,12 @@
     from_o, from_e, film_1 = swap(x_o, "ax", 3), swap(x_e, "ax", 1), swap(film, "ax", 2)
     coef_2, fixed = call(
         step_kernel,
-        (velocity, face_frac, branch, velocity_tangent, film),
+        (velocity_tangent, vel, share, kind, film),
         [((6 * n, lanes), F32), (tangent.shape, F32)],
-        [
-            (velocity.shape, F32), (velocity.shape, F32), (velocity.shape, branch.dtype), (basis.shape, BF16),
-            ((9 * n, 2 * radial), BF16), ((3 * n, lanes), F32), ((6 * n, lanes), F32),
-        ],
-        in_hbm=4,
+        [(basis.shape, BF16), ((9 * n, 2 * radial), BF16), ((3 * n, lanes), F32), ((6 * n, lanes), F32)],
+        in_hbm=1,
         out_hbm=1,
-        sems=5,
+        sems=1 + lanes // CHUNK,
         cost=pl.CostEstimate(flops=10**9, bytes_accessed=10 * 10**6, transcendentals=0),
     )
     count = 3 * rows + 16

time: 36.8 us -> 35 us (0.951)
  Pallas kernels: 14.1 us -> 11.9 us
    pallas_call x6, Pallas kernels: 14.1 us -> 11.9 us  [call(): pl.pallas_call(kernel, out_shape=shapes_out, in_specs=[hbm] * in_hbm + [v...]
  transfers between devices with their start and end apart: 6 -> 6, of which waited for: 0 -> 1; matrix products, arithmetic and copies ran while one was open for 0% -> 0% of each run, Pallas kernels for 28% -> 23%
where the time goes in v6:
time: 35 us; the launch traced here: 34.5 us
  starting transfers between devices  21.8 us (62%)
  Pallas kernels  11.9 us (34%)
  between operations  0.71 us (2%)
    ppermute x5, starting transfers between devices, swap(): return lax.ppermute(value, axis, list(enumerate(other)))  14.4 us
    pallas_call x6, Pallas kernels, call(): pl.pallas_call(kernel, out_shape=shapes_out, in_specs=[hbm] * in_hbm + [v...  11.9 us
    all_to_all x1, starting transfers between devices, local(): totals = lax.all_to_all(sums, 'az', 0, 0)  7.38 us
  transfers between devices with their start and end apart: 6, of which 1 were waited for; matrix products, arithmetic and copies ran while one was open for 0% of the time, Pallas kernels for 23%

profile of v6, /device:TPU:1, one launch (start us, length us, event | category | flops | bytes accessed | tf_op | source)
XLA Modules:
  0.0 34.5 jit_solution(6626168835875410448)
XLA Ops:
  0.6 3.3 %edge_kernel.1 = (f32[40,2048]{1,0:T(8,128)S(1)}, f32[40,2048]{1,0:T(8,128)S(1)}, f32[64,2,128]{2,1,0:T(2,128)}, f32[4,16,2048]{2,1,0:T(8,128)S(1)}, f32[3,4,16,...) custom-call(f32[4,16,2048]{2,1,0:T(8,128)} %tangent.1, ...), custom_call_target="tpu_custom_call" | custom-call | tf_op jit(solution)/shard_map/edge_kernel/pallas_call | solution.py:573
  4.0 3.8 %collective-permute-start = (f32[40,2048]{1,0:T(8,128)S(1)}, f32[40,2048]{1,0:T(8,128)S(1)}, u32[]{:S(2)}, u32[]{:S(2)}) collective-permute-start(f32[40,2048]{1,0:T(8,128)S(1)} %get-tuple-element.32), channel_id=1, source_target_pairs={{0,4},{4,0},{8,12},{12,8},{16,20},{20,16},{24,28},{28,24},{32,36},... | collective-permute-start | bytes 983048 | tf_op jit(solution)/shard_map/ppermute | solution.py:553
  7.8 7.6 %collective-permute-start.1 = (f32[40,2048]{1,0:T(8,128)S(1)}, f32[40,2048]{1,0:T(8,128)S(1)}, u32[]{:S(2)}, u32[]{:S(2)}) collective-permute-start(f32[40,2048]{1,0:T(8,128)S(1)} %get-tuple-element.33), channel_id=1, source_target_pairs={{0,252},{4,8},{8,4},{12,16},{16,12},{20,24},{24,20},{28,32},{32,28... | collective-permute-start | bytes 983048 | tf_op jit(solution)/shard_map/ppermute | solution.py:553
  15.4 7.4 %all-to-all-start = ((f32[64,2,128]{2,1,0:T(2,128)}), f32[64,2,128]{2,1,0:T(2,128)S(1)}, u32[]{:S(2)}, u32[]{:S(2)}) async-start(f32[64,2,128]{2,1,0:T(2,128)} %get-tuple-element.42), calls=%async_computation | async-start | bytes 131072 | tf_op jit(solution)/shard_map/all_to_all | solution.py:608
  22.8 2.7 %local_kernel.1 = (bf16[3,4,16,2048]{3,2,1,0:T(8,128)(2,1)}, f32[32,2048]{1,0:T(8,128)S(1)}, f32[4,16,2048]{2,1,0:T(8,128)S(1)}, f32[64,2048]{1,0:T(8,128)S(1)}, f32[4,128]{1,0:T(4,128)S(1)}) custom-call(f32[4,16,2048]{2,1,0:T(8,128)S(1)} %get-tuple-element.23.field, f32[3,4,16,64]{3,2,1,0:T(8,128)S(1)} %get-tuple-element.24.vel, ...), custom_call_target="tpu_custom_call" | custom-call | flops 1000000000 | bytes 10000000 | tf_op jit(solution)/shard_map/local_kernel/pallas_call | solution.py:573
  25.5 0.0 collective-permute-done.in_e
  25.5 0.0 collective-permute-done.1.in_o
  25.5 0.2 middle_kernel.1
  25.8 1.9 %collective-permute-start.2 = (f32[3,4,2048]{2,1,0:T(4,128)S(1)}, f32[3,4,2048]{2,1,0:T(4,128)S(1)}, u32[]{:S(2)}, u32[]{:S(2)}) collective-permute-start(f32[3,4,2048]{2,1,0:T(4,128)S(1)} %get-tuple-element.39), channel_id=1, source_target_pairs={{0,3},{1,2},{2,1},{3,0},{4,7},{5,6},{6,5},{7,4},{8,11},{9,10},{10,... | collective-permute-start | bytes 294920 | tf_op jit(solution)/shard_map/ppermute | solution.py:553
  27.7 0.0 collective-permute-start.3
  27.7 1.1 %collective-permute-start.4 = (f32[8,128]{1,0:T(8,128)S(1)}, f32[8,128]{1,0:T(8,128)S(1)}, u32[]{:S(2)}, u32[]{:S(2)}) collective-permute-start(f32[8,128]{1,0:T(8,128)S(1)} %get-tuple-element.34.after.film_own), channel_id=1, source_target_pairs={{0,2},{1,3},{2,0},{3,1},{4,6},{5,7},{6,4},{7,5},{8,10},{9,11},{10,... | collective-permute-start | bytes 12296 | tf_op jit(solution)/shard_map/ppermute | solution.py:553
  28.7 2.1 %step_kernel.1 = (f32[384,2048]{1,0:T(8,128)}, f32[4,16,2048]{2,1,0:T(8,128)S(1)}) custom-call(bf16[3,4,16,2048]{3,2,1,0:T(8,128)(2,1)} %get-tuple-element.21.vel_tan, f32[3,4,16,64]{3,2,1,0:T(8,128)S(1)} %get-tuple-element.24.vel, f32[2,3,4,16,64]{4,3,2,1,0:T(8,128)S(1)} %get-tuple-element.25.share, s32[2,3,4,16,64]{4,3,2,1,0:T(8,128)S(1)} %get-tuple-element.26.kind, ...), custom_call_target="tpu_custom_call" | custom-call | flops 1000000000 | bytes 10000000 | tf_op jit(solution)/shard_map/step_kernel/pallas_call | solution.py:573
  30.9 0.0 collective-permute-done.2.x_o
  30.9 0.0 collective-permute-done.3.x_e
  30.9 2.8 %last_kernel.1.done = f32[4,16,2048]{2,1,0:T(8,128)} custom-call(f32[384,2048]{1,0:T(8,128)} %get-tuple-element.35.coef_2, f32[4,16,2048]{2,1,0:T(8,128)S(1)} %get-tuple-element.36.partial, f32[4,16,2048]{2,1,0:T(8,128)S(1)} %get-tuple-element.37.fixed, f32[64,2048]{1,0:T(8,128)S(1)} %get-tuple-element.38.edges, f32[40,2048]{1,0:T(8,128)S(1)} %collective-permute-done.in_e, ...), custom_call_target="tpu_custom_call" | custom-call | tf_op jit(solution)/shard_map/last_kernel/pallas_call | solution.py:573
  33.6 0.2 all-to-all-done.totals
  33.8 0.0 collective-permute-done.4.film_1
  33.8 0.7 %film_kernel.1 = f32[4,8]{1,0:T(4,128)} custom-call(f32[4,16,2048]{2,1,0:T(8,128)} %last_kernel.1.done, f32[4,128]{1,0:T(4,128)S(1)} %get-tuple-element.41.row_film, f32[8,128]{1,0:T(8,128)S(1)} %get-tuple-element.34.after.film_own, f32[8,128]{1,0:T(8,128)S(1)} %collective-permute-done.4.film_1, f32[3,4,2048]{2,1,0:T(4,128)S(1)} %collective-permute-done.2.x_o, ...), custom_call_target="tpu_custom_call" | custom-call | tf_op jit(solution)/shard_map/film_kernel/pallas_call | solution.py:573
Async XLA Ops:
  4.0 21.5 %collective-permute-start = (f32[40,2048]{1,0:T(8,128)S(1)}, f32[40,2048]{1,0:T(8,128)S(1)}, u32[]{:S(2)}, u32[]{:S(2)}) collective-permute-start(f32[40,2048]{1,0:T(8,128)S(1)} %get-tuple-element.32), channel_id=1, source_target_pairs={{0,4},{4,0},{8,12},{12,8},{16,20},{20,16},{24,28},{28,24},{32,36},... | collective-permute-start | bytes 983048 | tf_op jit(solution)/shard_map/ppermute | solution.py:553
  7.8 17.7 %collective-permute-start.1 = (f32[40,2048]{1,0:T(8,128)S(1)}, f32[40,2048]{1,0:T(8,128)S(1)}, u32[]{:S(2)}, u32[]{:S(2)}) collective-permute-start(f32[40,2048]{1,0:T(8,128)S(1)} %get-tuple-element.33), channel_id=1, source_target_pairs={{0,252},{4,8},{8,4},{12,16},{16,12},{20,24},{24,20},{28,32},{32,28... | collective-permute-start | bytes 983048 | tf_op jit(solution)/shard_map/ppermute | solution.py:553
  15.4 18.4 %all-to-all-start = ((f32[64,2,128]{2,1,0:T(2,128)}), f32[64,2,128]{2,1,0:T(2,128)S(1)}, u32[]{:S(2)}, u32[]{:S(2)}) async-start(f32[64,2,128]{2,1,0:T(2,128)} %get-tuple-element.42), calls=%async_computation | async-start | bytes 131072 | tf_op jit(solution)/shard_map/all_to_all | solution.py:608
  25.8 5.1 %collective-permute-start.2 = (f32[3,4,2048]{2,1,0:T(4,128)S(1)}, f32[3,4,2048]{2,1,0:T(4,128)S(1)}, u32[]{:S(2)}, u32[]{:S(2)}) collective-permute-start(f32[3,4,2048]{2,1,0:T(4,128)S(1)} %get-tuple-element.39), channel_id=1, source_target_pairs={{0,3},{1,2},{2,1},{3,0},{4,7},{5,6},{6,5},{7,4},{8,11},{9,10},{10,... | collective-permute-start | bytes 294920 | tf_op jit(solution)/shard_map/ppermute | solution.py:553
  27.7 3.2 %collective-permute-start.3 = (f32[3,4,2048]{2,1,0:T(4,128)S(1)}, f32[3,4,2048]{2,1,0:T(4,128)S(1)}, u32[]{:S(2)}, u32[]{:S(2)}) collective-permute-start(f32[3,4,2048]{2,1,0:T(4,128)S(1)} %get-tuple-element.40), channel_id=1, source_target_pairs={{0,1},{1,0},{2,3},{3,2},{4,5},{5,4},{6,7},{7,6},{8,9},{9,8},{10,11... | collective-permute-start | bytes 294920 | tf_op jit(solution)/shard_map/ppermute | solution.py:553
  27.7 6.1 %collective-permute-start.4 = (f32[8,128]{1,0:T(8,128)S(1)}, f32[8,128]{1,0:T(8,128)S(1)}, u32[]{:S(2)}, u32[]{:S(2)}) collective-permute-start(f32[8,128]{1,0:T(8,128)S(1)} %get-tuple-element.34.after.film_own), channel_id=1, source_target_pairs={{0,2},{1,3},{2,0},{3,1},{4,6},{5,7},{6,4},{7,5},{8,10},{9,11},{10,... | collective-permute-start | bytes 12296 | tf_op jit(solution)/shard_map/ppermute | solution.py:553

commit v7 on v6

--- a/solution.py
+++ b/solution.py
@@ -98,8 +98,8 @@
 
 def edge_kernel(
     tangent, velocity, frac, branch, basis, design, exit_film,
-    msg_e, msg_o, sums, field, vel, share, kind, left, mat, film,
-    vel_tan, packed, spread, work, ends, edge, faces, face_a, sems,
+    msg_e, msg_o, sums, field, vel, share, kind, left, weights, film,
+    mat, vel_tan, packed, spread, work, ends, edge, faces, face_a, sems,
 ):
     cells, rows, lanes = field.shape
     radial = vel.shape[-1]
@@ -107,14 +107,16 @@
     last, end = cells - 1, rows - 1
     inner = wall(radial)
     pairs = [
-        (exit_film, film), (velocity, vel), (branch, kind), (frac, share), (design, mat), (tangent, field), (basis, left),
+        (exit_film, film), (design, mat), (velocity, vel), (branch, kind), (frac, share), (tangent, field), (basis, left),
     ]
     copies = [pltpu.make_async_copy(src, dst, sems.at[i]) for i, (src, dst) in enumerate(pairs)]
     for copy in copies:
         copy.start()
     copies[0].wait()
     sums[...] = jnp.full(sums.shape, jnp.sum(film[...] * radial_weights(radial)), F32)
-    for copy in copies[1:4]:
+    copies[1].wait()
+    weights[...] = blocks_of(mat[...])
+    for copy in copies[2:5]:
         copy.wait()
 
     at = {}
@@ -136,15 +138,14 @@
         row += rows
     spread_all(packed, [spread], radial, dirs)
 
-    for copy in copies[4:]:
+    for copy in copies[5:]:
         copy.wait()
-    weights = blocks_of(mat[...])
 
     @pl.loop(0, lanes // CHUNK, unroll=UNROLL)
     def _(k):
         lane = pl.ds(pl.multiple_of(k * CHUNK, CHUNK), CHUNK)
         part = jnp.concatenate([left[c, a, :, lane] for c, a in EDGE], axis=0)
-        vel_tan[:, lane] = jnp.dot(part, weights, preferred_element_type=F32).astype(BF16)
+        vel_tan[:, lane] = jnp.dot(part, weights[...], preferred_element_type=F32).astype(BF16)
 
     def sp(*key):
         return spread[pl.ds(at[key], rows), :]
@@ -214,7 +215,7 @@
 
 
 def local_kernel(
-    field, vel, share, kind, left, mat, film,
+    field, vel, share, kind, left, weights, film,
     vel_tan, middle, partial, edges, row_film,
     product, packed, spread, sems,
 ):
@@ -239,12 +240,11 @@
         for a in range(cells):
             middle[pl.ds(MIDDLE["coefs"], 1), pl.ds(128 * (start + a), radial)] = part[a, end:, :]
     spread_all(packed, [spread], radial, dirs)
-    weights = blocks_of(mat[...])
 
     @pl.loop(0, lanes // CHUNK, unroll=UNROLL)
     def _(k):
         lane = pl.ds(pl.multiple_of(k * CHUNK, CHUNK), CHUNK)
-        block = jnp.dot(left[:, :, :, lane].reshape(3 * n, CHUNK), weights, preferred_element_type=F32)
+        block = jnp.dot(left[:, :, :, lane].reshape(3 * n, CHUNK), weights[...], preferred_element_type=F32)
         product[:, :, :, lane] = block.astype(BF16).reshape(3, cells, rows, CHUNK)
 
     output = pltpu.make_async_copy(product, vel_tan, sems.at[0])
@@ -590,25 +590,26 @@
     devices = lax.axis_size("az")
     layer, cell_layer = (rows, lanes), (rows, radial)
     z_msg, x_msg, line = (2 * rows + 8, lanes), (3, cells, lanes), (cells, lanes)
-    inputs = inputs_in_order = (tangent, velocity, face_frac, branch, basis, design, exit_film)
+    inputs = (tangent, velocity, face_frac, branch, basis, design, exit_film)
     count = (3 * len(EDGE) + 2) * rows
-    z_e, z_o, sums, *inputs = call(
+    kept = [(value.shape, value.dtype) for value in inputs]
+    kept[5] = ((CHUNK, CHUNK), BF16)
+    z_e, z_o, sums, field, vel, share, kind, left, weights, film_in = call(
         edge_kernel,
         inputs,
-        [(z_msg, F32), (z_msg, F32), ((devices, 2, 128), F32)] + [(value.shape, value.dtype) for value in inputs_in_order],
+        [(z_msg, F32), (z_msg, F32), ((devices, 2, 128), F32)] + kept,
         [
-            ((len(EDGE) * rows, lanes), BF16), ((count, 2 * radial), BF16), ((count, lanes), F32), (layer, F32),
+            (design.shape, BF16), ((len(EDGE) * rows, lanes), BF16), ((count, 2 * radial), BF16), ((count, lanes), F32), (layer, F32),
             ((2, lanes), F32), ((2, *layer), F32), ((2, *layer), F32), (layer, F32),
         ],
         in_hbm=7,
         sems=7,
     )
-    field, vel, share, kind, left, mat, film_in = inputs
     in_e, in_o = swap(z_e, "az", 0), swap(z_o, "az", 1)
     totals = lax.all_to_all(sums, "az", 0, 0)
     velocity_tangent, middle, partial, edges, row_film = call(
         local_kernel,
-        (field, vel, share, kind, left, mat, film_in),
+        (field, vel, share, kind, left, weights, film_in),
         [
             (basis.shape, BF16), ((32, lanes), F32), (tangent.shape, F32), ((3 * rows + 16, lanes), F32),
             ((cells, 128), F32),

time: 35 us -> 34.7 us (level)
  Pallas kernels: 11.9 us -> 11.2 us
  waiting for transfers between devices: 0.19 us -> 0.66 us
    pallas_call x6, Pallas kernels: 11.9 us -> 11.2 us  [call(): pl.pallas_call(kernel, out_shape=shapes_out, in_specs=[hbm] * in_hbm + [v...]
    all_to_all x1, waiting for transfers between devices: 0.17 us -> 0.6 us  [local(): totals = lax.all_to_all(sums, 'az', 0, 0)]
  transfers between devices with their start and end apart: 6 -> 6, of which waited for: 1 -> 1; matrix products, arithmetic and copies ran while one was open for 0% -> 0% of each run, Pallas kernels for 23% -> 21%
where the time goes in v7:
time: 34.7 us; the launch traced here: 34.3 us
  starting transfers between devices  21.8 us (63%)
  Pallas kernels  11.2 us (32%)
  between operations  0.7 us (2%)
  waiting for transfers between devices  0.66 us (2%)
    ppermute x5, starting transfers between devices, swap(): return lax.ppermute(value, axis, list(enumerate(other)))  14.4 us
    pallas_call x6, Pallas kernels, call(): pl.pallas_call(kernel, out_shape=shapes_out, in_specs=[hbm] * in_hbm + [v...  11.2 us
    all_to_all x1, starting transfers between devices, local(): totals = lax.all_to_all(sums, 'az', 0, 0)  7.39 us
  transfers between devices with their start and end apart: 6, of which 1 were waited for; matrix products, arithmetic and copies ran while one was open for 0% of the time, Pallas kernels for 21%

profile of v7, /device:TPU:1, one launch (start us, length us, event | category | flops | bytes accessed | tf_op | source)
XLA Modules:
  0.0 34.3 jit_solution(3845181181905254667)
XLA Ops:
  0.6 3.1 %edge_kernel.1 = (f32[40,2048]{1,0:T(8,128)S(1)}, f32[40,2048]{1,0:T(8,128)S(1)}, f32[64,2,128]{2,1,0:T(2,128)}, f32[4,16,2048]{2,1,0:T(8,128)S(1)}, f32[3,4,16,...) custom-call(f32[4,16,2048]{2,1,0:T(8,128)} %tangent.1, ...), custom_call_target="tpu_custom_call" | custom-call | tf_op jit(solution)/shard_map/edge_kernel/pallas_call | solution.py:573
  3.7 3.8 %collective-permute-start = (f32[40,2048]{1,0:T(8,128)S(1)}, f32[40,2048]{1,0:T(8,128)S(1)}, u32[]{:S(2)}, u32[]{:S(2)}) collective-permute-start(f32[40,2048]{1,0:T(8,128)S(1)} %get-tuple-element.32), channel_id=1, source_target_pairs={{0,4},{4,0},{8,12},{12,8},{16,20},{20,16},{24,28},{28,24},{32,36},... | collective-permute-start | bytes 983048 | tf_op jit(solution)/shard_map/ppermute | solution.py:553
  7.6 7.6 %collective-permute-start.1 = (f32[40,2048]{1,0:T(8,128)S(1)}, f32[40,2048]{1,0:T(8,128)S(1)}, u32[]{:S(2)}, u32[]{:S(2)}) collective-permute-start(f32[40,2048]{1,0:T(8,128)S(1)} %get-tuple-element.33), channel_id=1, source_target_pairs={{0,252},{4,8},{8,4},{12,16},{16,12},{20,24},{24,20},{28,32},{32,28... | collective-permute-start | bytes 983048 | tf_op jit(solution)/shard_map/ppermute | solution.py:553
  15.1 7.4 %all-to-all-start = ((f32[64,2,128]{2,1,0:T(2,128)}), f32[64,2,128]{2,1,0:T(2,128)S(1)}, u32[]{:S(2)}, u32[]{:S(2)}) async-start(f32[64,2,128]{2,1,0:T(2,128)} %get-tuple-element.42), calls=%async_computation | async-start | bytes 131072 | tf_op jit(solution)/shard_map/all_to_all | solution.py:609
  22.5 2.3 %local_kernel.1 = (bf16[3,4,16,2048]{3,2,1,0:T(8,128)(2,1)}, f32[32,2048]{1,0:T(8,128)S(1)}, f32[4,16,2048]{2,1,0:T(8,128)S(1)}, f32[64,2048]{1,0:T(8,128)S(1)}, f32[4,128]{1,0:T(4,128)S(1)}) custom-call(f32[4,16,2048]{2,1,0:T(8,128)S(1)} %get-tuple-element.23.field, f32[3,4,16,64]{3,2,1,0:T(8,128)S(1)} %get-tuple-element.24.vel, ...), custom_call_target="tpu_custom_call" | custom-call | flops 1000000000 | bytes 10000000 | tf_op jit(solution)/shard_map/local_kernel/pallas_call | solution.py:573
  24.8 0.0 collective-permute-done.in_e
  24.8 0.0 collective-permute-done.1.in_o
  24.8 0.2 middle_kernel.1
  25.1 1.9 %collective-permute-start.2 = (f32[3,4,2048]{2,1,0:T(4,128)S(1)}, f32[3,4,2048]{2,1,0:T(4,128)S(1)}, u32[]{:S(2)}, u32[]{:S(2)}) collective-permute-start(f32[3,4,2048]{2,1,0:T(4,128)S(1)} %get-tuple-element.39), channel_id=1, source_target_pairs={{0,3},{1,2},{2,1},{3,0},{4,7},{5,6},{6,5},{7,4},{8,11},{9,10},{10,... | collective-permute-start | bytes 294920 | tf_op jit(solution)/shard_map/ppermute | solution.py:553
  27.0 0.0 collective-permute-start.3
  27.0 1.1 %collective-permute-start.4 = (f32[8,128]{1,0:T(8,128)S(1)}, f32[8,128]{1,0:T(8,128)S(1)}, u32[]{:S(2)}, u32[]{:S(2)}) collective-permute-start(f32[8,128]{1,0:T(8,128)S(1)} %get-tuple-element.34.after.film_own), channel_id=1, source_target_pairs={{0,2},{1,3},{2,0},{3,1},{4,6},{5,7},{6,4},{7,5},{8,10},{9,11},{10,... | collective-permute-start | bytes 12296 | tf_op jit(solution)/shard_map/ppermute | solution.py:553
  28.0 2.1 %step_kernel.1 = (f32[384,2048]{1,0:T(8,128)}, f32[4,16,2048]{2,1,0:T(8,128)S(1)}) custom-call(bf16[3,4,16,2048]{3,2,1,0:T(8,128)(2,1)} %get-tuple-element.21.vel_tan, f32[3,4,16,64]{3,2,1,0:T(8,128)S(1)} %get-tuple-element.24.vel, f32[2,3,4,16,64]{4,3,2,1,0:T(8,128)S(1)} %get-tuple-element.25.share, s32[2,3,4,16,64]{4,3,2,1,0:T(8,128)S(1)} %get-tuple-element.26.kind, ...), custom_call_target="tpu_custom_call" | custom-call | flops 1000000000 | bytes 10000000 | tf_op jit(solution)/shard_map/step_kernel/pallas_call | solution.py:573
  30.1 0.0 collective-permute-done.2.x_o
  30.2 0.0 collective-permute-done.3.x_e
  30.2 2.8 %last_kernel.1.done = f32[4,16,2048]{2,1,0:T(8,128)} custom-call(f32[384,2048]{1,0:T(8,128)} %get-tuple-element.35.coef_2, f32[4,16,2048]{2,1,0:T(8,128)S(1)} %get-tuple-element.36.partial, f32[4,16,2048]{2,1,0:T(8,128)S(1)} %get-tuple-element.37.fixed, f32[64,2048]{1,0:T(8,128)S(1)} %get-tuple-element.38.edges, f32[40,2048]{1,0:T(8,128)S(1)} %collective-permute-done.in_e, ...), custom_call_target="tpu_custom_call" | custom-call | tf_op jit(solution)/shard_map/last_kernel/pallas_call | solution.py:573
  32.9 0.6 %all-to-all-done.totals = f32[64,2,128]{2,1,0:T(2,128)S(1)} async-done(((f32[64,2,128]{2,1,0:T(2,128)}), f32[64,2,128]{2,1,0:T(2,128)S(1)}, u32[]{:S(2)}, u32[]{:S(2)}) %all-to-all-start) | async-done | bytes 65568 | tf_op jit(solution)/shard_map/all_to_all | solution.py:609
  33.6 0.0 collective-permute-done.4.film_1
  33.6 0.7 %film_kernel.1 = f32[4,8]{1,0:T(4,128)} custom-call(f32[4,16,2048]{2,1,0:T(8,128)} %last_kernel.1.done, f32[4,128]{1,0:T(4,128)S(1)} %get-tuple-element.41.row_film, f32[8,128]{1,0:T(8,128)S(1)} %get-tuple-element.34.after.film_own, f32[8,128]{1,0:T(8,128)S(1)} %collective-permute-done.4.film_1, f32[3,4,2048]{2,1,0:T(4,128)S(1)} %collective-permute-done.2.x_o, ...), custom_call_target="tpu_custom_call" | custom-call | tf_op jit(solution)/shard_map/film_kernel/pallas_call | solution.py:573
Async XLA Ops:
  3.7 21.1 %collective-permute-start = (f32[40,2048]{1,0:T(8,128)S(1)}, f32[40,2048]{1,0:T(8,128)S(1)}, u32[]{:S(2)}, u32[]{:S(2)}) collective-permute-start(f32[40,2048]{1,0:T(8,128)S(1)} %get-tuple-element.32), channel_id=1, source_target_pairs={{0,4},{4,0},{8,12},{12,8},{16,20},{20,16},{24,28},{28,24},{32,36},... | collective-permute-start | bytes 983048 | tf_op jit(solution)/shard_map/ppermute | solution.py:553
  7.6 17.3 %collective-permute-start.1 = (f32[40,2048]{1,0:T(8,128)S(1)}, f32[40,2048]{1,0:T(8,128)S(1)}, u32[]{:S(2)}, u32[]{:S(2)}) collective-permute-start(f32[40,2048]{1,0:T(8,128)S(1)} %get-tuple-element.33), channel_id=1, source_target_pairs={{0,252},{4,8},{8,4},{12,16},{16,12},{20,24},{24,20},{28,32},{32,28... | collective-permute-start | bytes 983048 | tf_op jit(solution)/shard_map/ppermute | solution.py:553
  15.1 18.4 %all-to-all-start = ((f32[64,2,128]{2,1,0:T(2,128)}), f32[64,2,128]{2,1,0:T(2,128)S(1)}, u32[]{:S(2)}, u32[]{:S(2)}) async-start(f32[64,2,128]{2,1,0:T(2,128)} %get-tuple-element.42), calls=%async_computation | async-start | bytes 131072 | tf_op jit(solution)/shard_map/all_to_all | solution.py:609
  25.1 5.1 %collective-permute-start.2 = (f32[3,4,2048]{2,1,0:T(4,128)S(1)}, f32[3,4,2048]{2,1,0:T(4,128)S(1)}, u32[]{:S(2)}, u32[]{:S(2)}) collective-permute-start(f32[3,4,2048]{2,1,0:T(4,128)S(1)} %get-tuple-element.39), channel_id=1, source_target_pairs={{0,3},{1,2},{2,1},{3,0},{4,7},{5,6},{6,5},{7,4},{8,11},{9,10},{10,... | collective-permute-start | bytes 294920 | tf_op jit(solution)/shard_map/ppermute | solution.py:553
  27.0 3.2 %collective-permute-start.3 = (f32[3,4,2048]{2,1,0:T(4,128)S(1)}, f32[3,4,2048]{2,1,0:T(4,128)S(1)}, u32[]{:S(2)}, u32[]{:S(2)}) collective-permute-start(f32[3,4,2048]{2,1,0:T(4,128)S(1)} %get-tuple-element.40), channel_id=1, source_target_pairs={{0,1},{1,0},{2,3},{3,2},{4,5},{5,4},{6,7},{7,6},{8,9},{9,8},{10,11... | collective-permute-start | bytes 294920 | tf_op jit(solution)/shard_map/ppermute | solution.py:553
  27.0 6.6 %collective-permute-start.4 = (f32[8,128]{1,0:T(8,128)S(1)}, f32[8,128]{1,0:T(8,128)S(1)}, u32[]{:S(2)}, u32[]{:S(2)}) collective-permute-start(f32[8,128]{1,0:T(8,128)S(1)} %get-tuple-element.34.after.film_own), channel_id=1, source_target_pairs={{0,2},{1,3},{2,0},{3,1},{4,6},{5,7},{6,4},{7,5},{8,10},{9,11},{10,... | collective-permute-start | bytes 12296 | tf_op jit(solution)/shard_map/ppermute | solution.py:553

commit v8 on v7

--- a/solution.py
+++ b/solution.py
@@ -106,9 +106,14 @@
     dirs = lanes // radial
     last, end = cells - 1, rows - 1
     inner = wall(radial)
-    pairs = [
-        (exit_film, film), (design, mat), (velocity, vel), (branch, kind), (frac, share), (tangent, field), (basis, left),
-    ]
+    blocks = [(c, a) for c in range(3) for a in range(cells)]
+    later = [block for block in blocks if block not in EDGE]
+    pairs = [(exit_film, film), (design, mat), (velocity, vel)]
+    pairs += [(src.at[at], dst.at[at]) for src, dst in ((branch, kind), (frac, share)) for at in (0, (1, 0))]
+    pairs += [(tangent, field)] + [(basis.at[at], left.at[at]) for at in EDGE]
+    needed = len(pairs)
+    pairs += [(src.at[1, c], dst.at[1, c]) for src, dst in ((branch, kind), (frac, share)) for c in (1, 2)]
+    pairs += [(basis.at[at], left.at[at]) for at in later]
     copies = [pltpu.make_async_copy(src, dst, sems.at[i]) for i, (src, dst) in enumerate(pairs)]
     for copy in copies:
         copy.start()
@@ -116,7 +121,7 @@
     sums[...] = jnp.full(sums.shape, jnp.sum(film[...] * radial_weights(radial)), F32)
     copies[1].wait()
     weights[...] = blocks_of(mat[...])
-    for copy in copies[2:5]:
+    for copy in copies[2:7]:
         copy.wait()
 
     at = {}
@@ -138,7 +143,7 @@
         row += rows
     spread_all(packed, [spread], radial, dirs)
 
-    for copy in copies[5:]:
+    for copy in copies[7:needed]:
         copy.wait()
 
     @pl.loop(0, lanes // CHUNK, unroll=UNROLL)
@@ -207,6 +212,9 @@
     @pl.when(jnp.logical_not(even))
     def _():
         fill(msg_o, msg_e)
+
+    for copy in copies[needed:]:
+        copy.wait()
 
 
 MIDDLE = dict(
@@ -297,8 +305,8 @@
 
 def step_kernel(
     vel_tan, vel, share, kind, after,
-    coef_2, fixed,
-    product, packed, spread, mixed, sems,
+    mixed, fixed,
+    product, packed, spread, sems,
 ):
     del after
     _, cells, rows, lanes = product.shape
@@ -318,13 +326,10 @@
             for a in range(cells):
                 row = 3 * n + ((a * 2 + k - 1) * 3 + c) * rows
                 packed[pl.ds(row, rows), :] = part[a * rows:(a + 1) * rows]
-    copies = []
     for k in range(lanes // CHUNK):
         lane = pl.ds(k * CHUNK, CHUNK)
         ones = spreader(k * CHUNK, CHUNK, radial, dirs)
         mixed[:, lane] = jnp.dot(packed[pl.ds(3 * n, 6 * n), :], ones, preferred_element_type=F32)
-        copies.append(pltpu.make_async_copy(mixed.at[:, lane], coef_2.at[:, lane], sems.at[1 + k]))
-        copies[k].start()
         spread[:, lane] = jnp.dot(packed[pl.ds(0, 3 * n), :], ones, preferred_element_type=F32)
     fetch.wait()
     before = None
@@ -334,8 +339,6 @@
         before = faces[0]
         change = change + (faces[1] - behind_x(faces[1], 0.0))
         fixed[a] = change + (faces[2] - behind_r(faces[2], dirs))
-    for copy in copies:
-        copy.wait()
 
 
 def gathered_row(msg, row, lane, lanes):
@@ -414,9 +417,9 @@
 
 
 def last_kernel(
-    coef_2, partial, fixed, edges, in_e, in_o, x_o, x_e,
+    mixed, partial, fixed, edges, in_e, in_o, x_o, x_e,
     out,
-    packed, spread, up, down, below, above, now, edge, result, mixed, sems,
+    packed, spread, up, down, below, above, now, edge, result, sems,
 ):
     cells, rows, lanes = partial.shape
     radial = packed.shape[1] // 2
@@ -427,13 +430,6 @@
     place = lax.axis_index("ax")
     even_x = lax.rem(place, 2) == 0
     final = lax.axis_size("ax") - 1
-    layer = 6 * rows
-    loads = [
-        pltpu.make_async_copy(coef_2.at[pl.ds(a * layer, layer)], mixed.at[pl.ds(a * layer, layer)], sems.at[cells + a])
-        for a in range(cells)
-    ]
-    for copy in loads:
-        copy.start()
 
     @pl.when(even)
     def _():
@@ -508,7 +504,6 @@
 
     copies = []
     for a in range(cells):
-        loads[a].wait()
         f = now[a]
         face = low(0, a) * f + high(0, a) * now[a + 1]
         change = fixed[a] + (face - before)
@@ -603,7 +598,7 @@
             ((2, lanes), F32), ((2, *layer), F32), ((2, *layer), F32), (layer, F32),
         ],
         in_hbm=7,
-        sems=7,
+        sems=24,
     )
     in_e, in_o = swap(z_e, "az", 0), swap(z_o, "az", 1)
     totals = lax.all_to_all(sums, "az", 0, 0)
@@ -627,10 +622,9 @@
         step_kernel,
         (velocity_tangent, vel, share, kind, film),
         [((6 * n, lanes), F32), (tangent.shape, F32)],
-        [(basis.shape, BF16), ((9 * n, 2 * radial), BF16), ((3 * n, lanes), F32), ((6 * n, lanes), F32)],
+        [(basis.shape, BF16), ((9 * n, 2 * radial), BF16), ((3 * n, lanes), F32)],
         in_hbm=1,
-        out_hbm=1,
-        sems=1 + lanes // CHUNK,
+        sems=1,
         cost=pl.CostEstimate(flops=10**9, bytes_accessed=10 * 10**6, transcendentals=0),
     )
     count = 3 * rows + 16
@@ -640,11 +634,10 @@
         [(tangent.shape, F32)],
         [
             ((count, 2 * radial), BF16), ((count, lanes), F32), (z_msg, F32), (z_msg, F32), (x_msg, F32), (x_msg, F32),
-            ((cells + 1, *layer), F32), (line, F32), (tangent.shape, F32), ((6 * n, lanes), F32),
+            ((cells + 1, *layer), F32), (line, F32), (tangent.shape, F32),
         ],
-        in_hbm=1,
         out_hbm=1,
-        sems=2 * cells,
+        sems=cells,
     )
     (film_out,) = call(
         film_kernel,

time: 34.7 us -> 35 us (level)
  waiting for transfers between devices: 0.66 us -> 2.35 us
  Pallas kernels: 11.2 us -> 9.69 us
    pallas_call x6, Pallas kernels: 11.2 us -> 9.69 us  [call(): pl.pallas_call(kernel, out_shape=shapes_out, in_specs=[hbm] * in_hbm + [v...]
    all_to_all x1, waiting for transfers between devices: 0.6 us -> 1.59 us  [local(): totals = lax.all_to_all(sums, 'az', 0, 0)]
    ppermute x5, waiting for transfers between devices: 0.06 us -> 0.76 us  [swap(): return lax.ppermute(value, axis, list(enumerate(other)))]
  transfers between devices with their start and end apart: 6 -> 6, of which waited for: 1 -> 2; matrix products, arithmetic and copies ran while one was open for 0% -> 0% of each run, Pallas kernels for 21% -> 17%
where the time goes in v8:
time: 35 us; the launch traced here: 34.5 us
  starting transfers between devices  21.8 us (62%)
  Pallas kernels  9.69 us (28%)
  waiting for transfers between devices  2.35 us (7%)
  between operations  0.7 us (2%)
    ppermute x5, starting transfers between devices, swap(): return lax.ppermute(value, axis, list(enumerate(other)))  14.4 us
    pallas_call x6, Pallas kernels, call(): pl.pallas_call(kernel, out_shape=shapes_out, in_specs=[hbm] * in_hbm + [v...  9.69 us
    all_to_all x1, starting transfers between devices, local(): totals = lax.all_to_all(sums, 'az', 0, 0)  7.39 us
    all_to_all x1, waiting for transfers between devices, local(): totals = lax.all_to_all(sums, 'az', 0, 0)  1.59 us
    ppermute x5, waiting for transfers between devices, swap(): return lax.ppermute(value, axis, list(enumerate(other)))  0.76 us
  transfers between devices with their start and end apart: 6, of which 2 were waited for; matrix products, arithmetic and copies ran while one was open for 0% of the time, Pallas kernels for 17%

profile of v8, /device:TPU:1, one launch (start us, length us, event | category | flops | bytes accessed | tf_op | source)
XLA Modules:
  0.0 34.5 jit_solution(2469913866558315993)
XLA Ops:
  0.6 3.3 %edge_kernel.1 = (f32[40,2048]{1,0:T(8,128)S(1)}, f32[40,2048]{1,0:T(8,128)S(1)}, f32[64,2,128]{2,1,0:T(2,128)}, f32[4,16,2048]{2,1,0:T(8,128)S(1)}, f32[3,4,16,...) custom-call(f32[4,16,2048]{2,1,0:T(8,128)} %tangent.1, ...), custom_call_target="tpu_custom_call" | custom-call | tf_op jit(solution)/shard_map/edge_kernel/pallas_call | solution.py:568
  3.9 3.8 %collective-permute-start = (f32[40,2048]{1,0:T(8,128)S(1)}, f32[40,2048]{1,0:T(8,128)S(1)}, u32[]{:S(2)}, u32[]{:S(2)}) collective-permute-start(f32[40,2048]{1,0:T(8,128)S(1)} %get-tuple-element.32), channel_id=1, source_target_pairs={{0,4},{4,0},{8,12},{12,8},{16,20},{20,16},{24,28},{28,24},{32,36},... | collective-permute-start | bytes 983048 | tf_op jit(solution)/shard_map/ppermute | solution.py:548
  7.7 7.6 %collective-permute-start.1 = (f32[40,2048]{1,0:T(8,128)S(1)}, f32[40,2048]{1,0:T(8,128)S(1)}, u32[]{:S(2)}, u32[]{:S(2)}) collective-permute-start(f32[40,2048]{1,0:T(8,128)S(1)} %get-tuple-element.33), channel_id=1, source_target_pairs={{0,252},{4,8},{8,4},{12,16},{16,12},{20,24},{24,20},{28,32},{32,28... | collective-permute-start | bytes 983048 | tf_op jit(solution)/shard_map/ppermute | solution.py:548
  15.3 7.4 %all-to-all-start = ((f32[64,2,128]{2,1,0:T(2,128)}), f32[64,2,128]{2,1,0:T(2,128)S(1)}, u32[]{:S(2)}, u32[]{:S(2)}) async-start(f32[64,2,128]{2,1,0:T(2,128)} %get-tuple-element.42), calls=%async_computation | async-start | bytes 131072 | tf_op jit(solution)/shard_map/all_to_all | solution.py:604
  22.7 2.2 %local_kernel.1 = (bf16[3,4,16,2048]{3,2,1,0:T(8,128)(2,1)}, f32[32,2048]{1,0:T(8,128)S(1)}, f32[4,16,2048]{2,1,0:T(8,128)S(1)}, f32[64,2048]{1,0:T(8,128)S(1)}, f32[4,128]{1,0:T(4,128)S(1)}) custom-call(f32[4,16,2048]{2,1,0:T(8,128)S(1)} %get-tuple-element.23.field, f32[3,4,16,64]{3,2,1,0:T(8,128)S(1)} %get-tuple-element.24.vel, ...), custom_call_target="tpu_custom_call" | custom-call | flops 1000000000 | bytes 10000000 | tf_op jit(solution)/shard_map/local_kernel/pallas_call | solution.py:568
  25.0 0.0 collective-permute-done.in_e
  25.0 0.0 collective-permute-done.1.in_o
  25.0 0.2 middle_kernel.1
  25.3 1.9 %collective-permute-start.2 = (f32[3,4,2048]{2,1,0:T(4,128)S(1)}, f32[3,4,2048]{2,1,0:T(4,128)S(1)}, u32[]{:S(2)}, u32[]{:S(2)}) collective-permute-start(f32[3,4,2048]{2,1,0:T(4,128)S(1)} %get-tuple-element.39), channel_id=1, source_target_pairs={{0,3},{1,2},{2,1},{3,0},{4,7},{5,6},{6,5},{7,4},{8,11},{9,10},{10,... | collective-permute-start | bytes 294920 | tf_op jit(solution)/shard_map/ppermute | solution.py:548
  27.1 0.0 collective-permute-start.3
  27.1 1.1 %collective-permute-start.4 = (f32[8,128]{1,0:T(8,128)S(1)}, f32[8,128]{1,0:T(8,128)S(1)}, u32[]{:S(2)}, u32[]{:S(2)}) collective-permute-start(f32[8,128]{1,0:T(8,128)S(1)} %get-tuple-element.34.after.film_own), channel_id=1, source_target_pairs={{0,2},{1,3},{2,0},{3,1},{4,6},{5,7},{6,4},{7,5},{8,10},{9,11},{10,... | collective-permute-start | bytes 12296 | tf_op jit(solution)/shard_map/ppermute | solution.py:548
  28.2 1.4 %step_kernel.1 = (f32[384,2048]{1,0:T(8,128)S(1)}, f32[4,16,2048]{2,1,0:T(8,128)S(1)}) custom-call(bf16[3,4,16,2048]{3,2,1,0:T(8,128)(2,1)} %get-tuple-element.21.vel_tan, f32[3,4,16,64]{3,2,1,0:T(8,128)S(1)} %get-tuple-element.24.vel, f32[2,3,4,16,64]{4,3,2,1,0:T(8,128)S(1)} %get-tuple-element.25.share, s32[2,3,4,16,64]{4,3,2,1,0:T(8,128)S(1)} %get-tuple-element.26.kind, ...), custom_call_target="tpu_custom_call" | custom-call | flops 1000000000 | bytes 10000000 | tf_op jit(solution)/shard_map/step_kernel/pallas_call | solution.py:568
  29.6 0.8 %collective-permute-done.2.x_o = f32[3,4,2048]{2,1,0:T(4,128)S(1)} collective-permute-done((f32[3,4,2048]{2,1,0:T(4,128)S(1)}, f32[3,4,2048]{2,1,0:T(4,128)S(1)}, u32[]{:S(2)}, u32[]{:S(2)}) %collective-permute-start.2) | collective-permute-done | bytes 98336 | tf_op jit(solution)/shard_map/ppermute | solution.py:548
  30.4 0.0 collective-permute-done.3.x_e
  30.4 1.8 %last_kernel.1.done = f32[4,16,2048]{2,1,0:T(8,128)} custom-call(f32[384,2048]{1,0:T(8,128)S(1)} %get-tuple-element.35.mixed, f32[4,16,2048]{2,1,0:T(8,128)S(1)} %get-tuple-element.36.partial, f32[4,16,2048]{2,1,0:T(8,128)S(1)} %get-tuple-element.37.fixed, f32[64,2048]{1,0:T(8,128)S(1)} %get-tuple-element.38.edges, ...), custom_call_target="tpu_custom_call" | custom-call | tf_op jit(solution)/shard_map/last_kernel/pallas_call | solution.py:568
  32.2 1.6 %all-to-all-done.totals = f32[64,2,128]{2,1,0:T(2,128)S(1)} async-done(((f32[64,2,128]{2,1,0:T(2,128)}), f32[64,2,128]{2,1,0:T(2,128)S(1)}, u32[]{:S(2)}, u32[]{:S(2)}) %all-to-all-start) | async-done | bytes 65568 | tf_op jit(solution)/shard_map/all_to_all | solution.py:604
  33.8 0.0 collective-permute-done.4.film_1
  33.8 0.7 %film_kernel.1 = f32[4,8]{1,0:T(4,128)} custom-call(f32[4,16,2048]{2,1,0:T(8,128)} %last_kernel.1.done, f32[4,128]{1,0:T(4,128)S(1)} %get-tuple-element.41.row_film, f32[8,128]{1,0:T(8,128)S(1)} %get-tuple-element.34.after.film_own, f32[8,128]{1,0:T(8,128)S(1)} %collective-permute-done.4.film_1, f32[3,4,2048]{2,1,0:T(4,128)S(1)} %collective-permute-done.2.x_o, ...), custom_call_target="tpu_custom_call" | custom-call | tf_op jit(solution)/shard_map/film_kernel/pallas_call | solution.py:568
Async XLA Ops:
  3.9 21.1 %collective-permute-start = (f32[40,2048]{1,0:T(8,128)S(1)}, f32[40,2048]{1,0:T(8,128)S(1)}, u32[]{:S(2)}, u32[]{:S(2)}) collective-permute-start(f32[40,2048]{1,0:T(8,128)S(1)} %get-tuple-element.32), channel_id=1, source_target_pairs={{0,4},{4,0},{8,12},{12,8},{16,20},{20,16},{24,28},{28,24},{32,36},... | collective-permute-start | bytes 983048 | tf_op jit(solution)/shard_map/ppermute | solution.py:548
  7.7 17.3 %collective-permute-start.1 = (f32[40,2048]{1,0:T(8,128)S(1)}, f32[40,2048]{1,0:T(8,128)S(1)}, u32[]{:S(2)}, u32[]{:S(2)}) collective-permute-start(f32[40,2048]{1,0:T(8,128)S(1)} %get-tuple-element.33), channel_id=1, source_target_pairs={{0,252},{4,8},{8,4},{12,16},{16,12},{20,24},{24,20},{28,32},{32,28... | collective-permute-start | bytes 983048 | tf_op jit(solution)/shard_map/ppermute | solution.py:548
  15.3 18.5 %all-to-all-start = ((f32[64,2,128]{2,1,0:T(2,128)}), f32[64,2,128]{2,1,0:T(2,128)S(1)}, u32[]{:S(2)}, u32[]{:S(2)}) async-start(f32[64,2,128]{2,1,0:T(2,128)} %get-tuple-element.42), calls=%async_computation | async-start | bytes 131072 | tf_op jit(solution)/shard_map/all_to_all | solution.py:604
  25.3 5.1 %collective-permute-start.2 = (f32[3,4,2048]{2,1,0:T(4,128)S(1)}, f32[3,4,2048]{2,1,0:T(4,128)S(1)}, u32[]{:S(2)}, u32[]{:S(2)}) collective-permute-start(f32[3,4,2048]{2,1,0:T(4,128)S(1)} %get-tuple-element.39), channel_id=1, source_target_pairs={{0,3},{1,2},{2,1},{3,0},{4,7},{5,6},{6,5},{7,4},{8,11},{9,10},{10,... | collective-permute-start | bytes 294920 | tf_op jit(solution)/shard_map/ppermute | solution.py:548
  27.1 3.2 %collective-permute-start.3 = (f32[3,4,2048]{2,1,0:T(4,128)S(1)}, f32[3,4,2048]{2,1,0:T(4,128)S(1)}, u32[]{:S(2)}, u32[]{:S(2)}) collective-permute-start(f32[3,4,2048]{2,1,0:T(4,128)S(1)} %get-tuple-element.40), channel_id=1, source_target_pairs={{0,1},{1,0},{2,3},{3,2},{4,5},{5,4},{6,7},{7,6},{8,9},{9,8},{10,11... | collective-permute-start | bytes 294920 | tf_op jit(solution)/shard_map/ppermute | solution.py:548
  27.1 6.6 %collective-permute-start.4 = (f32[8,128]{1,0:T(8,128)S(1)}, f32[8,128]{1,0:T(8,128)S(1)}, u32[]{:S(2)}, u32[]{:S(2)}) collective-permute-start(f32[8,128]{1,0:T(8,128)S(1)} %get-tuple-element.34.after.film_own), channel_id=1, source_target_pairs={{0,2},{1,3},{2,0},{3,1},{4,6},{5,7},{6,4},{7,5},{8,10},{9,11},{10,... | collective-permute-start | bytes 12296 | tf_op jit(solution)/shard_map/ppermute | solution.py:548

commit v9 on v8

--- a/solution.py
+++ b/solution.py
@@ -106,14 +106,9 @@
     dirs = lanes // radial
     last, end = cells - 1, rows - 1
     inner = wall(radial)
-    blocks = [(c, a) for c in range(3) for a in range(cells)]
-    later = [block for block in blocks if block not in EDGE]
-    pairs = [(exit_film, film), (design, mat), (velocity, vel)]
-    pairs += [(src.at[at], dst.at[at]) for src, dst in ((branch, kind), (frac, share)) for at in (0, (1, 0))]
-    pairs += [(tangent, field)] + [(basis.at[at], left.at[at]) for at in EDGE]
-    needed = len(pairs)
-    pairs += [(src.at[1, c], dst.at[1, c]) for src, dst in ((branch, kind), (frac, share)) for c in (1, 2)]
-    pairs += [(basis.at[at], left.at[at]) for at in later]
+    pairs = [
+        (exit_film, film), (design, mat), (velocity, vel), (branch, kind), (frac, share), (basis, left), (tangent, field),
+    ]
     copies = [pltpu.make_async_copy(src, dst, sems.at[i]) for i, (src, dst) in enumerate(pairs)]
     for copy in copies:
         copy.start()
@@ -121,7 +116,7 @@
     sums[...] = jnp.full(sums.shape, jnp.sum(film[...] * radial_weights(radial)), F32)
     copies[1].wait()
     weights[...] = blocks_of(mat[...])
-    for copy in copies[2:7]:
+    for copy in copies[2:5]:
         copy.wait()
 
     at = {}
@@ -143,7 +138,7 @@
         row += rows
     spread_all(packed, [spread], radial, dirs)
 
-    for copy in copies[7:needed]:
+    for copy in copies[5:]:
         copy.wait()
 
     @pl.loop(0, lanes // CHUNK, unroll=UNROLL)
@@ -212,9 +207,6 @@
     @pl.when(jnp.logical_not(even))
     def _():
         fill(msg_o, msg_e)
-
-    for copy in copies[needed:]:
-        copy.wait()
 
 
 MIDDLE = dict(
@@ -598,7 +590,7 @@
             ((2, lanes), F32), ((2, *layer), F32), ((2, *layer), F32), (layer, F32),
         ],
         in_hbm=7,
-        sems=24,
+        sems=7,
     )
     in_e, in_o = swap(z_e, "az", 0), swap(z_o, "az", 1)
     totals = lax.all_to_all(sums, "az", 0, 0)

time: 35 us -> 34.8 us (level)
  no operation moved by 1% of the time
where the time goes in v9:
time: 34.8 us; the launch traced here: 34.3 us
  starting transfers between devices  21.8 us (63%)
  Pallas kernels  9.51 us (27%)
  waiting for transfers between devices  2.35 us (7%)
  between operations  0.7 us (2%)
    ppermute x5, starting transfers between devices, swap(): return lax.ppermute(value, axis, list(enumerate(other)))  14.4 us
    pallas_call x6, Pallas kernels, call(): pl.pallas_call(kernel, out_shape=shapes_out, in_specs=[hbm] * in_hbm + [v...  9.51 us
    all_to_all x1, starting transfers between devices, local(): totals = lax.all_to_all(sums, 'az', 0, 0)  7.39 us
    all_to_all x1, waiting for transfers between devices, local(): totals = lax.all_to_all(sums, 'az', 0, 0)  1.59 us
    ppermute x5, waiting for transfers between devices, swap(): return lax.ppermute(value, axis, list(enumerate(other)))  0.76 us
  transfers between devices with their start and end apart: 6, of which 2 were waited for; matrix products, arithmetic and copies ran while one was open for 0% of the time, Pallas kernels for 17%

profile of v9, /device:TPU:1, one launch (start us, length us, event | category | flops | bytes accessed | tf_op | source)
XLA Modules:
  0.0 34.3 jit_solution(12666050107435646166)
XLA Ops:
  0.6 3.1 %edge_kernel.1 = (f32[40,2048]{1,0:T(8,128)S(1)}, f32[40,2048]{1,0:T(8,128)S(1)}, f32[64,2,128]{2,1,0:T(2,128)}, f32[4,16,2048]{2,1,0:T(8,128)S(1)}, f32[3,4,16,...) custom-call(f32[4,16,2048]{2,1,0:T(8,128)} %tangent.1, ...), custom_call_target="tpu_custom_call" | custom-call | tf_op jit(solution)/shard_map/edge_kernel/pallas_call | solution.py:560
  3.7 3.8 %collective-permute-start = (f32[40,2048]{1,0:T(8,128)S(1)}, f32[40,2048]{1,0:T(8,128)S(1)}, u32[]{:S(2)}, u32[]{:S(2)}) collective-permute-start(f32[40,2048]{1,0:T(8,128)S(1)} %get-tuple-element.32), channel_id=1, source_target_pairs={{0,4},{4,0},{8,12},{12,8},{16,20},{20,16},{24,28},{28,24},{32,36},... | collective-permute-start | bytes 983048 | tf_op jit(solution)/shard_map/ppermute | solution.py:540
  7.6 7.6 %collective-permute-start.1 = (f32[40,2048]{1,0:T(8,128)S(1)}, f32[40,2048]{1,0:T(8,128)S(1)}, u32[]{:S(2)}, u32[]{:S(2)}) collective-permute-start(f32[40,2048]{1,0:T(8,128)S(1)} %get-tuple-element.33), channel_id=1, source_target_pairs={{0,252},{4,8},{8,4},{12,16},{16,12},{20,24},{24,20},{28,32},{32,28... | collective-permute-start | bytes 983048 | tf_op jit(solution)/shard_map/ppermute | solution.py:540
  15.1 7.4 %all-to-all-start = ((f32[64,2,128]{2,1,0:T(2,128)}), f32[64,2,128]{2,1,0:T(2,128)S(1)}, u32[]{:S(2)}, u32[]{:S(2)}) async-start(f32[64,2,128]{2,1,0:T(2,128)} %get-tuple-element.42), calls=%async_computation | async-start | bytes 131072 | tf_op jit(solution)/shard_map/all_to_all | solution.py:596
  22.5 2.2 %local_kernel.1 = (bf16[3,4,16,2048]{3,2,1,0:T(8,128)(2,1)}, f32[32,2048]{1,0:T(8,128)S(1)}, f32[4,16,2048]{2,1,0:T(8,128)S(1)}, f32[64,2048]{1,0:T(8,128)S(1)}, f32[4,128]{1,0:T(4,128)S(1)}) custom-call(f32[4,16,2048]{2,1,0:T(8,128)S(1)} %get-tuple-element.23.field, f32[3,4,16,64]{3,2,1,0:T(8,128)S(1)} %get-tuple-element.24.vel, ...), custom_call_target="tpu_custom_call" | custom-call | flops 1000000000 | bytes 10000000 | tf_op jit(solution)/shard_map/local_kernel/pallas_call | solution.py:560
  24.8 0.0 collective-permute-done.in_e
  24.8 0.0 collective-permute-done.1.in_o
  24.8 0.2 middle_kernel.1
  25.1 1.9 %collective-permute-start.2 = (f32[3,4,2048]{2,1,0:T(4,128)S(1)}, f32[3,4,2048]{2,1,0:T(4,128)S(1)}, u32[]{:S(2)}, u32[]{:S(2)}) collective-permute-start(f32[3,4,2048]{2,1,0:T(4,128)S(1)} %get-tuple-element.39), channel_id=1, source_target_pairs={{0,3},{1,2},{2,1},{3,0},{4,7},{5,6},{6,5},{7,4},{8,11},{9,10},{10,... | collective-permute-start | bytes 294920 | tf_op jit(solution)/shard_map/ppermute | solution.py:540
  27.0 0.0 collective-permute-start.3
  27.0 1.1 %collective-permute-start.4 = (f32[8,128]{1,0:T(8,128)S(1)}, f32[8,128]{1,0:T(8,128)S(1)}, u32[]{:S(2)}, u32[]{:S(2)}) collective-permute-start(f32[8,128]{1,0:T(8,128)S(1)} %get-tuple-element.34.after.film_own), channel_id=1, source_target_pairs={{0,2},{1,3},{2,0},{3,1},{4,6},{5,7},{6,4},{7,5},{8,10},{9,11},{10,... | collective-permute-start | bytes 12296 | tf_op jit(solution)/shard_map/ppermute | solution.py:540
  28.0 1.4 %step_kernel.1 = (f32[384,2048]{1,0:T(8,128)S(1)}, f32[4,16,2048]{2,1,0:T(8,128)S(1)}) custom-call(bf16[3,4,16,2048]{3,2,1,0:T(8,128)(2,1)} %get-tuple-element.21.vel_tan, f32[3,4,16,64]{3,2,1,0:T(8,128)S(1)} %get-tuple-element.24.vel, f32[2,3,4,16,64]{4,3,2,1,0:T(8,128)S(1)} %get-tuple-element.25.share, s32[2,3,4,16,64]{4,3,2,1,0:T(8,128)S(1)} %get-tuple-element.26.kind, ...), custom_call_target="tpu_custom_call" | custom-call | flops 1000000000 | bytes 10000000 | tf_op jit(solution)/shard_map/step_kernel/pallas_call | solution.py:560
  29.4 0.8 %collective-permute-done.2.x_o = f32[3,4,2048]{2,1,0:T(4,128)S(1)} collective-permute-done((f32[3,4,2048]{2,1,0:T(4,128)S(1)}, f32[3,4,2048]{2,1,0:T(4,128)S(1)}, u32[]{:S(2)}, u32[]{:S(2)}) %collective-permute-start.2) | collective-permute-done | bytes 98336 | tf_op jit(solution)/shard_map/ppermute | solution.py:540
  30.2 0.0 collective-permute-done.3.x_e
  30.2 1.8 %last_kernel.1.done = f32[4,16,2048]{2,1,0:T(8,128)} custom-call(f32[384,2048]{1,0:T(8,128)S(1)} %get-tuple-element.35.mixed, f32[4,16,2048]{2,1,0:T(8,128)S(1)} %get-tuple-element.36.partial, f32[4,16,2048]{2,1,0:T(8,128)S(1)} %get-tuple-element.37.fixed, f32[64,2048]{1,0:T(8,128)S(1)} %get-tuple-element.38.edges, ...), custom_call_target="tpu_custom_call" | custom-call | tf_op jit(solution)/shard_map/last_kernel/pallas_call | solution.py:560
  32.0 1.6 %all-to-all-done.totals = f32[64,2,128]{2,1,0:T(2,128)S(1)} async-done(((f32[64,2,128]{2,1,0:T(2,128)}), f32[64,2,128]{2,1,0:T(2,128)S(1)}, u32[]{:S(2)}, u32[]{:S(2)}) %all-to-all-start) | async-done | bytes 65568 | tf_op jit(solution)/shard_map/all_to_all | solution.py:596
  33.6 0.0 collective-permute-done.4.film_1
  33.6 0.7 %film_kernel.1 = f32[4,8]{1,0:T(4,128)} custom-call(f32[4,16,2048]{2,1,0:T(8,128)} %last_kernel.1.done, f32[4,128]{1,0:T(4,128)S(1)} %get-tuple-element.41.row_film, f32[8,128]{1,0:T(8,128)S(1)} %get-tuple-element.34.after.film_own, f32[8,128]{1,0:T(8,128)S(1)} %collective-permute-done.4.film_1, f32[3,4,2048]{2,1,0:T(4,128)S(1)} %collective-permute-done.2.x_o, ...), custom_call_target="tpu_custom_call" | custom-call | tf_op jit(solution)/shard_map/film_kernel/pallas_call | solution.py:560
Async XLA Ops:
  3.7 21.1 %collective-permute-start = (f32[40,2048]{1,0:T(8,128)S(1)}, f32[40,2048]{1,0:T(8,128)S(1)}, u32[]{:S(2)}, u32[]{:S(2)}) collective-permute-start(f32[40,2048]{1,0:T(8,128)S(1)} %get-tuple-element.32), channel_id=1, source_target_pairs={{0,4},{4,0},{8,12},{12,8},{16,20},{20,16},{24,28},{28,24},{32,36},... | collective-permute-start | bytes 983048 | tf_op jit(solution)/shard_map/ppermute | solution.py:540
  7.6 17.3 %collective-permute-start.1 = (f32[40,2048]{1,0:T(8,128)S(1)}, f32[40,2048]{1,0:T(8,128)S(1)}, u32[]{:S(2)}, u32[]{:S(2)}) collective-permute-start(f32[40,2048]{1,0:T(8,128)S(1)} %get-tuple-element.33), channel_id=1, source_target_pairs={{0,252},{4,8},{8,4},{12,16},{16,12},{20,24},{24,20},{28,32},{32,28... | collective-permute-start | bytes 983048 | tf_op jit(solution)/shard_map/ppermute | solution.py:540
  15.1 18.5 %all-to-all-start = ((f32[64,2,128]{2,1,0:T(2,128)}), f32[64,2,128]{2,1,0:T(2,128)S(1)}, u32[]{:S(2)}, u32[]{:S(2)}) async-start(f32[64,2,128]{2,1,0:T(2,128)} %get-tuple-element.42), calls=%async_computation | async-start | bytes 131072 | tf_op jit(solution)/shard_map/all_to_all | solution.py:596
  25.1 5.1 %collective-permute-start.2 = (f32[3,4,2048]{2,1,0:T(4,128)S(1)}, f32[3,4,2048]{2,1,0:T(4,128)S(1)}, u32[]{:S(2)}, u32[]{:S(2)}) collective-permute-start(f32[3,4,2048]{2,1,0:T(4,128)S(1)} %get-tuple-element.39), channel_id=1, source_target_pairs={{0,3},{1,2},{2,1},{3,0},{4,7},{5,6},{6,5},{7,4},{8,11},{9,10},{10,... | collective-permute-start | bytes 294920 | tf_op jit(solution)/shard_map/ppermute | solution.py:540
  27.0 3.2 %collective-permute-start.3 = (f32[3,4,2048]{2,1,0:T(4,128)S(1)}, f32[3,4,2048]{2,1,0:T(4,128)S(1)}, u32[]{:S(2)}, u32[]{:S(2)}) collective-permute-start(f32[3,4,2048]{2,1,0:T(4,128)S(1)} %get-tuple-element.40), channel_id=1, source_target_pairs={{0,1},{1,0},{2,3},{3,2},{4,5},{5,4},{6,7},{7,6},{8,9},{9,8},{10,11... | collective-permute-start | bytes 294920 | tf_op jit(solution)/shard_map/ppermute | solution.py:540
  27.0 6.6 %collective-permute-start.4 = (f32[8,128]{1,0:T(8,128)S(1)}, f32[8,128]{1,0:T(8,128)S(1)}, u32[]{:S(2)}, u32[]{:S(2)}) collective-permute-start(f32[8,128]{1,0:T(8,128)S(1)} %get-tuple-element.34.after.film_own), channel_id=1, source_target_pairs={{0,2},{1,3},{2,0},{3,1},{4,6},{5,7},{6,4},{7,5},{8,10},{9,11},{10,... | collective-permute-start | bytes 12296 | tf_op jit(solution)/shard_map/ppermute | solution.py:540
